TPU v7x, 32 devices: a whole 2x2x4 slice. The times are simulated.
32 devices in a mesh: rows: 8 (over z, y), heads: 4 (over x, core).
Axes of the slice: x: 2, y: 2, z: 4, core: 2. Of those that a mesh axis runs over, the one named last changes fastest.
Arguments:
- tokens: bfloat16 [32, 512, 768], P('rows', None, 'heads'), may hold values from -24 to 24
- qkv_weight: bfloat16 [2, 768, 3, 768], replicated, may hold values from -0.21875 to 0.21875
- out_weight: bfloat16 [2, 768, 768], replicated, may hold values from -0.21875 to 0.21875
- norm_gain: bfloat16 [2, 768], replicated, may hold values from 0.099609375 to 1.8984375
Outputs:
- stream: bfloat16 [32, 512, 768], P('rows', None, 'heads')
All inputs are finite; a program needn't handle non-finite values.
Results may differ from a plain program's by a relative error of at most 0.0096.
Values may be sent and summed in bfloat16 or wider, within the bound.
No kernel may reach another device: no remote copies, remote signals or barrier semaphores. Data moves between devices by JAX's collectives and lax.ppermute only.
A program may use at most 64 MiB of HBM per device.

v0:
```python
import jax
import jax.numpy as jnp
from jax import lax
from jax.sharding import PartitionSpec as P

D = 768
HEADS = 12
HEAD_DIM = 64
LAYERS = 2
BLOCKS = 2


epsilon = 1e-06


def attend(projected, score_scale):
    residues = projected.shape[1]
    queries = projected[:, :, 0]
    key_vecs = projected[:, :, 1]
    values = projected[:, :, 2]
    block_rows = residues // BLOCKS
    pieces_out = []
    for block_index in range(BLOCKS):
        block_queries = queries[:, block_index * block_rows : (block_index + 1) * block_rows]
        partial_value = (
            jnp.einsum(
                "sihc,sjhc->hij", block_queries, key_vecs, preferred_element_type=jnp.float32
            )
            * score_scale
        )
        scores = lax.psum(partial_value, "rows")
        weights = jax.nn.softmax(scores, axis=-1).astype(jnp.bfloat16)
        attended = jnp.einsum("hij,sjhc->sihc", weights, values, preferred_element_type=jnp.float32)
        pieces_out.append(attended.astype(jnp.bfloat16))
    return jnp.concatenate(pieces_out, axis=1)


def on_device(tokens, qkv_weight, out_weight, norm_gain):
    seq_dev, residues, slice_width = tokens.shape
    heads_here = HEADS // lax.axis_size("heads")
    score_scale = 1.0 / (HEAD_DIM * seq_dev * lax.axis_size("rows")) ** 0.5
    group_index = lax.axis_index("heads")
    stream = tokens
    for layer_index in range(LAYERS):
        own_columns = lax.dynamic_slice_in_dim(
            qkv_weight[layer_index], group_index * slice_width, slice_width, 2
        )
        qkv_matrix = own_columns.reshape(D, 3 * slice_width)
        portion = lax.all_gather(stream, "heads", axis=2, tiled=True)
        flat_portion = portion.reshape(seq_dev * residues, portion.shape[2])
        projected = jnp.dot(flat_portion, qkv_matrix, preferred_element_type=jnp.float32)
        projected = projected.astype(jnp.bfloat16).reshape(
            seq_dev, residues, 3, heads_here, HEAD_DIM
        )
        attended = attend(projected, score_scale).reshape(seq_dev * residues, slice_width)
        own_rows = lax.dynamic_slice_in_dim(
            out_weight[layer_index], group_index * slice_width, slice_width, 0
        )
        update = jnp.dot(attended, own_rows, preferred_element_type=jnp.float32).reshape(
            seq_dev, residues, D
        )
        summed = stream.astype(jnp.float32) + lax.psum_scatter(
            update.astype(jnp.bfloat16), "heads", scatter_dimension=2, tiled=True
        ).astype(jnp.float32)
        sum_squares = lax.psum(jnp.sum(summed * summed, axis=-1, keepdims=True), "heads")
        gain_row = lax.dynamic_slice_in_dim(
            norm_gain[layer_index], group_index * slice_width, slice_width, 0
        )
        normed = summed * lax.rsqrt(sum_squares / D + epsilon) * gain_row.astype(jnp.float32)
        stream = normed.astype(jnp.bfloat16)
    return stream


def solution(mesh):
    return jax.shard_map(
        on_device,
        mesh=mesh,
        in_specs=(P("rows", None, "heads"), P(), P(), P()),
        out_specs=P("rows", None, "heads"),
        check_vma=False,
    )
```

profile of v0, /device:TPU:0, one launch (start us, length us, event | category | flops | bytes accessed | tf_op | source)
XLA Modules:
  0.0 489.4 jit_solution(3792800548769480505)
XLA Ops:
  6.5 2.6 copy.24
  9.2 5.3 %fusion.37 = (bf16[1,768,3,768]{3,1,2,0:T(8,128)(2,1)}, bf16[1,768,3,768]{3,1,2,0:T(8,128)(2,1)S(1)}) fusion(bf16[2,768,3,768]{3,1,2,0:T(8,128)(2,1)} %param.5), kind=kLoop, calls=%fused_computation.73 | loop fusion | bytes 14155776 | tf_op jit(solution)/shard_map/slice | solution.py:46
  16.4 24.1 %all-gather.3.cloned.1.call-done = bf16[4,512,768]{1,0,2:T(4,128)(2,1)} async-done(((bf16[4,512,192]{1,0,2:T(4,128)(2,1)}), bf16[4,512,768]{1,0,2:T(4,128)(2,1)}) %all-gather.3.cloned.1.call-update) | async-done | bytes 3145744 | tf_op jit(solution)/shard_map/all_gather | solution.py:49
  40.6 4.4 copy.25
  44.9 4.6 fusion.4
  49.6 5.1 %reshape.58 = bf16[4,512,3,3,64]{1,0,4,3,2:T(4,128)(2,1)S(1)} reshape(bf16[2048,576]{0,1:T(8,128)(2,1)} %fusion.4) | data formatting | bytes 4718592 | tf_op jit(solution)/shard_map/reshape | solution.py:52
  54.6 1.7 fusion.40
  56.5 1.7 bitcast_multiply_fusion.3
  58.2 1.6 bitcast_multiply_fusion.2
  59.8 1.6 copy-done.4
  62.6 126.7 %all-reduce.7.cloned.1.call-done = (f32[3,256,512]{2,1,0:T(8,128)}, f32[3,256,512]{2,1,0:T(8,128)}) async-done(((f32[3,256,512]{2,1,0:T(8,128)}, f32[3,256,512]{2,1,0:T(8,128)}), (f32[3,256,512]{2,1,0:T(8,128)}, f32[3,256,512]{2,1,0:T(8,128)})) %all-reduce.7.cloned.1.call-update) | async-done | bytes 3145744 | tf_op jit(solution)/shard_map/psum | solution.py:31
  189.3 2.4 fusion.43
  192.3 4.3 fusion.13
  196.6 2.4 fusion.14
  200.2 2.7 convolution_convert_fusion.3
  203.7 36.3 %reduce-scatter.3.cloned.1.call-done = bf16[4,512,192]{1,2,0:T(8,128)(2,1)} async-done(((bf16[4,512,768]{1,2,0:T(8,128)(2,1)}), bf16[4,512,192]{1,2,0:T(8,128)(2,1)}) %reduce-scatter.3.cloned.1.call-update) | async-done | bytes 786448 | tf_op jit(solution)/shard_map/reduce_scatter | solution.py:62
  241.5 5.9 %psum.44 = f32[4,512,1]{1,0,2:T(4,128)S(1)} all-reduce(f32[4,512,1]{1,0,2:T(4,128)S(1)} %bitcast.114), channel_id=1, replica_groups=mesh['rows'=8,'heads'=4] {'heads'}, use_global_device_ids=true, to_apply=%region_8.0 | all-reduce | flops 2048 | bytes 16384 | tf_op jit(solution)/shard_map/psum | solution.py:65
  248.6 2.0 constant_dynamic-slice_fusion.1
  252.0 26.4 %all-gather.5.cloned.1.call-done = bf16[4,512,768]{1,2,0:T(8,128)(2,1)} async-done(((bf16[4,512,192]{1,2,0:T(8,128)(2,1)}), bf16[4,512,768]{1,2,0:T(8,128)(2,1)}) %all-gather.5.cloned.1.call-update) | async-done | bytes 3145744 | tf_op jit(solution)/shard_map/all_gather | solution.py:49
  278.4 3.2 copy.30
  281.6 4.6 convolution_convert_fusion
  286.2 5.1 %reshape.61 = bf16[4,512,3,3,64]{1,0,4,3,2:T(4,128)(2,1)S(1)} reshape(bf16[2048,576]{0,1:T(8,128)(2,1)} %convolution_convert_fusion) | data formatting | bytes 4718592 | tf_op jit(solution)/shard_map/reshape | solution.py:52
  292.3 1.6 bitcast_multiply_fusion.1
  293.9 1.6 bitcast_multiply_fusion
  295.5 129.5 %all-reduce.5.cloned.1.call-done = (f32[3,256,512]{2,1,0:T(8,128)}, f32[3,256,512]{2,1,0:T(8,128)}) async-done(((f32[3,256,512]{2,1,0:T(8,128)}, f32[3,256,512]{2,1,0:T(8,128)}), (f32[3,256,512]{2,1,0:T(8,128)}, f32[3,256,512]{2,1,0:T(8,128)})) %all-reduce.5.cloned.1.call-update) | async-done | bytes 3145744 | tf_op jit(solution)/shard_map/psum | solution.py:31
  425.0 2.4 fusion.45
  427.9 3.5 fusion.15
  431.5 1.6 fusion.16
  433.2 3.7 convolution_convert_fusion.2
  437.0 37.0 %reduce-scatter.5.cloned.1.call-done = bf16[4,512,192]{1,2,0:T(8,128)(2,1)} async-done(((bf16[4,512,768]{1,2,0:T(8,128)(2,1)}), bf16[4,512,192]{1,2,0:T(8,128)(2,1)}) %reduce-scatter.5.cloned.1.call-update) | async-done | bytes 786448 | tf_op jit(solution)/shard_map/reduce_scatter | solution.py:62
  474.0 1.5 multiply_reduce_fusion
  475.4 5.9 %psum.47 = f32[4,512,1]{1,0,2:T(4,128)S(1)} all-reduce(f32[4,512,1]{1,0,2:T(4,128)S(1)} %bitcast.115), channel_id=1, replica_groups=mesh['rows'=8,'heads'=4] {'heads'}, use_global_device_ids=true, to_apply=%region_17.0 | all-reduce | flops 2048 | bytes 16384 | tf_op jit(solution)/shard_map/psum | solution.py:65
  (50 shorter events, 12.9 us)
Async XLA Ops:
  6.5 34.0 %all-gather.3.cloned.1.call-start = ((), (), s32[]{:S(2)}) async-start(), calls=%async_computation.2 | async-start | bytes 3932160 | tf_op jit(solution)/shard_map/all_gather | solution.py:49
  9.2 180.2 %all-reduce.7.cloned.1.call-start = ((), (), s32[]{:S(2)}) async-start(), calls=%async_computation.7 | async-start | bytes 6291456 | tf_op jit(solution)/shard_map/psum | solution.py:31
  59.7 1.7 copy-start.4
  59.8 180.2 %reduce-scatter.3.cloned.1.call-start = ((), (), s32[]{:S(2)}) async-start(), calls=%async_computation.3 | async-start | bytes 3932160 | tf_op jit(solution)/shard_map/reduce_scatter | solution.py:62
  189.3 2.4 copy-start.5
  189.3 2.9 copy-start.7
  202.9 0.7 copy-start.8
  202.9 37.1 %copy-start.1 = (bf16[4,512,192]{1,2,0:T(8,128)(2,1)S(1)}, bf16[4,512,192]{1,2,0:T(8,128)(2,1)}, u32[]{:S(2)}) copy-start(bf16[4,512,192]{1,2,0:T(8,128)(2,1)} %param.4) | copy-start | bytes 2359300
  203.0 75.5 %all-gather.5.cloned.1.call-start = ((), (), s32[]{:S(2)}) async-start(), calls=%async_computation.4 | async-start | bytes 3932160 | tf_op jit(solution)/shard_map/all_gather | solution.py:49
  240.0 7.4 %copy-start.2 = (bf16[4,512,192]{1,2,0:T(8,128)(2,1)S(1)}, bf16[4,512,192]{1,2,0:T(8,128)(2,1)}, u32[]{:S(2)}) copy-start(bf16[4,512,192]{1,2,0:T(8,128)(2,1)} %reduce-scatter.3.cloned.1.call-done) | copy-start | bytes 2359300
  248.6 176.4 %all-reduce.5.cloned.1.call-start = ((), (), s32[]{:S(2)}) async-start(), calls=%async_computation.6 | async-start | bytes 6291456 | tf_op jit(solution)/shard_map/psum | solution.py:31
  295.5 178.5 %reduce-scatter.5.cloned.1.call-start = ((), (), s32[]{:S(2)}) async-start(), calls=%async_computation.5 | async-start | bytes 3932160 | tf_op jit(solution)/shard_map/reduce_scatter | solution.py:62
  425.0 2.4 copy-start.6
  436.9 37.1 %copy-start = (bf16[4,512,192]{1,2,0:T(8,128)(2,1)S(1)}, bf16[4,512,192]{1,2,0:T(8,128)(2,1)}, u32[]{:S(2)}) copy-start(bf16[4,512,192]{1,2,0:T(8,128)(2,1)} %multiply_convert_fusion.1) | copy-start | bytes 2359300
  474.0 7.4 %copy-start.3 = (bf16[4,512,192]{1,2,0:T(8,128)(2,1)S(1)}, bf16[4,512,192]{1,2,0:T(8,128)(2,1)}, u32[]{:S(2)}) copy-start(bf16[4,512,192]{1,2,0:T(8,128)(2,1)} %reduce-scatter.5.cloned.1.call-done) | copy-start | bytes 2359300
Sparse Core Ops, SparseCore 0:
  9.3 31.2 all-gather.2
  59.9 129.4 all-reduce.6
  203.1 36.8 reduce-scatter.2
  248.7 29.6 all-gather.4
  295.6 129.4 all-reduce.4
  437.0 36.8 reduce-scatter.4
where the time goes:
time: 490 us; the launch traced here: 489 us
  waiting for transfers between devices  380 us (78%)
  local copies, waits for them, and re-layouts  37.1 us (8%)
  matrix products  33.8 us (7%)
  between operations  13.7 us (3%)
  other arithmetic  12.5 us (3%)
  blocking collectives  11.7 us (2%)
    psum x2, waiting for transfers between devices, attend(): scores = lax.psum(partial_value, 'rows')  256 us
    reduce_scatter x2, waiting for transfers between devices, on_device(): lax.psum_scatter(update.astype(jnp.bfloat16), 'heads', scatter_dimension=...  73.2 us
    all_gather x2, waiting for transfers between devices, on_device(): portion = lax.all_gather(stream, 'heads', axis=2, tiled=True)  50.5 us
    dot_general x4, matrix products, attend(): jnp.einsum('hij,sjhc->sihc', weights, values, preferred_element_type=jnp....  11.8 us
    psum x2, blocking collectives, on_device(): lax.psum(jnp.sum(summed * summed, axis=-1, keepdims=True), 'heads')  11.7 us
    reshape x2, local copies, waits for them, and re-layouts, on_device(): projected.astype(jnp.bfloat16)  10.2 us
  transfers between devices with their start and end apart: 6, of which 6 were waited for; matrix products, arithmetic and copies ran while one was open for 2% of the time, Pallas kernels for 0%

commit v1 on v0

v1 whole, which is shorter than its diff:
```python
import functools

import jax
import jax.numpy as jnp
from jax import lax
from jax.experimental import pallas as pl
from jax.experimental.pallas import tpu as pltpu
from jax.sharding import PartitionSpec as P

HEAD_DIM = 64
epsilon = 1e-06
VMEM_LIMIT = 40 * 1024 * 1024
F32 = jnp.float32
BF16 = jnp.bfloat16


def dot(a, b):
    return jnp.dot(a, b, preferred_element_type=F32)


def dot_t(a, b):
    return lax.dot_general(a, b, (((1,), (1,)), ((), ())), preferred_element_type=F32)


def params():
    return pltpu.CompilerParams(vmem_limit_bytes=VMEM_LIMIT)


def cost(flops, nbytes, trans=0):
    return pl.CostEstimate(flops=int(flops), bytes_accessed=int(nbytes), transcendentals=int(trans))


def nbytes(*arrays):
    return sum(a.size * a.dtype.itemsize for a in arrays)


def hold_type(rows):
    return BF16 if rows % 16 == 0 else F32


SMEM = pl.BlockSpec(memory_space=pltpu.SMEM)


def whole(array):
    return pl.BlockSpec(array.shape, lambda p, r=len(array.shape): (0,) * r)


def store_projections(pair, weight, heads, outs):
    made = [dot(rows, weight).astype(BF16) for rows in pair]
    width = heads * HEAD_DIM
    for which, out in enumerate(outs):
        for head in range(heads):
            at = which * width + head * HEAD_DIM
            out[head] = jnp.concatenate([m[:, at : at + HEAD_DIM] for m in made], axis=1)


def first_kernel(heads, place, near, far, weight, x_out, q_out, k_out, v_out):
    x_bit, core = place[0], place[1]
    quarter = near.shape[2] // 2
    pair = []
    for s in range(near.shape[0]):
        halves = []
        for ref in (near, far):
            rows = ref[s]
            swapped = jnp.concatenate([rows[:, quarter:], rows[:, :quarter]], axis=1)
            halves.append(jnp.where(core == 1, swapped, rows))
        low = jnp.where(x_bit == 1, halves[1], halves[0])
        high = jnp.where(x_bit == 1, halves[0], halves[1])
        rows = jnp.concatenate([low, high], axis=1)
        x_out[s] = rows
        pair.append(rows)
    store_projections(pair, weight[...], heads, (q_out, k_out, v_out))


def first(place, near, far, weight, heads):
    seqs, residues, half = near.shape
    width = 2 * half
    lanes = 2 * HEAD_DIM
    wide = jax.ShapeDtypeStruct((heads, residues, seqs * HEAD_DIM), BF16)
    flops = 2 * seqs * residues * width * weight.shape[1]
    piece = pl.BlockSpec((2, residues, half), lambda p: (p, 0, 0))
    out_block = pl.BlockSpec((heads, residues, lanes), lambda p: (0, 0, p))
    return pl.pallas_call(
        functools.partial(first_kernel, heads),
        grid=(seqs // 2,),
        in_specs=[SMEM, piece, piece, whole(weight)],
        out_specs=[pl.BlockSpec((2, residues, width), lambda p: (p, 0, 0))] + [out_block] * 3,
        out_shape=[jax.ShapeDtypeStruct((seqs, residues, width), BF16)] + [wide] * 3,
        compiler_params=params(),
        cost_estimate=cost(flops, 4 * nbytes(near, far) + nbytes(weight)),
    )(place, near, far, weight)


def score_kernel(scale, z_ref, *refs):
    queries, keys, others, outs, hold = refs[0:2], refs[2:4], refs[4:6], refs[6:-1], refs[-1]
    z = z_ref[0]
    heads, rows = outs[0].shape[0], outs[0].shape[1]
    residues = queries[0].shape[1]
    for head in range(heads):
        near = dot_t(queries[0][head], keys[0][head]) + dot_t(queries[1][head], keys[1][head])
        hold[:, :residues] = (near * scale).astype(hold.dtype)
        far = dot_t(queries[0][head], others[0][head]) + dot_t(queries[1][head], others[1][head])
        hold[:, residues:] = (far * scale).astype(hold.dtype)
        for d, out in enumerate(outs):
            start = pl.multiple_of(jnp.bitwise_xor(z, d) * rows, rows)
            out[head] = hold[pl.ds(start, rows), :].astype(BF16)


def score_chunks(z, queries, keys, others, scale, chunks):
    heads, residues, depth = queries[0].shape
    rows = residues // chunks
    args = (*queries, *keys, *others)
    return pl.pallas_call(
        functools.partial(score_kernel, scale),
        in_specs=[SMEM] + [pl.BlockSpec(memory_space=pltpu.VMEM)] * 6,
        out_specs=[pl.BlockSpec(memory_space=pltpu.VMEM)] * chunks,
        out_shape=[jax.ShapeDtypeStruct((heads, rows, 2 * residues), BF16)] * chunks,
        scratch_shapes=[pltpu.VMEM((residues, 2 * residues), hold_type(rows))],
        compiler_params=params(),
        cost_estimate=cost(8 * heads * residues * residues * depth, 2 * nbytes(*args)),
    )(z, *args)


def softmax_kernel(*refs):
    terms, out = refs[:-1], refs[-1]
    total = terms[0][...].astype(F32)
    for term in terms[1:]:
        total = total + term[...].astype(F32)
    top = jnp.max(total, axis=-1, keepdims=True)
    grown = jnp.exp(total - top)
    out[...] = (grown / jnp.sum(grown, axis=-1, keepdims=True)).astype(BF16)


def softmax_sum(terms):
    return pl.pallas_call(
        softmax_kernel,
        out_shape=jax.ShapeDtypeStruct(terms[0].shape, BF16),
        compiler_params=params(),
        cost_estimate=cost(10 * terms[0].size, nbytes(*terms), terms[0].size),
    )(*terms)


def value_kernel(chunks, z_ref, *refs):
    pieces, values, others = refs[:chunks], refs[chunks : chunks + 2], refs[chunks + 2 : chunks + 4]
    outs, hold = refs[chunks + 4 : chunks + 6], refs[-1]
    z = z_ref[0]
    heads, rows = pieces[0].shape[0], pieces[0].shape[1]
    residues = values[0].shape[1]
    for head in range(heads):
        for d, piece in enumerate(pieces):
            start = pl.multiple_of(jnp.bitwise_xor(z, d) * rows, rows)
            hold[pl.ds(start, rows), :] = piece[head].astype(hold.dtype)
        near, far = hold[:, :residues].astype(BF16), hold[:, residues:].astype(BF16)
        for value, other, out in zip(values, others, outs):
            out[head] = (dot(near, value[head]) + dot(far, other[head])).astype(BF16)


def weighted_values(z, pieces, values, others):
    heads, residues, depth = values[0].shape
    args = (*pieces, *values, *others)
    return pl.pallas_call(
        functools.partial(value_kernel, len(pieces)),
        in_specs=[SMEM] + [pl.BlockSpec(memory_space=pltpu.VMEM)] * len(args),
        out_specs=[pl.BlockSpec(memory_space=pltpu.VMEM)] * 2,
        out_shape=[jax.ShapeDtypeStruct((heads, residues, depth), BF16)] * 2,
        scratch_shapes=[pltpu.VMEM((residues, 2 * residues), hold_type(pieces[0].shape[1]))],
        compiler_params=params(),
        cost_estimate=cost(8 * heads * residues * residues * depth, 2 * nbytes(*args)),
    )(z, *args)


def normalized(attended, x, out_weight, gain, s):
    columns = [
        ref[head][:, s * HEAD_DIM : (s + 1) * HEAD_DIM] for ref in attended for head in range(ref.shape[0])
    ]
    rows = jnp.concatenate(columns, axis=1)
    summed = x[s].astype(F32) + dot(rows, out_weight[...])
    mean_sq = jnp.mean(summed * summed, axis=-1, keepdims=True)
    return summed * lax.rsqrt(mean_sq + epsilon) * gain[...].astype(F32)


def next_kernel(heads, a0, a1, a2, a3, x, out_weight, gain, weight, x_out, q_out, k_out, v_out):
    pair = []
    for s in range(2):
        rows = normalized((a0, a1, a2, a3), x, out_weight, gain, s).astype(BF16)
        x_out[s] = rows
        pair.append(rows)
    store_projections(pair, weight[...], heads, (q_out, k_out, v_out))


def next_layer(attended, x, out_weight, gain, weight):
    seqs, residues, width = x.shape
    heads = attended[0].shape[0]
    lanes = 2 * HEAD_DIM
    wide = jax.ShapeDtypeStruct((heads, residues, seqs * HEAD_DIM), BF16)
    block = pl.BlockSpec((heads, residues, lanes), lambda p: (0, 0, p))
    x_block = pl.BlockSpec((2, residues, width), lambda p: (p, 0, 0))
    flops = 2 * seqs * residues * width * (weight.shape[1] + width)
    return pl.pallas_call(
        functools.partial(next_kernel, heads),
        grid=(seqs // 2,),
        in_specs=[block] * 4 + [x_block, whole(out_weight), whole(gain), whole(weight)],
        out_specs=[x_block] + [block] * 3,
        out_shape=[jax.ShapeDtypeStruct(x.shape, BF16)] + [wide] * 3,
        compiler_params=params(),
        cost_estimate=cost(flops, 4 * nbytes(x) + nbytes(out_weight, weight)),
    )(*attended, x, out_weight, gain, weight)


def last_kernel(place, a0, a1, a2, a3, x, out_weight, gain, keep, send):
    x_bit, core = place[0], place[1]
    quarter = keep.shape[2]
    for s in range(2):
        rows = normalized((a0, a1, a2, a3), x, out_weight, gain, s)
        half = jnp.where(x_bit == 1, rows[:, 2 * quarter :], rows[:, : 2 * quarter])
        low, high = half[:, :quarter], half[:, quarter:]
        keep[s] = jnp.where(core == 1, high, low).astype(BF16)
        send[s] = jnp.where(core == 1, low, high).astype(BF16)


def last_layer(place, attended, x, out_weight, gain):
    seqs, residues, width = x.shape
    heads = attended[0].shape[0]
    block = pl.BlockSpec((heads, residues, 2 * HEAD_DIM), lambda p: (0, 0, p))
    x_block = pl.BlockSpec((2, residues, width), lambda p: (p, 0, 0))
    out_block = pl.BlockSpec((2, residues, width // 4), lambda p: (p, 0, 0))
    return pl.pallas_call(
        last_kernel,
        grid=(seqs // 2,),
        in_specs=[SMEM] + [block] * 4 + [x_block, whole(out_weight), whole(gain)],
        out_specs=[out_block] * 2,
        out_shape=[jax.ShapeDtypeStruct((seqs, residues, width // 4), BF16)] * 2,
        compiler_params=params(),
        cost_estimate=cost(2 * seqs * residues * width * width, 3 * nbytes(x) + nbytes(out_weight)),
    )(place, *attended, x, out_weight, gain)


def on_device(tokens, qkv_weight, out_weight, norm_gain):
    seqs, residues, _ = tokens.shape
    layers, width = norm_gain.shape
    n_rows, n_groups = lax.axis_size("rows"), lax.axis_size("heads")
    all_heads = width // HEAD_DIM
    row, group = lax.axis_index("rows"), lax.axis_index("heads")
    core, x_bit = group % 2, group // 2
    y_bit, z = row % 2, row // 2
    depth = n_rows // 2
    own = x_bit * 2 + y_bit
    heads = all_heads // 4
    own_width = heads * HEAD_DIM
    half = residues // 2
    scale = 1.0 / (HEAD_DIM * seqs * n_rows) ** 0.5
    place = jnp.stack([x_bit, core]).astype(jnp.int32)
    z_at = z.astype(jnp.int32).reshape(1)

    def over_core(a):
        return lax.ppermute(a, "heads", [(i, i ^ 1) for i in range(n_groups)])

    def over_x(a):
        return lax.ppermute(a, "heads", [(i, i ^ 2) for i in range(n_groups)])

    def over_y(a):
        return lax.ppermute(a, "rows", [(i, i ^ 1) for i in range(n_rows)])

    def over_z(a, d):
        return lax.ppermute(a, "rows", [(i, i ^ (2 * d)) for i in range(n_rows)])

    def own_columns(layer):
        columns = lax.dynamic_slice_in_dim(qkv_weight[layer], own * own_width, own_width, 2)
        return columns.reshape(width, 3 * own_width)

    def out_rows(layer):
        parts = [
            lax.dynamic_slice_in_dim(out_weight[layer], (own ^ d) * own_width, own_width, 0)
            for d in (0, 2, 1, 3)
        ]
        return jnp.concatenate(parts, axis=0)

    mine = lax.dynamic_slice_in_dim(tokens, core * half, half, 1)
    theirs = lax.dynamic_slice_in_dim(tokens, (1 - core) * half, half, 1)
    packed = jnp.concatenate([mine, over_core(theirs)], axis=2)
    cut = seqs // 2
    lows, highs = packed[:cut], packed[cut:]
    x_low, x_high = over_x(lows), over_x(highs)
    y_low, y_high = over_y(lows), over_y(highs)
    d_low, d_high = over_y(x_low), over_x(y_high)
    weight = own_columns(0)
    streams, queries, keys, values = [], [], [], []
    for near, far in (
        (packed, jnp.concatenate([x_low, x_high])),
        (jnp.concatenate([y_low, y_high]), jnp.concatenate([d_low, d_high])),
    ):
        made = first(place, near, far, weight, heads)
        for kept, one in zip((streams, queries, keys, values), made):
            kept.append(one)

    for layer in range(layers):
        other_keys = [over_core(k) for k in keys]
        other_values = [over_core(v) for v in values]
        chunks = score_chunks(z_at, queries, keys, other_keys, scale, depth)
        terms = [chunks[0]] + [over_z(chunks[d], d) for d in range(1, depth)]
        weights = softmax_sum(terms)
        pieces = [weights] + [over_z(weights, d) for d in range(1, depth)]
        near, far = weighted_values(z_at, pieces, values, other_values)
        gain = norm_gain[layer : layer + 1]
        if layer + 1 < layers:
            x_near, x_far = over_x(near), over_x(far)
            y_far, y_near = over_y(near), over_y(far)
            d_far = over_y(x_near)
            d_near = over_x(y_near)
            weight, out_mat = own_columns(layer + 1), out_rows(layer)
            queries, keys, values, new_streams = [], [], [], []
            for attended, x in (
                ((near, x_near, y_near, d_near), streams[0]),
                ((far, x_far, y_far, d_far), streams[1]),
            ):
                made = next_layer(attended, x, out_mat, gain, weight)
                for kept, one in zip((new_streams, queries, keys, values), made):
                    kept.append(one)
            streams = new_streams
        else:
            x_near, y_near = over_x(near), over_y(far)
            d_near = over_x(y_near)
            keep, send = last_layer(
                place, (near, x_near, y_near, d_near), streams[0], out_rows(layer), gain
            )
    other = over_core(send)
    ordered = [jnp.where(core == 0, keep, other), jnp.where(core == 0, other, keep)]
    return jnp.concatenate(ordered, axis=1)


def solution(mesh):
    return jax.shard_map(
        on_device,
        mesh=mesh,
        in_specs=(P("rows", None, "heads"), P(), P(), P()),
        out_specs=P("rows", None, "heads"),
        check_vma=False,
    )
```

time: 490 us -> 195 us (0.40)
  waiting for transfers between devices: 380 us -> 95.4 us
  starting transfers between devices: 0.39 us -> 44.1 us
  matrix products: 33.8 us -> 0 us
  Pallas kernels: 0 us -> 22 us
  between operations: 13.7 us -> 0.29 us
  local copies, waits for them, and re-layouts: 37.1 us -> 23.8 us
  blocking collectives: 11.7 us -> 0 us
  other arithmetic: 12.5 us -> 5.73 us
    psum x2 -> x0, waiting for transfers between devices: 256 us -> none  [attend(): scores = lax.psum(partial_value, 'rows')]
    ppermute x0 -> x37, waiting for transfers between devices: none -> 95.4 us  [the longest x12 53.8 us: over_z(): return lax.ppermute(a, 'rows', [(i, i ^ 2 * d) for i in range(n_rows)])]
    reduce_scatter x2 -> x0, waiting for transfers between devices: 73.2 us -> none  [on_device(): lax.psum_scatter(update.astype(jnp.bfloat16), 'heads', scatter_dimension=...]
    all_gather x2 -> x0, waiting for transfers between devices: 50.5 us -> none  [on_device(): portion = lax.all_gather(stream, 'heads', axis=2, tiled=True)]
    ppermute x0 -> x37, starting transfers between devices: none -> 44.1 us  [the longest x12 25.8 us: over_z(): return lax.ppermute(a, 'rows', [(i, i ^ 2 * d) for i in range(n_rows)])]
    dot_general x12 -> x0, matrix products: 33.8 us -> none  [the longest x4 11.8 us: attend(): jnp.einsum('hij,sjhc->sihc', weights, values, preferred_element_type=jnp....]
    pallas_call x0 -> x11, Pallas kernels: none -> 22 us  [the longest x2 8.93 us: next_layer(): pl.pallas_call(functools.partial(next_kernel, heads), grid=(seqs // 2,),...]
    psum x2 -> x0, blocking collectives: 11.7 us -> none  [on_device(): lax.psum(jnp.sum(summed * summed, axis=-1, keepdims=True), 'heads')]
  transfers between devices with their start and end apart: 6 -> 37, of which waited for: 6 -> 21; matrix products, arithmetic and copies ran while one was open for 2% -> 13% of each run, Pallas kernels for 0% -> 8%
where the time goes in v1:
time: 195 us; the launch traced here: 191 us
  waiting for transfers between devices  95.4 us (49%)
  starting transfers between devices  44.1 us (23%)
  local copies, waits for them, and re-layouts  23.8 us (12%)
  Pallas kernels  22 us (11%)
  other arithmetic  5.73 us (3%)
    ppermute x12, waiting for transfers between devices, over_z(): return lax.ppermute(a, 'rows', [(i, i ^ 2 * d) for i in range(n_rows)])  53.8 us
    ppermute x12, starting transfers between devices, over_z(): return lax.ppermute(a, 'rows', [(i, i ^ 2 * d) for i in range(n_rows)])  25.8 us
    ppermute x7, waiting for transfers between devices, over_y(): return lax.ppermute(a, 'rows', [(i, i ^ 1) for i in range(n_rows)])  20.7 us
    ppermute x8, waiting for transfers between devices, over_x(): return lax.ppermute(a, 'heads', [(i, i ^ 2) for i in range(n_groups)])  14.4 us
    ppermute x8, starting transfers between devices, over_x(): return lax.ppermute(a, 'heads', [(i, i ^ 2) for i in range(n_groups)])  9.8 us
    pallas_call x2, Pallas kernels, next_layer(): pl.pallas_call(functools.partial(next_kernel, heads), grid=(seqs // 2,),...  8.93 us
    ppermute x10, waiting for transfers between devices, over_core(): return lax.ppermute(a, 'heads', [(i, i ^ 1) for i in range(n_groups)])  6.5 us
    ppermute x7, starting transfers between devices, over_y(): return lax.ppermute(a, 'rows', [(i, i ^ 1) for i in range(n_rows)])  6.25 us
  transfers between devices with their start and end apart: 37, of which 21 were waited for; matrix products, arithmetic and copies ran while one was open for 13% of the time, Pallas kernels for 8%

profile of v1, /device:TPU:0, one launch (start us, length us, event | category | flops | bytes accessed | tf_op | source)
XLA Modules:
  0.0 191.3 jit_solution(8425881596256096364)
XLA Ops:
  4.6 2.9 %collective-permute-start.1 = (bf16[2,256,384]{2,1,0:T(8,128)(2,1)}, bf16[2,256,384]{2,1,0:T(8,128)(2,1)}, u32[]{:S(2)}, u32[]{:S(2)}) collective-permute-start(bf16[2,256,384]{2,1,0:T(8,128)(2,1)} %get-tuple-element.77), channel_id=1, source_target_pairs={{0,2},{1,3},{2,0},{3,1},{4,6},{5,7},{6,4},{7,5},{8,10},{9,11},{10,... | collective-permute-start | bytes 1179656 | tf_op jit(solution)/shard_map/ppermute | solution.py:259
  9.0 5.3 %fusion.2 = (bf16[1,768,3,768]{3,1,2,0:T(8,128)(2,1)S(1)}, bf16[1,768,3,768]{3,1,2,0:T(8,128)(2,1)}) fusion(bf16[2,768,3,768]{3,1,2,0:T(8,128)(2,1)} %param.5), kind=kLoop, calls=%fused_computation.28 | loop fusion | bytes 14155776 | tf_op jit(solution)/shard_map/slice | solution.py:268
  14.9 4.2 %constant_dynamic-slice_fusion = (bf16[1,768,3,192]{3,1,2,0:T(8,128)(2,1)}, bf16[1,768,3,192]{3,1,2,0:T(8,128)(2,1)}) fusion(bf16[1,768,3,768]{3,1,2,0:T(8,128)(2,1)S(1)} %get-tuple-element.63, s32[]{:T(128)S(6)} %select_n.61, bf16[1,768,3,768]{3,1,2,0:T(8,128)(2,1)} %get-tuple-element.64), kind=kLoop, calls=%fused_computation.23 | loop fusion | bytes 3538948 | tf_op jit(solution)/shard_map/dynamic_slice | solution.py:268
  19.2 1.9 copy.22
  21.8 2.0 %collective-permute-start.5 = (bf16[2,256,384]{2,1,0:T(8,128)(2,1)}, bf16[2,256,384]{2,1,0:T(8,128)(2,1)S(1)}, u32[]{:S(2)}, u32[]{:S(2)}) collective-permute-start(bf16[2,256,384]{2,1,0:T(8,128)(2,1)} %collective-permute-done.1), channel_id=1, source_target_pairs={{0,4},{4,0},{8,12},{12,8},{16,20},{20,16},{24,28},{28,24},{1,5},{5... | collective-permute-start | bytes 1179656 | tf_op jit(solution)/shard_map/ppermute | solution.py:262
  27.0 2.6 %shard_map.46 = (bf16[4,256,768]{2,1,0:T(8,128)(2,1)S(1)}, bf16[3,256,256]{2,1,0:T(8,128)(2,1)S(1)}, bf16[3,256,256]{2,1,0:T(8,128)(2,1)S(1)}, bf16[3,256,256]{2,1,0:T(8,128)(2,1)S(1)}) custom-call(s32[2]{0:T(128)S(1)} %pad_add_fusion.place, bf16[4,256,384]{2,1,0:T(8,128)(2,1)S(1)} %pad_maximum_fusion.3.near, ...), custom_call_target="tpu_custom_call" | custom-call | flops 905969664 | bytes 7176192 | tf_op jit(solution)/shard_map/pallas_call | solution.py:83
  32.5 5.6 %collective-permute-done.5 = bf16[2,256,384]{2,1,0:T(8,128)(2,1)S(1)} collective-permute-done((bf16[2,256,384]{2,1,0:T(8,128)(2,1)}, bf16[2,256,384]{2,1,0:T(8,128)(2,1)S(1)}, u32[]{:S(2)}, u32[]{:S(2)}) %collective-permute-start.5) | collective-permute-done | bytes 393248 | tf_op jit(solution)/shard_map/ppermute | solution.py:262
  38.2 3.2 %shard_map.47 = (bf16[4,256,768]{2,1,0:T(8,128)(2,1)S(1)}, bf16[3,256,256]{2,1,0:T(8,128)(2,1)S(1)}, bf16[3,256,256]{2,1,0:T(8,128)(2,1)}, bf16[3,256,256]{2,1,0:T(8,128)(2,1)S(1)}) custom-call(s32[2]{0:T(128)S(1)} %pad_add_fusion.place, bf16[4,256,384]{2,1,0:T(8,128)(2,1)S(1)} %pad_maximum_fusion.5.near, bf16[4,256,384]{2,1,0:T(8,128)(2,1)S(1)} %pad_maximum_fusion.6.far, ...), custom_call_target="tpu_custom_call" | custom-call | flops 905969664 | bytes 7176192 | tf_op jit(solution)/shard_map/pallas_call | solution.py:83
  42.6 1.9 %collective-permute-done.8.refs_5_ = bf16[3,256,256]{2,1,0:T(8,128)(2,1)S(1)} collective-permute-done((bf16[3,256,256]{2,1,0:T(8,128)(2,1)}, bf16[3,256,256]{2,1,0:T(8,128)(2,1)S(1)}, u32[]{:S(2)}, u32[]{:S(2)}) %collective-permute-start.8) | collective-permute-done | bytes 393248 | tf_op jit(solution)/shard_map/ppermute | solution.py:256
  46.1 2.6 %collective-permute-start.10 = (bf16[3,64,512]{2,1,0:T(8,128)(2,1)S(1)}, bf16[3,64,512]{2,1,0:T(8,128)(2,1)S(1)}, u32[]{:S(2)}, u32[]{:S(2)}) collective-permute-start(bf16[3,64,512]{2,1,0:T(8,128)(2,1)S(1)} %get-tuple-element.40), channel_id=1, source_target_pairs={{0,16},{4,20},{8,24},{12,28},{16,0},{20,4},{24,8},{28,12},{1,17},{... | collective-permute-start | bytes 589832 | tf_op jit(solution)/shard_map/ppermute | solution.py:265
  50.9 12.4 %collective-permute-done.10.refs_2_ = bf16[3,64,512]{2,1,0:T(8,128)(2,1)S(1)} collective-permute-done((bf16[3,64,512]{2,1,0:T(8,128)(2,1)S(1)}, bf16[3,64,512]{2,1,0:T(8,128)(2,1)S(1)}, u32[]{:S(2)}, u32[]{:S(2)}) %collective-permute-start.10) | collective-permute-done | bytes 196640 | tf_op jit(solution)/shard_map/ppermute | solution.py:265
  64.1 3.6 %collective-permute-start.12 = (bf16[3,64,512]{2,1,0:T(8,128)(2,1)S(1)}, bf16[3,64,512]{2,1,0:T(8,128)(2,1)S(1)}, u32[]{:S(2)}, u32[]{:S(2)}) collective-permute-start(bf16[3,64,512]{2,1,0:T(8,128)(2,1)S(1)} %shard_map.49.refs_0_), channel_id=1, source_target_pairs={{0,8},{4,12},{8,0},{12,4},{16,24},{20,28},{24,16},{28,20},{1,9},{5... | collective-permute-start | bytes 589832 | tf_op jit(solution)/shard_map/ppermute | solution.py:265
  67.7 2.0 %collective-permute-start.13 = (bf16[3,64,512]{2,1,0:T(8,128)(2,1)S(1)}, bf16[3,64,512]{2,1,0:T(8,128)(2,1)S(1)}, u32[]{:S(2)}, u32[]{:S(2)}) collective-permute-start(bf16[3,64,512]{2,1,0:T(8,128)(2,1)S(1)} %shard_map.49.refs_0_), channel_id=1, source_target_pairs={{0,16},{4,20},{8,24},{12,28},{16,0},{20,4},{24,8},{28,12},{1,17},{... | collective-permute-start | bytes 589832 | tf_op jit(solution)/shard_map/ppermute | solution.py:265
  71.1 5.6 %collective-permute-done.12.refs_1_ = bf16[3,64,512]{2,1,0:T(8,128)(2,1)S(1)} collective-permute-done((bf16[3,64,512]{2,1,0:T(8,128)(2,1)S(1)}, bf16[3,64,512]{2,1,0:T(8,128)(2,1)S(1)}, u32[]{:S(2)}, u32[]{:S(2)}) %collective-permute-start.12) | collective-permute-done | bytes 196640 | tf_op jit(solution)/shard_map/ppermute | solution.py:265
  76.7 8.1 %collective-permute-done.13.refs_2_ = bf16[3,64,512]{2,1,0:T(8,128)(2,1)S(1)} collective-permute-done((bf16[3,64,512]{2,1,0:T(8,128)(2,1)S(1)}, bf16[3,64,512]{2,1,0:T(8,128)(2,1)S(1)}, u32[]{:S(2)}, u32[]{:S(2)}) %collective-permute-start.13) | collective-permute-done | bytes 196640 | tf_op jit(solution)/shard_map/ppermute | solution.py:265
  91.2 6.4 %collective-permute-done.17.a1 = bf16[3,256,256]{2,1,0:T(8,128)(2,1)S(1)} collective-permute-done((bf16[3,256,256]{2,1,0:T(8,128)(2,1)S(1)}, bf16[3,256,256]{2,1,0:T(8,128)(2,1)S(1)}, u32[]{:S(2)}, u32[]{:S(2)}) %collective-permute-start.17) | collective-permute-done | bytes 393248 | tf_op jit(solution)/shard_map/ppermute | solution.py:259
  98.0 3.1 %dynamic-slice_bitcast_fusion.3 = (bf16[192,768]{1,0:T(8,128)(2,1)}, bf16[192,768]{1,0:T(8,128)(2,1)}, bf16[192,768]{1,0:T(8,128)(2,1)}, bf16[192,768]{1,0:T(8,1...) fusion(bf16[1,768,768]{2,1,0:T(8,128)(2,1)} %get-tuple-element., ...), kind=kLoop, calls=%fused_computation.18 | loop fusion | bytes 4718608 | tf_op jit(solution)/shard_map/dynamic_slice | solution.py:273
  107.5 5.9 %collective-permute-done.22.a3 = bf16[3,256,256]{2,1,0:T(8,128)(2,1)} collective-permute-done((bf16[3,256,256]{2,1,0:T(8,128)(2,1)S(1)}, bf16[3,256,256]{2,1,0:T(8,128)(2,1)}, u32[]{:S(2)}, u32[]{:S(2)}) %collective-permute-start.22) | collective-permute-done | bytes 393248 | tf_op jit(solution)/shard_map/ppermute | solution.py:262
  113.4 4.9 %shard_map.52 = (bf16[4,256,768]{2,1,0:T(8,128)(2,1)}, bf16[3,256,256]{2,1,0:T(8,128)(2,1)S(1)}, bf16[3,256,256]{2,1,0:T(8,128)(2,1)S(1)}, bf16[3,256,256]{2,1,0:T(8,128)(2,1)S(1)}) custom-call(bf16[3,256,256]{2,1,0:T(8,128)(2,1)S(1)} %get-tuple-element.45.a0, bf16[3,256,256]{2,1,0:T(8,128)(2,1)S(1)} %collective-permute-done.20.a1, ...), custom_call_target="tpu_custom_call" | custom-call | flops 2113929216 | bytes 8355840 | tf_op jit(solution)/shard_map/pallas_call | solution.py:199
  118.3 4.1 %shard_map.51 = (bf16[4,256,768]{2,1,0:T(8,128)(2,1)S(1)}, bf16[3,256,256]{2,1,0:T(8,128)(2,1)S(1)}, bf16[3,256,256]{2,1,0:T(8,128)(2,1)S(1)}, bf16[3,256,256]{2,1,0:T(8,128)(2,1)S(1)}) custom-call(bf16[3,256,256]{2,1,0:T(8,128)(2,1)S(1)} %get-tuple-element.44.a0, bf16[3,256,256]{2,1,0:T(8,128)(2,1)S(1)} %collective-permute-done.17.a1, ...), custom_call_target="tpu_custom_call" | custom-call | flops 2113929216 | bytes 8355840 | tf_op jit(solution)/shard_map/pallas_call | solution.py:199
  124.9 3.9 %collective-permute-start.25 = (bf16[3,64,512]{2,1,0:T(8,128)(2,1)S(1)}, bf16[3,64,512]{2,1,0:T(8,128)(2,1)S(1)}, u32[]{:S(2)}, u32[]{:S(2)}) collective-permute-start(bf16[3,64,512]{2,1,0:T(8,128)(2,1)S(1)} %get-tuple-element.53), channel_id=1, source_target_pairs={{0,8},{4,12},{8,0},{12,4},{16,24},{20,28},{24,16},{28,20},{1,9},{5... | collective-permute-start | bytes 589832 | tf_op jit(solution)/shard_map/ppermute | solution.py:265
  128.8 2.0 %collective-permute-start.26 = (bf16[3,64,512]{2,1,0:T(8,128)(2,1)S(1)}, bf16[3,64,512]{2,1,0:T(8,128)(2,1)S(1)}, u32[]{:S(2)}, u32[]{:S(2)}) collective-permute-start(bf16[3,64,512]{2,1,0:T(8,128)(2,1)S(1)} %get-tuple-element.54), channel_id=1, source_target_pairs={{0,16},{4,20},{8,24},{12,28},{16,0},{20,4},{24,8},{28,12},{1,17},{... | collective-permute-start | bytes 589832 | tf_op jit(solution)/shard_map/ppermute | solution.py:265
  132.7 5.7 %collective-permute-done.25.refs_1_ = bf16[3,64,512]{2,1,0:T(8,128)(2,1)S(1)} collective-permute-done((bf16[3,64,512]{2,1,0:T(8,128)(2,1)S(1)}, bf16[3,64,512]{2,1,0:T(8,128)(2,1)S(1)}, u32[]{:S(2)}, u32[]{:S(2)}) %collective-permute-start.25) | collective-permute-done | bytes 196640 | tf_op jit(solution)/shard_map/ppermute | solution.py:265
  138.4 7.5 %collective-permute-done.26.refs_2_ = bf16[3,64,512]{2,1,0:T(8,128)(2,1)S(1)} collective-permute-done((bf16[3,64,512]{2,1,0:T(8,128)(2,1)S(1)}, bf16[3,64,512]{2,1,0:T(8,128)(2,1)S(1)}, u32[]{:S(2)}, u32[]{:S(2)}) %collective-permute-start.26) | collective-permute-done | bytes 196640 | tf_op jit(solution)/shard_map/ppermute | solution.py:265
  146.3 4.0 %collective-permute-start.28 = (bf16[3,64,512]{2,1,0:T(8,128)(2,1)S(1)}, bf16[3,64,512]{2,1,0:T(8,128)(2,1)S(1)}, u32[]{:S(2)}, u32[]{:S(2)}) collective-permute-start(bf16[3,64,512]{2,1,0:T(8,128)(2,1)S(1)} %shard_map.54.refs_0_), channel_id=1, source_target_pairs={{0,8},{4,12},{8,0},{12,4},{16,24},{20,28},{24,16},{28,20},{1,9},{5... | collective-permute-start | bytes 589832 | tf_op jit(solution)/shard_map/ppermute | solution.py:265
  150.2 2.0 %collective-permute-start.29 = (bf16[3,64,512]{2,1,0:T(8,128)(2,1)S(1)}, bf16[3,64,512]{2,1,0:T(8,128)(2,1)S(1)}, u32[]{:S(2)}, u32[]{:S(2)}) collective-permute-start(bf16[3,64,512]{2,1,0:T(8,128)(2,1)S(1)} %shard_map.54.refs_0_), channel_id=1, source_target_pairs={{0,16},{4,20},{8,24},{12,28},{16,0},{20,4},{24,8},{28,12},{1,17},{... | collective-permute-start | bytes 589832 | tf_op jit(solution)/shard_map/ppermute | solution.py:265
  153.6 4.0 %collective-permute-done.28.refs_1_ = bf16[3,64,512]{2,1,0:T(8,128)(2,1)S(1)} collective-permute-done((bf16[3,64,512]{2,1,0:T(8,128)(2,1)S(1)}, bf16[3,64,512]{2,1,0:T(8,128)(2,1)S(1)}, u32[]{:S(2)}, u32[]{:S(2)}) %collective-permute-start.28) | collective-permute-done | bytes 196640 | tf_op jit(solution)/shard_map/ppermute | solution.py:265
  157.6 9.8 %collective-permute-done.29.refs_2_ = bf16[3,64,512]{2,1,0:T(8,128)(2,1)S(1)} collective-permute-done((bf16[3,64,512]{2,1,0:T(8,128)(2,1)S(1)}, bf16[3,64,512]{2,1,0:T(8,128)(2,1)S(1)}, u32[]{:S(2)}, u32[]{:S(2)}) %collective-permute-start.29) | collective-permute-done | bytes 196640 | tf_op jit(solution)/shard_map/ppermute | solution.py:265
  169.1 7.0 %collective-permute-done.34.a2 = bf16[3,256,256]{2,1,0:T(8,128)(2,1)S(1)} collective-permute-done((bf16[3,256,256]{2,1,0:T(8,128)(2,1)S(1)}, bf16[3,256,256]{2,1,0:T(8,128)(2,1)S(1)}, u32[]{:S(2)}, u32[]{:S(2)}) %collective-permute-start.34) | collective-permute-done | bytes 393248 | tf_op jit(solution)/shard_map/ppermute | solution.py:262
  177.5 7.1 %collective-permute-done.35.a3 = bf16[3,256,256]{2,1,0:T(8,128)(2,1)S(1)} collective-permute-done((bf16[3,256,256]{2,1,0:T(8,128)(2,1)S(1)}, bf16[3,256,256]{2,1,0:T(8,128)(2,1)S(1)}, u32[]{:S(2)}, u32[]{:S(2)}) %collective-permute-start.35) | collective-permute-done | bytes 393248 | tf_op jit(solution)/shard_map/ppermute | solution.py:259
  184.6 3.3 %shard_map.56 = (bf16[4,256,192]{2,1,0:T(8,128)(2,1)S(1)}, bf16[4,256,192]{2,1,0:T(8,128)(2,1)S(1)}) custom-call(s32[2]{0:T(128)S(1)} %pad_add_fusion.place, bf16[3,256,256]{2,1,0:T(8,128)(2,1)S(1)} %get-tuple-element.58.a0, bf16[3,256,256]{2,1,0:T(8,128)(2,1)S(1)} %collective-permute-done.33.a1, bf16[3,256,256]{2,1,0:T(8,128)(2,1)S(1)} %collective-permute-done.34.a2, ...), custom_call_target="tpu_custom_call" | custom-call | flops 1207959552 | bytes 5898240 | tf_op jit(solution)/shard_map/pallas_call | solution.py:227
  187.9 1.9 collective-permute-done.36
  (106 shorter events, 44.4 us)
Async XLA Ops:
  4.6 17.1 %collective-permute-start.1 = (bf16[2,256,384]{2,1,0:T(8,128)(2,1)}, bf16[2,256,384]{2,1,0:T(8,128)(2,1)}, u32[]{:S(2)}, u32[]{:S(2)}) collective-permute-start(bf16[2,256,384]{2,1,0:T(8,128)(2,1)} %get-tuple-element.77), channel_id=1, source_target_pairs={{0,2},{1,3},{2,0},{3,1},{4,6},{5,7},{6,4},{7,5},{8,10},{9,11},{10,... | collective-permute-start | bytes 1179656 | tf_op jit(solution)/shard_map/ppermute | solution.py:259
  7.5 16.3 %collective-permute-start.4 = (bf16[2,256,384]{2,1,0:T(8,128)(2,1)}, bf16[2,256,384]{2,1,0:T(8,128)(2,1)}, u32[]{:S(2)}, u32[]{:S(2)}) collective-permute-start(bf16[2,256,384]{2,1,0:T(8,128)(2,1)} %get-tuple-element.78), channel_id=1, source_target_pairs={{0,4},{4,0},{8,12},{12,8},{16,20},{20,16},{24,28},{28,24},{1,5},{5... | collective-permute-start | bytes 1179656 | tf_op jit(solution)/shard_map/ppermute | solution.py:262
  14.3 11.4 %collective-permute-start.2 = (bf16[2,256,384]{2,1,0:T(8,128)(2,1)}, bf16[2,256,384]{2,1,0:T(8,128)(2,1)}, u32[]{:S(2)}, u32[]{:S(2)}) collective-permute-start(bf16[2,256,384]{2,1,0:T(8,128)(2,1)} %get-tuple-element.78), channel_id=1, source_target_pairs={{0,2},{1,3},{2,0},{3,1},{4,6},{5,7},{6,4},{7,5},{8,10},{9,11},{10,... | collective-permute-start | bytes 1179656 | tf_op jit(solution)/shard_map/ppermute | solution.py:259
  19.1 12.3 %collective-permute-start.3 = (bf16[2,256,384]{2,1,0:T(8,128)(2,1)}, bf16[2,256,384]{2,1,0:T(8,128)(2,1)S(1)}, u32[]{:S(2)}, u32[]{:S(2)}) collective-permute-start(bf16[2,256,384]{2,1,0:T(8,128)(2,1)} %get-tuple-element.77), channel_id=1, source_target_pairs={{0,4},{4,0},{8,12},{12,8},{16,20},{20,16},{24,28},{28,24},{1,5},{5... | collective-permute-start | bytes 1179656 | tf_op jit(solution)/shard_map/ppermute | solution.py:262
  21.8 16.3 %collective-permute-start.5 = (bf16[2,256,384]{2,1,0:T(8,128)(2,1)}, bf16[2,256,384]{2,1,0:T(8,128)(2,1)S(1)}, u32[]{:S(2)}, u32[]{:S(2)}) collective-permute-start(bf16[2,256,384]{2,1,0:T(8,128)(2,1)} %collective-permute-done.1), channel_id=1, source_target_pairs={{0,4},{4,0},{8,12},{12,8},{16,20},{20,16},{24,28},{28,24},{1,5},{5... | collective-permute-start | bytes 1179656 | tf_op jit(solution)/shard_map/ppermute | solution.py:262
  23.8 14.2 %collective-permute-start.6 = (bf16[2,256,384]{2,1,0:T(8,128)(2,1)}, bf16[2,256,384]{2,1,0:T(8,128)(2,1)S(1)}, u32[]{:S(2)}, u32[]{:S(2)}) collective-permute-start(bf16[2,256,384]{2,1,0:T(8,128)(2,1)} %collective-permute-done.4), channel_id=1, source_target_pairs={{0,2},{1,3},{2,0},{3,1},{4,6},{5,7},{6,4},{7,5},{8,10},{9,11},{10,... | collective-permute-start | bytes 1179656 | tf_op jit(solution)/shard_map/ppermute | solution.py:259
  29.6 12.9 %collective-permute-start.7 = (bf16[3,256,256]{2,1,0:T(8,128)(2,1)S(1)}, bf16[3,256,256]{2,1,0:T(8,128)(2,1)S(1)}, u32[]{:S(2)}, u32[]{:S(2)}) collective-permute-start(bf16[3,256,256]{2,1,0:T(8,128)(2,1)S(1)} %get-tuple-element.36.refs_2_), channel_id=1, source_target_pairs={{0,1},{1,0},{2,3},{3,2},{4,5},{5,4},{6,7},{7,6},{8,9},{9,8},{10,11... | collective-permute-start | bytes 1179656 | tf_op jit(solution)/shard_map/ppermute | solution.py:256
  46.1 17.2 %collective-permute-start.10 = (bf16[3,64,512]{2,1,0:T(8,128)(2,1)S(1)}, bf16[3,64,512]{2,1,0:T(8,128)(2,1)S(1)}, u32[]{:S(2)}, u32[]{:S(2)}) collective-permute-start(bf16[3,64,512]{2,1,0:T(8,128)(2,1)S(1)} %get-tuple-element.40), channel_id=1, source_target_pairs={{0,16},{4,20},{8,24},{12,28},{16,0},{20,4},{24,8},{28,12},{1,17},{... | collective-permute-start | bytes 589832 | tf_op jit(solution)/shard_map/ppermute | solution.py:265
  48.8 14.5 %collective-permute-start.11 = (bf16[3,64,512]{2,1,0:T(8,128)(2,1)S(1)}, bf16[3,64,512]{2,1,0:T(8,128)(2,1)S(1)}, u32[]{:S(2)}, u32[]{:S(2)}) collective-permute-start(bf16[3,64,512]{2,1,0:T(8,128)(2,1)S(1)} %get-tuple-element.41), channel_id=1, source_target_pairs={{0,24},{4,28},{8,16},{12,20},{16,8},{20,12},{24,0},{28,4},{1,25},{... | collective-permute-start | bytes 589832 | tf_op jit(solution)/shard_map/ppermute | solution.py:265
  50.1 13.8 %collective-permute-start.9 = (bf16[3,64,512]{2,1,0:T(8,128)(2,1)S(1)}, bf16[3,64,512]{2,1,0:T(8,128)(2,1)S(1)}, u32[]{:S(2)}, u32[]{:S(2)}) collective-permute-start(bf16[3,64,512]{2,1,0:T(8,128)(2,1)S(1)} %get-tuple-element.39), channel_id=1, source_target_pairs={{0,8},{4,12},{8,0},{12,4},{16,24},{20,28},{24,16},{28,20},{1,9},{5... | collective-permute-start | bytes 589832 | tf_op jit(solution)/shard_map/ppermute | solution.py:265
  50.4 20.7 %collective-permute-start.15 = (bf16[3,256,256]{2,1,0:T(8,128)(2,1)S(1)}, bf16[3,256,256]{2,1,0:T(8,128)(2,1)S(1)}, u32[]{:S(2)}, u32[]{:S(2)}) collective-permute-start(bf16[3,256,256]{2,1,0:T(8,128)(2,1)S(1)} %get-tuple-element.42.refs_4_), channel_id=1, source_target_pairs={{0,1},{1,0},{2,3},{3,2},{4,5},{5,4},{6,7},{7,6},{8,9},{9,8},{10,11... | collective-permute-start | bytes 1179656 | tf_op jit(solution)/shard_map/ppermute | solution.py:256
  50.4 20.7 %collective-permute-start.16 = (bf16[3,256,256]{2,1,0:T(8,128)(2,1)S(1)}, bf16[3,256,256]{2,1,0:T(8,128)(2,1)S(1)}, u32[]{:S(2)}, u32[]{:S(2)}) collective-permute-start(bf16[3,256,256]{2,1,0:T(8,128)(2,1)S(1)} %get-tuple-element.43.refs_5_), channel_id=1, source_target_pairs={{0,1},{1,0},{2,3},{3,2},{4,5},{5,4},{6,7},{7,6},{8,9},{9,8},{10,11... | collective-permute-start | bytes 1179656 | tf_op jit(solution)/shard_map/ppermute | solution.py:256
  64.1 12.6 %collective-permute-start.12 = (bf16[3,64,512]{2,1,0:T(8,128)(2,1)S(1)}, bf16[3,64,512]{2,1,0:T(8,128)(2,1)S(1)}, u32[]{:S(2)}, u32[]{:S(2)}) collective-permute-start(bf16[3,64,512]{2,1,0:T(8,128)(2,1)S(1)} %shard_map.49.refs_0_), channel_id=1, source_target_pairs={{0,8},{4,12},{8,0},{12,4},{16,24},{20,28},{24,16},{28,20},{1,9},{5... | collective-permute-start | bytes 589832 | tf_op jit(solution)/shard_map/ppermute | solution.py:265
  67.7 17.1 %collective-permute-start.13 = (bf16[3,64,512]{2,1,0:T(8,128)(2,1)S(1)}, bf16[3,64,512]{2,1,0:T(8,128)(2,1)S(1)}, u32[]{:S(2)}, u32[]{:S(2)}) collective-permute-start(bf16[3,64,512]{2,1,0:T(8,128)(2,1)S(1)} %shard_map.49.refs_0_), channel_id=1, source_target_pairs={{0,16},{4,20},{8,24},{12,28},{16,0},{20,4},{24,8},{28,12},{1,17},{... | collective-permute-start | bytes 589832 | tf_op jit(solution)/shard_map/ppermute | solution.py:265
  69.7 15.1 %collective-permute-start.14 = (bf16[3,64,512]{2,1,0:T(8,128)(2,1)S(1)}, bf16[3,64,512]{2,1,0:T(8,128)(2,1)S(1)}, u32[]{:S(2)}, u32[]{:S(2)}) collective-permute-start(bf16[3,64,512]{2,1,0:T(8,128)(2,1)S(1)} %shard_map.49.refs_0_), channel_id=1, source_target_pairs={{0,24},{4,28},{8,16},{12,20},{16,8},{20,12},{24,0},{28,4},{1,25},{... | collective-permute-start | bytes 589832 | tf_op jit(solution)/shard_map/ppermute | solution.py:265
  85.4 12.1 %collective-permute-start.17 = (bf16[3,256,256]{2,1,0:T(8,128)(2,1)S(1)}, bf16[3,256,256]{2,1,0:T(8,128)(2,1)S(1)}, u32[]{:S(2)}, u32[]{:S(2)}) collective-permute-start(bf16[3,256,256]{2,1,0:T(8,128)(2,1)S(1)} %get-tuple-element.44.a0), channel_id=1, source_target_pairs={{0,2},{1,3},{2,0},{3,1},{4,6},{5,7},{6,4},{7,5},{8,10},{9,11},{10,... | collective-permute-start | bytes 1179656 | tf_op jit(solution)/shard_map/ppermute | solution.py:259
  87.0 18.6 %collective-permute-start.18 = (bf16[3,256,256]{2,1,0:T(8,128)(2,1)S(1)}, bf16[3,256,256]{2,1,0:T(8,128)(2,1)S(1)}, u32[]{:S(2)}, u32[]{:S(2)}) collective-permute-start(bf16[3,256,256]{2,1,0:T(8,128)(2,1)S(1)} %get-tuple-element.45.a0), channel_id=1, source_target_pairs={{0,4},{4,0},{8,12},{12,8},{16,20},{20,16},{24,28},{28,24},{1,5},{5... | collective-permute-start | bytes 1179656 | tf_op jit(solution)/shard_map/ppermute | solution.py:262
  88.9 18.0 %collective-permute-start.20 = (bf16[3,256,256]{2,1,0:T(8,128)(2,1)S(1)}, bf16[3,256,256]{2,1,0:T(8,128)(2,1)S(1)}, u32[]{:S(2)}, u32[]{:S(2)}) collective-permute-start(bf16[3,256,256]{2,1,0:T(8,128)(2,1)S(1)} %get-tuple-element.45.a0), channel_id=1, source_target_pairs={{0,2},{1,3},{2,0},{3,1},{4,6},{5,7},{6,4},{7,5},{8,10},{9,11},{10,... | collective-permute-start | bytes 1179656 | tf_op jit(solution)/shard_map/ppermute | solution.py:259
  89.7 17.8 %collective-permute-start.21 = (bf16[3,256,256]{2,1,0:T(8,128)(2,1)S(1)}, bf16[3,256,256]{2,1,0:T(8,128)(2,1)S(1)}, u32[]{:S(2)}, u32[]{:S(2)}) collective-permute-start(bf16[3,256,256]{2,1,0:T(8,128)(2,1)S(1)} %get-tuple-element.44.a0), channel_id=1, source_target_pairs={{0,4},{4,0},{8,12},{12,8},{16,20},{20,16},{24,28},{28,24},{1,5},{5... | collective-permute-start | bytes 1179656 | tf_op jit(solution)/shard_map/ppermute | solution.py:262
  97.5 15.9 %collective-permute-start.22 = (bf16[3,256,256]{2,1,0:T(8,128)(2,1)S(1)}, bf16[3,256,256]{2,1,0:T(8,128)(2,1)}, u32[]{:S(2)}, u32[]{:S(2)}) collective-permute-start(bf16[3,256,256]{2,1,0:T(8,128)(2,1)S(1)} %collective-permute-done.17.a1), channel_id=1, source_target_pairs={{0,4},{4,0},{8,12},{12,8},{16,20},{20,16},{24,28},{28,24},{1,5},{5... | collective-permute-start | bytes 1179656 | tf_op jit(solution)/shard_map/ppermute | solution.py:262
  105.6 12.7 %collective-permute-start.19 = (bf16[3,256,256]{2,1,0:T(8,128)(2,1)S(1)}, bf16[3,256,256]{2,1,0:T(8,128)(2,1)S(1)}, u32[]{:S(2)}, u32[]{:S(2)}) collective-permute-start(bf16[3,256,256]{2,1,0:T(8,128)(2,1)S(1)} %collective-permute-done.18.a2), channel_id=1, source_target_pairs={{0,2},{1,3},{2,0},{3,1},{4,6},{5,7},{6,4},{7,5},{8,10},{9,11},{10,... | collective-permute-start | bytes 1179656 | tf_op jit(solution)/shard_map/ppermute | solution.py:259
  124.9 13.5 %collective-permute-start.25 = (bf16[3,64,512]{2,1,0:T(8,128)(2,1)S(1)}, bf16[3,64,512]{2,1,0:T(8,128)(2,1)S(1)}, u32[]{:S(2)}, u32[]{:S(2)}) collective-permute-start(bf16[3,64,512]{2,1,0:T(8,128)(2,1)S(1)} %get-tuple-element.53), channel_id=1, source_target_pairs={{0,8},{4,12},{8,0},{12,4},{16,24},{20,28},{24,16},{28,20},{1,9},{5... | collective-permute-start | bytes 589832 | tf_op jit(solution)/shard_map/ppermute | solution.py:265
  128.8 17.1 %collective-permute-start.26 = (bf16[3,64,512]{2,1,0:T(8,128)(2,1)S(1)}, bf16[3,64,512]{2,1,0:T(8,128)(2,1)S(1)}, u32[]{:S(2)}, u32[]{:S(2)}) collective-permute-start(bf16[3,64,512]{2,1,0:T(8,128)(2,1)S(1)} %get-tuple-element.54), channel_id=1, source_target_pairs={{0,16},{4,20},{8,24},{12,28},{16,0},{20,4},{24,8},{28,12},{1,17},{... | collective-permute-start | bytes 589832 | tf_op jit(solution)/shard_map/ppermute | solution.py:265
  130.8 15.1 %collective-permute-start.27 = (bf16[3,64,512]{2,1,0:T(8,128)(2,1)S(1)}, bf16[3,64,512]{2,1,0:T(8,128)(2,1)S(1)}, u32[]{:S(2)}, u32[]{:S(2)}) collective-permute-start(bf16[3,64,512]{2,1,0:T(8,128)(2,1)S(1)} %get-tuple-element.55), channel_id=1, source_target_pairs={{0,24},{4,28},{8,16},{12,20},{16,8},{20,12},{24,0},{28,4},{1,25},{... | collective-permute-start | bytes 589832 | tf_op jit(solution)/shard_map/ppermute | solution.py:265
  132.2 21.4 %collective-permute-start.32 = (bf16[3,256,256]{2,1,0:T(8,128)(2,1)S(1)}, bf16[3,256,256]{2,1,0:T(8,128)(2,1)S(1)}, u32[]{:S(2)}, u32[]{:S(2)}) collective-permute-start(bf16[3,256,256]{2,1,0:T(8,128)(2,1)S(1)} %get-tuple-element.57.refs_5_), channel_id=1, source_target_pairs={{0,1},{1,0},{2,3},{3,2},{4,5},{5,4},{6,7},{7,6},{8,9},{9,8},{10,11... | collective-permute-start | bytes 1179656 | tf_op jit(solution)/shard_map/ppermute | solution.py:256
  132.2 21.4 %collective-permute-start.31 = (bf16[3,256,256]{2,1,0:T(8,128)(2,1)S(1)}, bf16[3,256,256]{2,1,0:T(8,128)(2,1)S(1)}, u32[]{:S(2)}, u32[]{:S(2)}) collective-permute-start(bf16[3,256,256]{2,1,0:T(8,128)(2,1)S(1)} %get-tuple-element.56.refs_4_), channel_id=1, source_target_pairs={{0,1},{1,0},{2,3},{3,2},{4,5},{5,4},{6,7},{7,6},{8,9},{9,8},{10,11... | collective-permute-start | bytes 1179656 | tf_op jit(solution)/shard_map/ppermute | solution.py:256
  146.3 11.4 %collective-permute-start.28 = (bf16[3,64,512]{2,1,0:T(8,128)(2,1)S(1)}, bf16[3,64,512]{2,1,0:T(8,128)(2,1)S(1)}, u32[]{:S(2)}, u32[]{:S(2)}) collective-permute-start(bf16[3,64,512]{2,1,0:T(8,128)(2,1)S(1)} %shard_map.54.refs_0_), channel_id=1, source_target_pairs={{0,8},{4,12},{8,0},{12,4},{16,24},{20,28},{24,16},{28,20},{1,9},{5... | collective-permute-start | bytes 589832 | tf_op jit(solution)/shard_map/ppermute | solution.py:265
  150.2 17.2 %collective-permute-start.29 = (bf16[3,64,512]{2,1,0:T(8,128)(2,1)S(1)}, bf16[3,64,512]{2,1,0:T(8,128)(2,1)S(1)}, u32[]{:S(2)}, u32[]{:S(2)}) collective-permute-start(bf16[3,64,512]{2,1,0:T(8,128)(2,1)S(1)} %shard_map.54.refs_0_), channel_id=1, source_target_pairs={{0,16},{4,20},{8,24},{12,28},{16,0},{20,4},{24,8},{28,12},{1,17},{... | collective-permute-start | bytes 589832 | tf_op jit(solution)/shard_map/ppermute | solution.py:265
  152.2 15.2 %collective-permute-start.30 = (bf16[3,64,512]{2,1,0:T(8,128)(2,1)S(1)}, bf16[3,64,512]{2,1,0:T(8,128)(2,1)S(1)}, u32[]{:S(2)}, u32[]{:S(2)}) collective-permute-start(bf16[3,64,512]{2,1,0:T(8,128)(2,1)S(1)} %shard_map.54.refs_0_), channel_id=1, source_target_pairs={{0,24},{4,28},{8,16},{12,20},{16,8},{20,12},{24,0},{28,4},{1,25},{... | collective-permute-start | bytes 589832 | tf_op jit(solution)/shard_map/ppermute | solution.py:265
  168.0 8.1 %collective-permute-start.34 = (bf16[3,256,256]{2,1,0:T(8,128)(2,1)S(1)}, bf16[3,256,256]{2,1,0:T(8,128)(2,1)S(1)}, u32[]{:S(2)}, u32[]{:S(2)}) collective-permute-start(bf16[3,256,256]{2,1,0:T(8,128)(2,1)S(1)} %get-tuple-element.59), channel_id=1, source_target_pairs={{0,4},{4,0},{8,12},{12,8},{16,20},{20,16},{24,28},{28,24},{1,5},{5... | collective-permute-start | bytes 1179656 | tf_op jit(solution)/shard_map/ppermute | solution.py:262
  168.3 9.1 %collective-permute-start.33 = (bf16[3,256,256]{2,1,0:T(8,128)(2,1)S(1)}, bf16[3,256,256]{2,1,0:T(8,128)(2,1)S(1)}, u32[]{:S(2)}, u32[]{:S(2)}) collective-permute-start(bf16[3,256,256]{2,1,0:T(8,128)(2,1)S(1)} %get-tuple-element.58.a0), channel_id=1, source_target_pairs={{0,2},{1,3},{2,0},{3,1},{4,6},{5,7},{6,4},{7,5},{8,10},{9,11},{10,... | collective-permute-start | bytes 1179656 | tf_op jit(solution)/shard_map/ppermute | solution.py:259
  176.1 8.5 %collective-permute-start.35 = (bf16[3,256,256]{2,1,0:T(8,128)(2,1)S(1)}, bf16[3,256,256]{2,1,0:T(8,128)(2,1)S(1)}, u32[]{:S(2)}, u32[]{:S(2)}) collective-permute-start(bf16[3,256,256]{2,1,0:T(8,128)(2,1)S(1)} %collective-permute-done.34.a2), channel_id=1, source_target_pairs={{0,2},{1,3},{2,0},{3,1},{4,6},{5,7},{6,4},{7,5},{8,10},{9,11},{10,... | collective-permute-start | bytes 1179656 | tf_op jit(solution)/shard_map/ppermute | solution.py:259
  (20 other events, 209.7 us)

commit v2 on v0

v2 whole, which is shorter than its diff:
```python
import functools

import jax
import jax.numpy as jnp
from jax import lax
from jax.experimental import pallas as pl
from jax.experimental.pallas import tpu as pltpu
from jax.sharding import PartitionSpec as P

HEAD_DIM = 64
epsilon = 1e-06
VMEM_LIMIT = 12 * 1024 * 1024
PIECES = 2
F32 = jnp.float32
BF16 = jnp.bfloat16


def dot(a, b):
    return jnp.dot(a, b, preferred_element_type=F32)


def dot_t(a, b):
    return lax.dot_general(a, b, (((1,), (1,)), ((), ())), preferred_element_type=F32)


def params():
    return pltpu.CompilerParams(vmem_limit_bytes=VMEM_LIMIT)


def cost(flops, nbytes, trans=0):
    return pl.CostEstimate(flops=int(flops), bytes_accessed=int(nbytes), transcendentals=int(trans))


def nbytes(*arrays):
    return sum(a.size * a.dtype.itemsize for a in arrays)


def hold_type(rows):
    return BF16 if rows % 16 == 0 else F32


SMEM = pl.BlockSpec(memory_space=pltpu.SMEM)


FULL = pl.BlockSpec(memory_space=pltpu.VMEM)


def store_projections(rows, weights, parts, lane, outs):
    count = rows.shape[0] // parts
    for weight, out in zip(weights, outs):
        projected = dot(rows, weight[...]).astype(BF16)
        for head in range(out.shape[0]):
            at = head * HEAD_DIM
            out[head, :, lane : lane + parts * HEAD_DIM] = jnp.concatenate(
                [projected[n * count : (n + 1) * count, at : at + HEAD_DIM] for n in range(parts)], axis=1
            )


def first_kernel(place, p0, p1, p2, p3, *refs):
    weights, x_out, outs = refs[:3], refs[3], refs[4:]
    x_bit, core = place[0], place[1]
    quarter = p0.shape[2] // 2
    for p in range(p0.shape[0]):
        pair = []
        for s in range(2):
            parts = [ref[p][:, s * quarter : (s + 1) * quarter] for ref in (p0, p1, p2, p3)]
            swapped = [jnp.where(core == 1, parts[t ^ 1], parts[t]) for t in range(4)]
            rows = jnp.concatenate(
                [jnp.where(x_bit == 1, swapped[t ^ 2], swapped[t]) for t in range(4)], axis=1
            )
            x_out[2 * p + s] = rows
            pair.append(rows)
        store_projections(jnp.concatenate(pair, axis=0), weights, 2, 2 * p * HEAD_DIM, outs)


def first(place, pieces, weights, heads):
    pairs, residues, half = pieces[0].shape
    width = 2 * half
    wide = jax.ShapeDtypeStruct((heads, residues, 2 * pairs * HEAD_DIM), BF16)
    flops = 12 * pairs * residues * width * weights[0].shape[1]
    return pl.pallas_call(
        first_kernel,
        in_specs=[SMEM] + [FULL] * 7,
        out_specs=[FULL] * 4,
        out_shape=[jax.ShapeDtypeStruct((2 * pairs, residues, width), BF16)] + [wide] * 3,
        compiler_params=params(),
        cost_estimate=cost(flops, 4 * nbytes(*pieces, *weights)),
    )(place, *pieces, *weights)


def score_kernel(scale, place, *refs):
    queries, keys, others, outs, hold = refs[0:2], refs[2:4], refs[4:6], refs[6:-1], refs[-1]
    z = place[2]
    heads, rows = outs[0].shape[0], outs[0].shape[1]
    residues = queries[0].shape[1]
    for head in range(heads):
        near = dot_t(queries[0][head], keys[0][head]) + dot_t(queries[1][head], keys[1][head])
        hold[:, :residues] = (near * scale).astype(hold.dtype)
        far = dot_t(queries[0][head], others[0][head]) + dot_t(queries[1][head], others[1][head])
        hold[:, residues:] = (far * scale).astype(hold.dtype)
        for d, out in enumerate(outs):
            start = pl.multiple_of(jnp.bitwise_xor(z, d) * rows, rows)
            out[head] = hold[pl.ds(start, rows), :].astype(BF16)


def score_chunks(place, queries, keys, others, scale, chunks):
    heads, residues, depth = queries[0].shape
    rows = residues // chunks
    args = (*queries, *keys, *others)
    return pl.pallas_call(
        functools.partial(score_kernel, scale),
        in_specs=[SMEM] + [FULL] * 6,
        out_specs=[FULL] * chunks,
        out_shape=[jax.ShapeDtypeStruct((heads, rows, 2 * residues), BF16)] * chunks,
        scratch_shapes=[pltpu.VMEM((residues, 2 * residues), hold_type(rows))],
        compiler_params=params(),
        cost_estimate=cost(8 * heads * residues * residues * depth, 2 * nbytes(*args)),
    )(place, *args)


def joined_score_kernel(scale, count, place, *refs):
    queries, keys, others = (refs[i * count : (i + 1) * count] for i in range(3))
    outs, key_hold, hold = refs[3 * count : -2], refs[-2], refs[-1]
    high, low = place[3], place[4]
    heads, rows = outs[0].shape[0], outs[0].shape[1]
    piece_rows = queries[0].shape[1]
    each = piece_rows // rows
    residues = count * piece_rows
    for head in range(heads):
        for side, group in enumerate((keys, others)):
            for g, ref in enumerate(group):
                start = side * residues + jnp.bitwise_xor(high, g) * piece_rows
                key_hold[pl.ds(pl.multiple_of(start, piece_rows), piece_rows), :] = ref[head]
        query = jnp.concatenate([ref[head] for ref in queries], axis=0)
        scores = dot_t(query, key_hold[...]) * scale
        if each == 1:
            for g, out in enumerate(outs):
                out[head] = scores[g * rows : (g + 1) * rows].astype(BF16)
        else:
            hold[...] = scores.astype(hold.dtype)
            for d, out in enumerate(outs):
                start = (d // each) * piece_rows + jnp.bitwise_xor(low, d % each) * rows
                out[head] = hold[pl.ds(pl.multiple_of(start, rows), rows), :].astype(BF16)


def joined_score_chunks(place, queries, keys, others, scale, chunks):
    heads, piece_rows, depth = queries[0].shape
    count = len(queries)
    residues = count * piece_rows
    rows = residues // chunks
    args = (*queries, *keys, *others)
    return pl.pallas_call(
        functools.partial(joined_score_kernel, scale, count),
        in_specs=[SMEM] + [FULL] * len(args),
        out_specs=[FULL] * chunks,
        out_shape=[jax.ShapeDtypeStruct((heads, rows, 2 * residues), BF16)] * chunks,
        scratch_shapes=[
            pltpu.VMEM((2 * residues, depth), BF16),
            pltpu.VMEM((residues, 2 * residues), hold_type(rows)),
        ],
        compiler_params=params(),
        cost_estimate=cost(4 * heads * residues * residues * depth, 2 * nbytes(*args)),
    )(place, *args)


def softmax_kernel(*refs):
    terms, out = refs[:-1], refs[-1]
    total = terms[0][...].astype(F32)
    for term in terms[1:]:
        total = total + term[...].astype(F32)
    top = jnp.max(total, axis=-1, keepdims=True)
    grown = jnp.exp(total - top)
    out[...] = (grown / jnp.sum(grown, axis=-1, keepdims=True)).astype(BF16)


def softmax_sum(terms):
    return pl.pallas_call(
        softmax_kernel,
        out_shape=jax.ShapeDtypeStruct(terms[0].shape, BF16),
        compiler_params=params(),
        cost_estimate=cost(10 * terms[0].size, nbytes(*terms), terms[0].size),
    )(*terms)


def lane_blocks(pairs):
    return [(pair, side) for pair in range(pairs) for side in range(2)]


def gather_first_kernel(near, far, other_near, other_far, out):
    residues = near.shape[1]
    lanes = 2 * HEAD_DIM
    for n, (pair, side) in enumerate(lane_blocks(near.shape[2] // lanes)):
        at = slice(pair * lanes, (pair + 1) * lanes)
        out[:, :residues, n * lanes : (n + 1) * lanes] = (near, far)[side][:, :, at]
        out[:, residues:, n * lanes : (n + 1) * lanes] = (other_near, other_far)[side][:, :, at]


def gather_first(values, others):
    heads, residues, depth = values[0].shape
    return pl.pallas_call(
        gather_first_kernel,
        out_shape=jax.ShapeDtypeStruct((heads, 2 * residues, 2 * depth), BF16),
        compiler_params=params(),
        cost_estimate=cost(0, 4 * nbytes(*values)),
    )(*values, *others)


def gather_kernel(count, place, *refs):
    out = refs[-1]
    rows = refs[0].shape[1]
    for n, ref in enumerate(refs[:-1]):
        start = (n // count) * count * rows + jnp.bitwise_xor(place[3], n % count) * rows
        out[:, pl.ds(pl.multiple_of(start, rows), rows), :] = ref[...]


def gather(place, values, others):
    heads, rows, depth = values[0].shape
    count = len(values)
    return pl.pallas_call(
        functools.partial(gather_kernel, count),
        in_specs=[SMEM] + [FULL] * (2 * count),
        out_specs=FULL,
        out_shape=jax.ShapeDtypeStruct((heads, 2 * count * rows, depth), BF16),
        compiler_params=params(),
        cost_estimate=cost(0, 4 * nbytes(*values)),
    )(place, *values, *others)


def value_kernel(count, place, *refs):
    pieces, values, outs, hold = refs[:count], refs[count], refs[count + 1 : -1], refs[-1]
    heads, rows = pieces[0].shape[0], pieces[0].shape[1]
    lanes = 2 * HEAD_DIM
    for head in range(heads):
        if count == 1:
            weights = pieces[0][head]
        else:
            for e, piece in enumerate(pieces):
                start = pl.multiple_of(jnp.bitwise_xor(place[4], e) * rows, rows)
                hold[pl.ds(start, rows), :] = piece[head].astype(hold.dtype)
            weights = hold[...].astype(BF16)
        made = dot(weights, values[head]).astype(BF16)
        for n, (pair, side) in enumerate(lane_blocks(made.shape[1] // (2 * lanes))):
            outs[side][head, :, pair * lanes : (pair + 1) * lanes] = made[:, n * lanes : (n + 1) * lanes]


def weighted_values(place, pieces, values):
    heads, rows, residues = pieces[0].shape
    depth = values.shape[2]
    rows *= len(pieces)
    return pl.pallas_call(
        functools.partial(value_kernel, len(pieces)),
        in_specs=[SMEM] + [FULL] * (len(pieces) + 1),
        out_specs=[FULL] * 2,
        out_shape=[jax.ShapeDtypeStruct((heads, rows, depth // 2), BF16)] * 2,
        scratch_shapes=[pltpu.VMEM((rows, residues), hold_type(pieces[0].shape[1]))],
        compiler_params=params(),
        cost_estimate=cost(2 * heads * rows * residues * depth, nbytes(*pieces, values)),
    )(place, *pieces, values)


def normalized(rows, x, out_weight, gain):
    summed = x.astype(F32) + dot(rows, out_weight[...])
    mean_sq = jnp.mean(summed * summed, axis=-1, keepdims=True)
    return summed * lax.rsqrt(mean_sq + epsilon) * gain[...].astype(F32)


def head_columns(refs, lane):
    return jnp.concatenate(
        [ref[head][:, lane : lane + HEAD_DIM] for ref in refs for head in range(ref.shape[0])],
        axis=1,
    )


def next_kernel(g, place, *refs):
    attended_refs, (near, far, out_weight, gain), weights, outs = refs[:8], refs[8:12], refs[12:15], refs[15:]
    streams, projections = outs[:-3], outs[-3:]
    rows, depth = attended_refs[0].shape[1:]
    parts = [(side, s) for side in range(2) for s in range(2)]
    start = 0
    if near.shape[1] != rows:
        start = pl.multiple_of(jnp.bitwise_xor(place[3], g) * rows, rows)
    for p in range(depth // (2 * HEAD_DIM)):
        attended = [
            head_columns(attended_refs[4 * side : 4 * side + 4], (2 * p + s) * HEAD_DIM) for side, s in parts
        ]
        x = jnp.concatenate(
            [(near, far)[side][2 * p + s, pl.ds(start, rows), :] for side, s in parts], axis=0
        )
        made = normalized(jnp.concatenate(attended, axis=0), x, out_weight, gain).astype(BF16)
        for n, (side, s) in enumerate(parts):
            if side < len(streams):
                streams[side][2 * p + s] = made[n * rows : (n + 1) * rows]
        store_projections(made, weights, len(parts), p * len(parts) * HEAD_DIM, projections)


def next_layer(place, g, attended, near, far, out_weight, gain, weights, both):
    seqs, _, width = near.shape
    heads, rows, depth = attended[0].shape
    depth *= 2
    streams = 2 if both else 1
    flops = 4 * seqs * rows * width * (3 * weights[0].shape[1] + width)
    return pl.pallas_call(
        functools.partial(next_kernel, g),
        in_specs=[SMEM] + [FULL] * 15,
        out_specs=[FULL] * (streams + 3),
        out_shape=[jax.ShapeDtypeStruct((seqs, rows, width), BF16)] * streams
        + [jax.ShapeDtypeStruct((heads, rows, depth), BF16)] * 3,
        compiler_params=params(),
        cost_estimate=cost(flops, 8 * seqs * rows * width + nbytes(out_weight, *weights)),
    )(place, *attended, near, far, out_weight, gain, *weights)


def last_kernel(place, a0, a1, a2, a3, x, out_weight, gain, keep, send):
    x_bit, core = place[0], place[1]
    seqs, rows, _ = x.shape
    quarter = keep.shape[3]
    columns = [head_columns((a0, a1, a2, a3), s * HEAD_DIM) for s in range(seqs)]
    old = jnp.concatenate([x[s] for s in range(seqs)], axis=0)
    made = normalized(jnp.concatenate(columns, axis=0), old, out_weight, gain)
    half = jnp.where(x_bit == 1, made[:, 2 * quarter :], made[:, : 2 * quarter]).astype(BF16)
    low, high = half[:, :quarter], half[:, quarter:]
    mine, theirs = jnp.where(core == 1, high, low), jnp.where(core == 1, low, high)
    for s in range(seqs):
        keep[s % 2, s // 2] = mine[s * rows : (s + 1) * rows]
        send[s % 2, s // 2] = theirs[s * rows : (s + 1) * rows]


def last_layer(place, attended, x, out_weight, gain):
    seqs, rows, width = x.shape
    made = pl.pallas_call(
        last_kernel,
        in_specs=[SMEM] + [FULL] * 7,
        out_specs=[FULL] * 2,
        out_shape=[jax.ShapeDtypeStruct((2, seqs // 2, rows, width // 4), BF16)] * 2,
        compiler_params=params(),
        cost_estimate=cost(2 * seqs * rows * width * width, 3 * nbytes(x) + nbytes(out_weight)),
    )(place, *attended, x, out_weight, gain)
    return [a.reshape(seqs, rows, width // 4) for a in made]


def placed_kernel(count, place, *refs):
    out = refs[-1]
    rows = refs[0].shape[1]
    for n, ref in enumerate(refs[:-1]):
        core = jnp.bitwise_xor(place[1], n // count)
        start = (core * count + jnp.bitwise_xor(place[3], n % count)) * rows
        out[:, pl.ds(pl.multiple_of(start, rows), rows), :] = ref[...]


def placed(place, kept, other):
    seqs, rows, width = kept[0].shape
    count = len(kept)
    piece = pl.BlockSpec((2, rows, width), lambda s: (s, 0, 0))
    return pl.pallas_call(
        functools.partial(placed_kernel, count),
        grid=(seqs // 2,),
        in_specs=[SMEM] + [piece] * (2 * count),
        out_specs=pl.BlockSpec((2, 2 * count * rows, width), lambda s: (s, 0, 0)),
        out_shape=jax.ShapeDtypeStruct((seqs, 2 * count * rows, width), BF16),
        compiler_params=params(),
        cost_estimate=cost(0, 4 * nbytes(*kept)),
    )(place, *kept, *other)


def on_device(tokens, qkv_weight, out_weight, norm_gain):
    seqs, residues, _ = tokens.shape
    layers, width = norm_gain.shape
    n_rows, n_groups = lax.axis_size("rows"), lax.axis_size("heads")
    all_heads = width // HEAD_DIM
    row, group = lax.axis_index("rows"), lax.axis_index("heads")
    core, x_bit = group % 2, group // 2
    y_bit, z = row % 2, row // 2
    depth = n_rows // 2
    own = x_bit * 2 + y_bit
    heads = all_heads // 4
    own_width = heads * HEAD_DIM
    half = residues // 2
    scale = 1.0 / (HEAD_DIM * seqs * n_rows) ** 0.5
    count = min(depth, PIECES)
    each = depth // count
    place = jnp.stack([x_bit, core, z, z // each, z % each]).astype(jnp.int32)

    def over_core(a):
        return lax.ppermute(a, "heads", [(i, i ^ 1) for i in range(n_groups)])

    def over_x(a):
        return lax.ppermute(a, "heads", [(i, i ^ 2) for i in range(n_groups)])

    def over_y(a):
        return lax.ppermute(a, "rows", [(i, i ^ 1) for i in range(n_rows)])

    def over_z(a, d):
        return lax.ppermute(a, "rows", [(i, i ^ (2 * d)) for i in range(n_rows)])

    def own_columns(layer, at):
        return tuple(
            lax.dynamic_slice(
                qkv_weight, (layer, 0, which, at * own_width), (1, width, 1, own_width)
            ).reshape(width, own_width)
            for which in range(qkv_weight.shape[2])
        )

    def out_rows(layer, at):
        parts = [
            lax.dynamic_slice(out_weight, (layer, (at ^ d) * own_width, 0), (1, own_width, width))[0]
            for d in (0, 2, 1, 3)
        ]
        return jnp.concatenate(parts, axis=0)

    def packed(which):
        part = lax.dynamic_slice_in_dim(tokens, which * half, half, 1)
        return jnp.concatenate([part[: seqs // 2], part[seqs // 2 :]], axis=2)

    mine = packed(core)
    sibling = over_core(packed(1 - core))
    x_mine, y_mine = over_x(mine), over_y(mine)
    x_sibling, y_sibling = over_x(sibling), over_y(sibling)
    d_mine, d_sibling = over_y(x_mine), over_x(y_sibling)
    weight = own_columns(0, own)
    streams, queries, keys, values = [], [], [], []
    for pieces in ((mine, sibling, x_mine, x_sibling), (y_mine, y_sibling, d_mine, d_sibling)):
        made = first(place, pieces, weight, heads)
        for kept, one in zip((streams, queries, keys, values), made):
            kept.append(one)
    near, far = [streams[0]] * count, [streams[1]] * count

    for layer in range(layers):
        more = layer + 1 < layers
        other_keys = [over_core(k) for k in keys]
        other_values = [over_core(v) for v in values]
        if layer == 0:
            chunks = score_chunks(place, queries, keys, other_keys, scale, depth)
        else:
            chunks = joined_score_chunks(place, queries, keys, other_keys, scale, depth)
        terms = [chunks[0]] + [over_z(chunks[d], d) for d in range(1, depth)]
        if layer == 0:
            value = gather_first(values, other_values)
        else:
            value = gather(place, values, other_values)
        own_late, kept = lax.optimization_barrier((own, chunks[0]))
        out_mat = out_rows(layer, own_late)
        weight = own_columns(layer + 1, own_late) if more else ()
        terms[0], out_mat, weight, value = lax.optimization_barrier((kept, out_mat, weight, value))
        weights = softmax_sum(terms)
        gain = norm_gain[layer : layer + 1]
        pieces = [weights] + [over_z(weights, d) for d in range(1, depth)]
        attended = []
        for g in range(count):
            near_part, far_part = weighted_values(place, pieces[g * each : (g + 1) * each], value)
            if g:
                before = attended[-1]
                near_part, far_part, before[1], before[2] = lax.optimization_barrier(
                    (near_part, far_part, before[1], before[2])
                )
            x_near, y_near = over_x(near_part), over_y(far_part)
            parts = [near_part, x_near, y_near, over_x(y_near)]
            if more:
                parts += [far_part, over_x(far_part), over_y(near_part), over_y(x_near)]
            attended.append(parts)
        if more:
            both = layer + 2 < layers
            made = [
                next_layer(place, g, attended[g], near[g], far[g], out_mat, gain, weight, both)
                for g in range(count)
            ]
            near = [m[0] for m in made]
            far = [m[1] for m in made] if both else near
            queries, keys, values = ([m[i] for m in made] for i in (-3, -2, -1))
    kept, other = [], []
    for g in range(count):
        keep, send = last_layer(place, attended[g], near[g], out_mat, gain)
        kept.append(keep)
        other.append(over_core(send))
    return placed(place, kept, other)


def solution(mesh):
    return jax.shard_map(
        on_device,
        mesh=mesh,
        in_specs=(P("rows", None, "heads"), P(), P(), P()),
        out_specs=P("rows", None, "heads"),
        check_vma=False,
    )
```

time: 490 us -> 174 us (0.36)
  waiting for transfers between devices: 380 us -> 82.4 us
  starting transfers between devices: 0.39 us -> 52.4 us
  matrix products: 33.8 us -> 0 us
  Pallas kernels: 0 us -> 26.3 us
  local copies, waits for them, and re-layouts: 37.1 us -> 11.9 us
  between operations: 13.7 us -> 0.44 us
  other arithmetic: 12.5 us -> 0.46 us
  blocking collectives: 11.7 us -> 0 us
    psum x2 -> x0, waiting for transfers between devices: 256 us -> none  [attend(): scores = lax.psum(partial_value, 'rows')]
    ppermute x0 -> x47, waiting for transfers between devices: none -> 82.4 us  [the longest x12 46.1 us: over_z(): return lax.ppermute(a, 'rows', [(i, i ^ 2 * d) for i in range(n_rows)])]
    reduce_scatter x2 -> x0, waiting for transfers between devices: 73.2 us -> none  [on_device(): lax.psum_scatter(update.astype(jnp.bfloat16), 'heads', scatter_dimension=...]
    ppermute x0 -> x47, starting transfers between devices: none -> 52.4 us  [the longest x12 21.7 us: over_z(): return lax.ppermute(a, 'rows', [(i, i ^ 2 * d) for i in range(n_rows)])]
    all_gather x2 -> x0, waiting for transfers between devices: 50.5 us -> none  [on_device(): portion = lax.all_gather(stream, 'heads', axis=2, tiled=True)]
    dot_general x12 -> x0, matrix products: 33.8 us -> none  [the longest x4 11.8 us: attend(): jnp.einsum('hij,sjhc->sihc', weights, values, preferred_element_type=jnp....]
    pallas_call x0 -> x17, Pallas kernels: none -> 26.3 us  [the longest x2 8.37 us: next_layer(): pl.pallas_call(functools.partial(next_kernel, g), in_specs=[SMEM] + [FULL...]
    psum x2 -> x0, blocking collectives: 11.7 us -> none  [on_device(): lax.psum(jnp.sum(summed * summed, axis=-1, keepdims=True), 'heads')]
  transfers between devices with their start and end apart: 6 -> 47, of which waited for: 6 -> 22; matrix products, arithmetic and copies ran while one was open for 2% -> 4% of each run, Pallas kernels for 0% -> 14%
where the time goes in v2:
time: 174 us
  waiting for transfers between devices  82.4 us (47%)
  starting transfers between devices  52.4 us (30%)
  Pallas kernels  26.3 us (15%)
  local copies, waits for them, and re-layouts  11.9 us (7%)
    ppermute x12, waiting for transfers between devices, over_z(): return lax.ppermute(a, 'rows', [(i, i ^ 2 * d) for i in range(n_rows)])  46.1 us
    ppermute x12, starting transfers between devices, over_z(): return lax.ppermute(a, 'rows', [(i, i ^ 2 * d) for i in range(n_rows)])  21.7 us
    ppermute x11, waiting for transfers between devices, over_y(): return lax.ppermute(a, 'rows', [(i, i ^ 1) for i in range(n_rows)])  16.8 us
    ppermute x13, waiting for transfers between devices, over_x(): return lax.ppermute(a, 'heads', [(i, i ^ 2) for i in range(n_groups)])  15.9 us
    ppermute x13, starting transfers between devices, over_x(): return lax.ppermute(a, 'heads', [(i, i ^ 2) for i in range(n_groups)])  15.4 us
    ppermute x11, starting transfers between devices, over_y(): return lax.ppermute(a, 'rows', [(i, i ^ 1) for i in range(n_rows)])  13 us
    pallas_call x2, Pallas kernels, next_layer(): pl.pallas_call(functools.partial(next_kernel, g), in_specs=[SMEM] + [FULL...  8.37 us
    pallas_call x2, Pallas kernels, first(): pl.pallas_call(first_kernel, in_specs=[SMEM] + [FULL] * 7, out_specs=[FUL...  4.92 us
  transfers between devices with their start and end apart: 47, of which 22 were waited for; matrix products, arithmetic and copies ran while one was open for 4% of the time, Pallas kernels for 14%

profile of v2, /device:TPU:0, one launch (start us, length us, event | category | flops | bytes accessed | tf_op | source)
XLA Modules:
  0.0 173.9 jit_solution(1007441329713674976)
XLA Ops:
  2.7 2.6 %collective-permute-start.1 = (bf16[2,256,384]{2,1,0:T(8,128)(2,1)S(1)}, bf16[2,256,384]{2,1,0:T(8,128)(2,1)S(1)}, u32[]{:S(2)}, u32[]{:S(2)}) collective-permute-start(bf16[2,256,384]{2,1,0:T(8,128)(2,1)S(1)} %pad_maximum_fusion.2.p0), channel_id=1, source_target_pairs={{0,2},{1,3},{2,0},{3,1},{4,6},{5,7},{6,4},{7,5},{8,10},{9,11},{10,... | collective-permute-start | bytes 1179656 | tf_op jit(solution)/shard_map/ppermute | solution.py:387
  8.5 6.7 %collective-permute-done.1.p2 = bf16[2,256,384]{2,1,0:T(8,128)(2,1)S(1)} collective-permute-done((bf16[2,256,384]{2,1,0:T(8,128)(2,1)S(1)}, bf16[2,256,384]{2,1,0:T(8,128)(2,1)S(1)}, u32[]{:S(2)}, u32[]{:S(2)}) %collective-permute-start.1) | collective-permute-done | bytes 393248 | tf_op jit(solution)/shard_map/ppermute | solution.py:387
  15.2 2.0 %collective-permute-start.5 = (bf16[2,256,384]{2,1,0:T(8,128)(2,1)S(1)}, bf16[2,256,384]{2,1,0:T(8,128)(2,1)S(1)}, u32[]{:S(2)}, u32[]{:S(2)}) collective-permute-start(bf16[2,256,384]{2,1,0:T(8,128)(2,1)S(1)} %collective-permute-done.1.p2), channel_id=1, source_target_pairs={{0,4},{4,0},{8,12},{12,8},{16,20},{20,16},{24,28},{28,24},{1,5},{5... | collective-permute-start | bytes 1179656 | tf_op jit(solution)/shard_map/ppermute | solution.py:390
  18.7 2.0 %dynamic-slice_bitcast_fusion.3 = (bf16[768,192]{1,0:T(8,128)(2,1)S(1)}, bf16[768,192]{1,0:T(8,128)(2,1)S(1)}, bf16[768,192]{1,0:T(8,128)(2,1)S(1)}) fusion(bf16[2,768,3,768]{3,1,2,0:T(8,128)(2,1)} %param.5, s32[]{:T(128)S(6)} %select_n.71), kind=kLoop, calls=%fused_computation.7 | loop fusion | bytes 1769476 | tf_op jit(solution)/shard_map/reshape | solution.py:399
  20.7 2.9 %collective-permute-done.2.p3 = bf16[2,256,384]{2,1,0:T(8,128)(2,1)S(1)} collective-permute-done((bf16[2,256,384]{2,1,0:T(8,128)(2,1)S(1)}, bf16[2,256,384]{2,1,0:T(8,128)(2,1)S(1)}, u32[]{:S(2)}, u32[]{:S(2)}) %collective-permute-start.2) | collective-permute-done | bytes 393248 | tf_op jit(solution)/shard_map/ppermute | solution.py:387
  23.6 2.5 %shard_map.46 = (bf16[4,256,768]{2,1,0:T(8,128)(2,1)S(1)}, bf16[3,256,256]{2,1,0:T(8,128)(2,1)S(1)}, bf16[3,256,256]{2,1,0:T(8,128)(2,1)S(1)}, bf16[3,256,256]{2,1,0:T(8,128)(2,1)S(1)}) custom-call(s32[5]{0:T(128)S(1)} %stack.23.place, bf16[2,256,384]{2,1,0:T(8,128)(2,1)S(1)} %pad_maximum_fusion.2.p0, bf16[2,256,384]{2,1,0:T(8,128)(2,1)S(1)} %collective-permute-done.p1, ...), custom_call_target="tpu_custom_call" | custom-call | flops 905969664 | bytes 9830400 | tf_op jit(solution)/shard_map/pallas_call | solution.py:81
  27.3 6.0 %collective-permute-done.5.p2 = bf16[2,256,384]{2,1,0:T(8,128)(2,1)S(1)} collective-permute-done((bf16[2,256,384]{2,1,0:T(8,128)(2,1)S(1)}, bf16[2,256,384]{2,1,0:T(8,128)(2,1)S(1)}, u32[]{:S(2)}, u32[]{:S(2)}) %collective-permute-start.5) | collective-permute-done | bytes 393248 | tf_op jit(solution)/shard_map/ppermute | solution.py:390
  33.3 2.5 %shard_map.47 = (bf16[4,256,768]{2,1,0:T(8,128)(2,1)S(1)}, bf16[3,256,256]{2,1,0:T(8,128)(2,1)S(1)}, bf16[3,256,256]{2,1,0:T(8,128)(2,1)S(1)}, bf16[3,256,256]{2,1,0:T(8,128)(2,1)S(1)}) custom-call(s32[5]{0:T(128)S(1)} %stack.23.place, bf16[2,256,384]{2,1,0:T(8,128)(2,1)S(1)} %collective-permute-done.3.p0, ...), custom_call_target="tpu_custom_call" | custom-call | flops 905969664 | bytes 9830400 | tf_op jit(solution)/shard_map/pallas_call | solution.py:81
  40.4 2.6 %collective-permute-start.12 = (bf16[3,64,512]{2,1,0:T(8,128)(2,1)S(1)}, bf16[3,64,512]{2,1,0:T(8,128)(2,1)S(1)}, u32[]{:S(2)}, u32[]{:S(2)}) collective-permute-start(bf16[3,64,512]{2,1,0:T(8,128)(2,1)S(1)} %get-tuple-element.73), channel_id=1, source_target_pairs={{0,16},{4,20},{8,24},{12,28},{16,0},{20,4},{24,8},{28,12},{1,17},{... | collective-permute-start | bytes 589832 | tf_op jit(solution)/shard_map/ppermute | solution.py:393
  43.2 2.1 %dynamic-slice_bitcast_fusion = (bf16[768,192]{1,0:T(8,128)(2,1)S(1)}, bf16[768,192]{1,0:T(8,128)(2,1)S(1)}, bf16[768,192]{1,0:T(8,128)(2,1)S(1)}) fusion(bf16[2,768,3,768]{3,1,2,0:T(8,128)(2,1)} %param.5, s32[]{:T(128)S(6)} %select_n.72), kind=kLoop, calls=%fused_computation.4 | loop fusion | bytes 1769476 | tf_op jit(solution)/shard_map/reshape | solution.py:399
  45.9 3.5 %collective-permute-done.11.refs_1_ = bf16[3,64,512]{2,1,0:T(8,128)(2,1)S(1)} collective-permute-done((bf16[3,64,512]{2,1,0:T(8,128)(2,1)S(1)}, bf16[3,64,512]{2,1,0:T(8,128)(2,1)S(1)}, u32[]{:S(2)}, u32[]{:S(2)}) %collective-permute-start.11) | collective-permute-done | bytes 196640 | tf_op jit(solution)/shard_map/ppermute | solution.py:393
  49.4 8.1 %collective-permute-done.12.refs_2_ = bf16[3,64,512]{2,1,0:T(8,128)(2,1)S(1)} collective-permute-done((bf16[3,64,512]{2,1,0:T(8,128)(2,1)S(1)}, bf16[3,64,512]{2,1,0:T(8,128)(2,1)S(1)}, u32[]{:S(2)}, u32[]{:S(2)}) %collective-permute-start.12) | collective-permute-done | bytes 196640 | tf_op jit(solution)/shard_map/ppermute | solution.py:393
  57.8 3.8 %collective-permute-start.14 = (bf16[3,64,512]{2,1,0:T(8,128)(2,1)S(1)}, bf16[3,64,512]{2,1,0:T(8,128)(2,1)S(1)}, u32[]{:S(2)}, u32[]{:S(2)}) collective-permute-start(bf16[3,64,512]{2,1,0:T(8,128)(2,1)S(1)} %shard_map.50.refs_0_), channel_id=1, source_target_pairs={{0,8},{4,12},{8,0},{12,4},{16,24},{20,28},{24,16},{28,20},{1,9},{5... | collective-permute-start | bytes 589832 | tf_op jit(solution)/shard_map/ppermute | solution.py:393
  61.6 2.5 %collective-permute-start.16 = (bf16[3,64,512]{2,1,0:T(8,128)(2,1)S(1)}, bf16[3,64,512]{2,1,0:T(8,128)(2,1)S(1)}, u32[]{:S(2)}, u32[]{:S(2)}) collective-permute-start(bf16[3,64,512]{2,1,0:T(8,128)(2,1)S(1)} %shard_map.50.refs_0_), channel_id=1, source_target_pairs={{0,24},{4,28},{8,16},{12,20},{16,8},{20,12},{24,0},{28,4},{1,25},{... | collective-permute-start | bytes 589832 | tf_op jit(solution)/shard_map/ppermute | solution.py:393
  64.1 2.9 %collective-permute-done.14.refs_1_ = bf16[3,64,512]{2,1,0:T(8,128)(2,1)S(1)} collective-permute-done((bf16[3,64,512]{2,1,0:T(8,128)(2,1)S(1)}, bf16[3,64,512]{2,1,0:T(8,128)(2,1)S(1)}, u32[]{:S(2)}, u32[]{:S(2)}) %collective-permute-start.14) | collective-permute-done | bytes 196640 | tf_op jit(solution)/shard_map/ppermute | solution.py:393
  71.1 3.1 %collective-permute-done.16.refs_1_ = bf16[3,64,512]{2,1,0:T(8,128)(2,1)S(1)} collective-permute-done((bf16[3,64,512]{2,1,0:T(8,128)(2,1)S(1)}, bf16[3,64,512]{2,1,0:T(8,128)(2,1)S(1)}, u32[]{:S(2)}, u32[]{:S(2)}) %collective-permute-start.16) | collective-permute-done | bytes 196640 | tf_op jit(solution)/shard_map/ppermute | solution.py:393
  75.3 4.3 %collective-permute-done.15.refs_0_ = bf16[3,64,512]{2,1,0:T(8,128)(2,1)S(1)} collective-permute-done((bf16[3,64,512]{2,1,0:T(8,128)(2,1)S(1)}, bf16[3,64,512]{2,1,0:T(8,128)(2,1)S(1)}, u32[]{:S(2)}, u32[]{:S(2)}) %collective-permute-start.15) | collective-permute-done | bytes 196640 | tf_op jit(solution)/shard_map/ppermute | solution.py:393
  86.3 7.5 %collective-permute-done.22.refs_7_ = bf16[3,128,256]{2,1,0:T(8,128)(2,1)S(1)} collective-permute-done((bf16[3,128,256]{2,1,0:T(8,128)(2,1)S(1)}, bf16[3,128,256]{2,1,0:T(8,128)(2,1)S(1)}, u32[]{:S(2)}, u32[]{:S(2)}) %collective-permute-start.22) | collective-permute-done | bytes 196640 | tf_op jit(solution)/shard_map/ppermute | solution.py:390
  97.3 4.3 %shard_map.53 = (bf16[4,128,768]{2,1,0:T(8,128)(2,1)S(1)}, bf16[3,128,512]{2,1,0:T(8,128)(2,1)S(1)}, bf16[3,128,512]{2,1,0:T(8,128)(2,1)S(1)}, bf16[3,128,512]{2,1,0:T(8,128)(2,1)S(1)}) custom-call(s32[5]{0:T(128)S(1)} %stack.23.place, bf16[3,128,256]{2,1,0:T(8,128)(2,1)S(1)} %get-tuple-element.76.refs_0_, ...), custom_call_target="tpu_custom_call" | custom-call | flops 2113929216 | bytes 5210112 | tf_op jit(solution)/shard_map/pallas_call | solution.py:302
  101.9 4.1 %shard_map.54 = (bf16[4,128,768]{2,1,0:T(8,128)(2,1)S(1)}, bf16[3,128,512]{2,1,0:T(8,128)(2,1)S(1)}, bf16[3,128,512]{2,1,0:T(8,128)(2,1)S(1)}, bf16[3,128,512]{2,1,0:T(8,128)(2,1)S(1)}) custom-call(s32[5]{0:T(128)S(1)} %stack.23.place, bf16[3,128,256]{2,1,0:T(8,128)(2,1)S(1)} %get-tuple-element.89.refs_0_, ...), custom_call_target="tpu_custom_call" | custom-call | flops 2113929216 | bytes 5210112 | tf_op jit(solution)/shard_map/pallas_call | solution.py:302
  111.0 3.0 %collective-permute-start.34 = (bf16[3,64,512]{2,1,0:T(8,128)(2,1)}, bf16[3,64,512]{2,1,0:T(8,128)(2,1)}, u32[]{:S(2)}, u32[]{:S(2)}) collective-permute-start(bf16[3,64,512]{2,1,0:T(8,128)(2,1)} %copy-done.1), channel_id=1, source_target_pairs={{0,16},{4,20},{8,24},{12,28},{16,0},{20,4},{24,8},{28,12},{1,17},{... | collective-permute-start | bytes 589832 | tf_op jit(solution)/shard_map/ppermute | solution.py:393
  117.5 4.7 %collective-permute-done.33.refs_1_ = bf16[3,64,512]{2,1,0:T(8,128)(2,1)S(1)} collective-permute-done((bf16[3,64,512]{2,1,0:T(8,128)(2,1)}, bf16[3,64,512]{2,1,0:T(8,128)(2,1)S(1)}, u32[]{:S(2)}, u32[]{:S(2)}) %collective-permute-start.33) | collective-permute-done | bytes 196640 | tf_op jit(solution)/shard_map/ppermute | solution.py:393
  122.2 6.3 %collective-permute-done.34.refs_2_ = bf16[3,64,512]{2,1,0:T(8,128)(2,1)} collective-permute-done((bf16[3,64,512]{2,1,0:T(8,128)(2,1)}, bf16[3,64,512]{2,1,0:T(8,128)(2,1)}, u32[]{:S(2)}, u32[]{:S(2)}) %collective-permute-start.34) | collective-permute-done | bytes 196640 | tf_op jit(solution)/shard_map/ppermute | solution.py:393
  129.8 4.3 %collective-permute-start.36 = (bf16[3,64,512]{2,1,0:T(8,128)(2,1)S(1)}, bf16[3,64,512]{2,1,0:T(8,128)(2,1)S(1)}, u32[]{:S(2)}, u32[]{:S(2)}) collective-permute-start(bf16[3,64,512]{2,1,0:T(8,128)(2,1)S(1)} %shard_map.57.refs_0_), channel_id=1, source_target_pairs={{0,8},{4,12},{8,0},{12,4},{16,24},{20,28},{24,16},{28,20},{1,9},{5... | collective-permute-start | bytes 589832 | tf_op jit(solution)/shard_map/ppermute | solution.py:393
  134.1 2.4 %collective-permute-start.38 = (bf16[3,64,512]{2,1,0:T(8,128)(2,1)S(1)}, bf16[3,64,512]{2,1,0:T(8,128)(2,1)S(1)}, u32[]{:S(2)}, u32[]{:S(2)}) collective-permute-start(bf16[3,64,512]{2,1,0:T(8,128)(2,1)S(1)} %shard_map.57.refs_0_), channel_id=1, source_target_pairs={{0,24},{4,28},{8,16},{12,20},{16,8},{20,12},{24,0},{28,4},{1,25},{... | collective-permute-start | bytes 589832 | tf_op jit(solution)/shard_map/ppermute | solution.py:393
  136.5 3.0 %collective-permute-done.36.refs_1_ = bf16[3,64,512]{2,1,0:T(8,128)(2,1)S(1)} collective-permute-done((bf16[3,64,512]{2,1,0:T(8,128)(2,1)S(1)}, bf16[3,64,512]{2,1,0:T(8,128)(2,1)S(1)}, u32[]{:S(2)}, u32[]{:S(2)}) %collective-permute-start.36) | collective-permute-done | bytes 196640 | tf_op jit(solution)/shard_map/ppermute | solution.py:393
  142.4 4.2 %collective-permute-done.38.refs_1_ = bf16[3,64,512]{2,1,0:T(8,128)(2,1)S(1)} collective-permute-done((bf16[3,64,512]{2,1,0:T(8,128)(2,1)S(1)}, bf16[3,64,512]{2,1,0:T(8,128)(2,1)S(1)}, u32[]{:S(2)}, u32[]{:S(2)}) %collective-permute-start.38) | collective-permute-done | bytes 196640 | tf_op jit(solution)/shard_map/ppermute | solution.py:393
  146.6 6.0 %collective-permute-done.37.refs_0_ = bf16[3,64,512]{2,1,0:T(8,128)(2,1)S(1)} collective-permute-done((bf16[3,64,512]{2,1,0:T(8,128)(2,1)S(1)}, bf16[3,64,512]{2,1,0:T(8,128)(2,1)S(1)}, u32[]{:S(2)}, u32[]{:S(2)}) %collective-permute-start.37) | collective-permute-done | bytes 196640 | tf_op jit(solution)/shard_map/ppermute | solution.py:393
  156.4 3.2 %collective-permute-done.43.a2 = bf16[3,128,256]{2,1,0:T(8,128)(2,1)S(1)} collective-permute-done((bf16[3,128,256]{2,1,0:T(8,128)(2,1)S(1)}, bf16[3,128,256]{2,1,0:T(8,128)(2,1)S(1)}, u32[]{:S(2)}, u32[]{:S(2)}) %collective-permute-start.43) | collective-permute-done | bytes 196640 | tf_op jit(solution)/shard_map/ppermute | solution.py:390
  164.2 2.2 %collective-permute-done.42.a1 = bf16[3,128,256]{2,1,0:T(8,128)(2,1)S(1)} collective-permute-done((bf16[3,128,256]{2,1,0:T(8,128)(2,1)S(1)}, bf16[3,128,256]{2,1,0:T(8,128)(2,1)S(1)}, u32[]{:S(2)}, u32[]{:S(2)}) %collective-permute-start.42) | collective-permute-done | bytes 196640 | tf_op jit(solution)/shard_map/ppermute | solution.py:387
  166.4 2.1 %collective-permute-done.44.a3 = bf16[3,128,256]{2,1,0:T(8,128)(2,1)S(1)} collective-permute-done((bf16[3,128,256]{2,1,0:T(8,128)(2,1)S(1)}, bf16[3,128,256]{2,1,0:T(8,128)(2,1)S(1)}, u32[]{:S(2)}, u32[]{:S(2)}) %collective-permute-start.44) | collective-permute-done | bytes 196640 | tf_op jit(solution)/shard_map/ppermute | solution.py:387
  168.5 1.9 %shard_map.61 = (bf16[2,2,128,192]{3,2,1,0:T(8,128)(2,1)S(1)}, bf16[2,2,128,192]{3,2,1,0:T(8,128)(2,1)S(1)}) custom-call(s32[5]{0:T(128)S(1)} %stack.23.place, bf16[3,128,256]{2,1,0:T(8,128)(2,1)S(1)} %get-tuple-element.113.a0, bf16[3,128,256]{2,1,0:T(8,128)(2,1)S(1)} %collective-permute-done.42.a1, bf16[3,128,256]{2,1,0:T(8,128)(2,1)S(1)} %collective-permute-done.43.a2, ...), custom_call_target="tpu_custom_call" | custom-call | flops 603979776 | bytes 3538944 | tf_op jit(solution)/shard_map/pallas_call | solution.py:330
  (113 shorter events, 54.3 us)
Async XLA Ops:
  2.7 12.5 %collective-permute-start.1 = (bf16[2,256,384]{2,1,0:T(8,128)(2,1)S(1)}, bf16[2,256,384]{2,1,0:T(8,128)(2,1)S(1)}, u32[]{:S(2)}, u32[]{:S(2)}) collective-permute-start(bf16[2,256,384]{2,1,0:T(8,128)(2,1)S(1)} %pad_maximum_fusion.2.p0), channel_id=1, source_target_pairs={{0,2},{1,3},{2,0},{3,1},{4,6},{5,7},{6,4},{7,5},{8,10},{9,11},{10,... | collective-permute-start | bytes 1179656 | tf_op jit(solution)/shard_map/ppermute | solution.py:387
  5.2 11.9 %collective-permute-start.4 = (bf16[2,256,384]{2,1,0:T(8,128)(2,1)S(1)}, bf16[2,256,384]{2,1,0:T(8,128)(2,1)S(1)}, u32[]{:S(2)}, u32[]{:S(2)}) collective-permute-start(bf16[2,256,384]{2,1,0:T(8,128)(2,1)S(1)} %collective-permute-done.p1), channel_id=1, source_target_pairs={{0,4},{4,0},{8,12},{12,8},{16,20},{20,16},{24,28},{28,24},{1,5},{5... | collective-permute-start | bytes 1179656 | tf_op jit(solution)/shard_map/ppermute | solution.py:390
  6.8 16.9 %collective-permute-start.2 = (bf16[2,256,384]{2,1,0:T(8,128)(2,1)S(1)}, bf16[2,256,384]{2,1,0:T(8,128)(2,1)S(1)}, u32[]{:S(2)}, u32[]{:S(2)}) collective-permute-start(bf16[2,256,384]{2,1,0:T(8,128)(2,1)S(1)} %collective-permute-done.p1), channel_id=1, source_target_pairs={{0,2},{1,3},{2,0},{3,1},{4,6},{5,7},{6,4},{7,5},{8,10},{9,11},{10,... | collective-permute-start | bytes 1179656 | tf_op jit(solution)/shard_map/ppermute | solution.py:387
  8.0 19.3 %collective-permute-start.3 = (bf16[2,256,384]{2,1,0:T(8,128)(2,1)S(1)}, bf16[2,256,384]{2,1,0:T(8,128)(2,1)S(1)}, u32[]{:S(2)}, u32[]{:S(2)}) collective-permute-start(bf16[2,256,384]{2,1,0:T(8,128)(2,1)S(1)} %pad_maximum_fusion.2.p0), channel_id=1, source_target_pairs={{0,4},{4,0},{8,12},{12,8},{16,20},{20,16},{24,28},{28,24},{1,5},{5... | collective-permute-start | bytes 1179656 | tf_op jit(solution)/shard_map/ppermute | solution.py:390
  15.2 18.1 %collective-permute-start.5 = (bf16[2,256,384]{2,1,0:T(8,128)(2,1)S(1)}, bf16[2,256,384]{2,1,0:T(8,128)(2,1)S(1)}, u32[]{:S(2)}, u32[]{:S(2)}) collective-permute-start(bf16[2,256,384]{2,1,0:T(8,128)(2,1)S(1)} %collective-permute-done.1.p2), channel_id=1, source_target_pairs={{0,4},{4,0},{8,12},{12,8},{16,20},{20,16},{24,28},{28,24},{1,5},{5... | collective-permute-start | bytes 1179656 | tf_op jit(solution)/shard_map/ppermute | solution.py:390
  17.2 16.1 %collective-permute-start.6 = (bf16[2,256,384]{2,1,0:T(8,128)(2,1)S(1)}, bf16[2,256,384]{2,1,0:T(8,128)(2,1)S(1)}, u32[]{:S(2)}, u32[]{:S(2)}) collective-permute-start(bf16[2,256,384]{2,1,0:T(8,128)(2,1)S(1)} %collective-permute-done.4.p1), channel_id=1, source_target_pairs={{0,2},{1,3},{2,0},{3,1},{4,6},{5,7},{6,4},{7,5},{8,10},{9,11},{10,... | collective-permute-start | bytes 1179656 | tf_op jit(solution)/shard_map/ppermute | solution.py:387
  35.9 9.6 %collective-permute-start.9 = (bf16[3,256,256]{2,1,0:T(8,128)(2,1)S(1)}, bf16[3,256,256]{2,1,0:T(8,128)(2,1)S(1)}, u32[]{:S(2)}, u32[]{:S(2)}) collective-permute-start(bf16[3,256,256]{2,1,0:T(8,128)(2,1)S(1)} %get-tuple-element.69.near), channel_id=1, source_target_pairs={{0,1},{1,0},{2,3},{3,2},{4,5},{5,4},{6,7},{7,6},{8,9},{9,8},{10,11... | collective-permute-start | bytes 1179656 | tf_op jit(solution)/shard_map/ppermute | solution.py:384
  38.8 10.6 %collective-permute-start.11 = (bf16[3,64,512]{2,1,0:T(8,128)(2,1)S(1)}, bf16[3,64,512]{2,1,0:T(8,128)(2,1)S(1)}, u32[]{:S(2)}, u32[]{:S(2)}) collective-permute-start(bf16[3,64,512]{2,1,0:T(8,128)(2,1)S(1)} %get-tuple-element.72), channel_id=1, source_target_pairs={{0,8},{4,12},{8,0},{12,4},{16,24},{20,28},{24,16},{28,20},{1,9},{5... | collective-permute-start | bytes 589832 | tf_op jit(solution)/shard_map/ppermute | solution.py:393
  40.4 17.1 %collective-permute-start.12 = (bf16[3,64,512]{2,1,0:T(8,128)(2,1)S(1)}, bf16[3,64,512]{2,1,0:T(8,128)(2,1)S(1)}, u32[]{:S(2)}, u32[]{:S(2)}) collective-permute-start(bf16[3,64,512]{2,1,0:T(8,128)(2,1)S(1)} %get-tuple-element.73), channel_id=1, source_target_pairs={{0,16},{4,20},{8,24},{12,28},{16,0},{20,4},{24,8},{28,12},{1,17},{... | collective-permute-start | bytes 589832 | tf_op jit(solution)/shard_map/ppermute | solution.py:393
  43.0 14.5 %collective-permute-start.13 = (bf16[3,64,512]{2,1,0:T(8,128)(2,1)S(1)}, bf16[3,64,512]{2,1,0:T(8,128)(2,1)S(1)}, u32[]{:S(2)}, u32[]{:S(2)}) collective-permute-start(bf16[3,64,512]{2,1,0:T(8,128)(2,1)S(1)} %get-tuple-element.74), channel_id=1, source_target_pairs={{0,24},{4,28},{8,16},{12,20},{16,8},{20,12},{24,0},{28,4},{1,25},{... | collective-permute-start | bytes 589832 | tf_op jit(solution)/shard_map/ppermute | solution.py:393
  61.6 12.6 %collective-permute-start.16 = (bf16[3,64,512]{2,1,0:T(8,128)(2,1)S(1)}, bf16[3,64,512]{2,1,0:T(8,128)(2,1)S(1)}, u32[]{:S(2)}, u32[]{:S(2)}) collective-permute-start(bf16[3,64,512]{2,1,0:T(8,128)(2,1)S(1)} %shard_map.50.refs_0_), channel_id=1, source_target_pairs={{0,24},{4,28},{8,16},{12,20},{16,8},{20,12},{24,0},{28,4},{1,25},{... | collective-permute-start | bytes 589832 | tf_op jit(solution)/shard_map/ppermute | solution.py:393
  64.1 15.5 %collective-permute-start.15 = (bf16[3,64,512]{2,1,0:T(8,128)(2,1)S(1)}, bf16[3,64,512]{2,1,0:T(8,128)(2,1)S(1)}, u32[]{:S(2)}, u32[]{:S(2)}) collective-permute-start(bf16[3,64,512]{2,1,0:T(8,128)(2,1)S(1)} %shard_map.50.refs_0_), channel_id=1, source_target_pairs={{0,16},{4,20},{8,24},{12,28},{16,0},{20,4},{24,8},{28,12},{1,17},{... | collective-permute-start | bytes 589832 | tf_op jit(solution)/shard_map/ppermute | solution.py:393
  67.9 12.6 %collective-permute-start.17 = (bf16[3,128,256]{2,1,0:T(8,128)(2,1)S(1)}, bf16[3,128,256]{2,1,0:T(8,128)(2,1)S(1)}, u32[]{:S(2)}, u32[]{:S(2)}) collective-permute-start(bf16[3,128,256]{2,1,0:T(8,128)(2,1)S(1)} %get-tuple-element.76.refs_0_), channel_id=1, source_target_pairs={{0,2},{1,3},{2,0},{3,1},{4,6},{5,7},{6,4},{7,5},{8,10},{9,11},{10,... | collective-permute-start | bytes 589832 | tf_op jit(solution)/shard_map/ppermute | solution.py:387
  69.1 11.5 %collective-permute-start.18 = (bf16[3,128,256]{2,1,0:T(8,128)(2,1)S(1)}, bf16[3,128,256]{2,1,0:T(8,128)(2,1)S(1)}, u32[]{:S(2)}, u32[]{:S(2)}) collective-permute-start(bf16[3,128,256]{2,1,0:T(8,128)(2,1)S(1)} %get-tuple-element.79.refs_4_), channel_id=1, source_target_pairs={{0,4},{4,0},{8,12},{12,8},{16,20},{20,16},{24,28},{28,24},{1,5},{5... | collective-permute-start | bytes 589832 | tf_op jit(solution)/shard_map/ppermute | solution.py:390
  70.6 13.2 %collective-permute-start.21 = (bf16[3,128,256]{2,1,0:T(8,128)(2,1)S(1)}, bf16[3,128,256]{2,1,0:T(8,128)(2,1)S(1)}, u32[]{:S(2)}, u32[]{:S(2)}) collective-permute-start(bf16[3,128,256]{2,1,0:T(8,128)(2,1)S(1)} %get-tuple-element.76.refs_0_), channel_id=1, source_target_pairs={{0,4},{4,0},{8,12},{12,8},{16,20},{20,16},{24,28},{28,24},{1,5},{5... | collective-permute-start | bytes 589832 | tf_op jit(solution)/shard_map/ppermute | solution.py:390
  74.2 10.5 %collective-permute-start.20 = (bf16[3,128,256]{2,1,0:T(8,128)(2,1)S(1)}, bf16[3,128,256]{2,1,0:T(8,128)(2,1)S(1)}, u32[]{:S(2)}, u32[]{:S(2)}) collective-permute-start(bf16[3,128,256]{2,1,0:T(8,128)(2,1)S(1)} %get-tuple-element.79.refs_4_), channel_id=1, source_target_pairs={{0,2},{1,3},{2,0},{3,1},{4,6},{5,7},{6,4},{7,5},{8,10},{9,11},{10,... | collective-permute-start | bytes 589832 | tf_op jit(solution)/shard_map/ppermute | solution.py:387
  80.5 14.1 %collective-permute-start.23 = (bf16[3,128,256]{2,1,0:T(8,128)(2,1)S(1)}, bf16[3,128,256]{2,1,0:T(8,128)(2,1)S(1)}, u32[]{:S(2)}, u32[]{:S(2)}) collective-permute-start(bf16[3,128,256]{2,1,0:T(8,128)(2,1)S(1)} %get-tuple-element.89.refs_0_), channel_id=1, source_target_pairs={{0,2},{1,3},{2,0},{3,1},{4,6},{5,7},{6,4},{7,5},{8,10},{9,11},{10,... | collective-permute-start | bytes 589832 | tf_op jit(solution)/shard_map/ppermute | solution.py:387
  81.7 14.5 %collective-permute-start.24 = (bf16[3,128,256]{2,1,0:T(8,128)(2,1)S(1)}, bf16[3,128,256]{2,1,0:T(8,128)(2,1)S(1)}, u32[]{:S(2)}, u32[]{:S(2)}) collective-permute-start(bf16[3,128,256]{2,1,0:T(8,128)(2,1)S(1)} %get-tuple-element.90.refs_4_), channel_id=1, source_target_pairs={{0,4},{4,0},{8,12},{12,8},{16,20},{20,16},{24,28},{28,24},{1,5},{5... | collective-permute-start | bytes 589832 | tf_op jit(solution)/shard_map/ppermute | solution.py:390
  83.2 10.5 %collective-permute-start.22 = (bf16[3,128,256]{2,1,0:T(8,128)(2,1)S(1)}, bf16[3,128,256]{2,1,0:T(8,128)(2,1)S(1)}, u32[]{:S(2)}, u32[]{:S(2)}) collective-permute-start(bf16[3,128,256]{2,1,0:T(8,128)(2,1)S(1)} %collective-permute-done.17.refs_1_), channel_id=1, source_target_pairs={{0,4},{4,0},{8,12},{12,8},{16,20},{20,16},{24,28},{28,24},{1,5},{5... | collective-permute-start | bytes 589832 | tf_op jit(solution)/shard_map/ppermute | solution.py:390
  83.7 13.6 %collective-permute-start.19 = (bf16[3,128,256]{2,1,0:T(8,128)(2,1)S(1)}, bf16[3,128,256]{2,1,0:T(8,128)(2,1)S(1)}, u32[]{:S(2)}, u32[]{:S(2)}) collective-permute-start(bf16[3,128,256]{2,1,0:T(8,128)(2,1)S(1)} %collective-permute-done.18.refs_2_), channel_id=1, source_target_pairs={{0,2},{1,3},{2,0},{3,1},{4,6},{5,7},{6,4},{7,5},{8,10},{9,11},{10,... | collective-permute-start | bytes 589832 | tf_op jit(solution)/shard_map/ppermute | solution.py:387
  84.7 17.0 %collective-permute-start.27 = (bf16[3,128,256]{2,1,0:T(8,128)(2,1)S(1)}, bf16[3,128,256]{2,1,0:T(8,128)(2,1)S(1)}, u32[]{:S(2)}, u32[]{:S(2)}) collective-permute-start(bf16[3,128,256]{2,1,0:T(8,128)(2,1)S(1)} %get-tuple-element.89.refs_0_), channel_id=1, source_target_pairs={{0,4},{4,0},{8,12},{12,8},{16,20},{20,16},{24,28},{28,24},{1,5},{5... | collective-permute-start | bytes 589832 | tf_op jit(solution)/shard_map/ppermute | solution.py:390
  106.4 10.3 %collective-permute-start.31 = (bf16[3,128,512]{2,1,0:T(8,128)(2,1)S(1)}, bf16[3,128,512]{2,1,0:T(8,128)(2,1)S(1)}, u32[]{:S(2)}, u32[]{:S(2)}) collective-permute-start(bf16[3,128,512]{2,1,0:T(8,128)(2,1)S(1)} %get-tuple-element.97.refs_0_), channel_id=1, source_target_pairs={{0,1},{1,0},{2,3},{3,2},{4,5},{5,4},{6,7},{7,6},{8,9},{9,8},{10,11... | collective-permute-start | bytes 1179656 | tf_op jit(solution)/shard_map/ppermute | solution.py:384
  106.5 10.2 %collective-permute-start.32 = (bf16[3,128,512]{2,1,0:T(8,128)(2,1)S(1)}, bf16[3,128,512]{2,1,0:T(8,128)(2,1)S(1)}, u32[]{:S(2)}, u32[]{:S(2)}) collective-permute-start(bf16[3,128,512]{2,1,0:T(8,128)(2,1)S(1)} %get-tuple-element.98.refs_1_), channel_id=1, source_target_pairs={{0,1},{1,0},{2,3},{3,2},{4,5},{5,4},{6,7},{7,6},{8,9},{9,8},{10,11... | collective-permute-start | bytes 1179656 | tf_op jit(solution)/shard_map/ppermute | solution.py:384
  111.0 11.2 %collective-permute-start.33 = (bf16[3,64,512]{2,1,0:T(8,128)(2,1)}, bf16[3,64,512]{2,1,0:T(8,128)(2,1)S(1)}, u32[]{:S(2)}, u32[]{:S(2)}) collective-permute-start(bf16[3,64,512]{2,1,0:T(8,128)(2,1)} %copy-done.2), channel_id=1, source_target_pairs={{0,8},{4,12},{8,0},{12,4},{16,24},{20,28},{24,16},{28,20},{1,9},{5... | collective-permute-start | bytes 589832 | tf_op jit(solution)/shard_map/ppermute | solution.py:393
  111.0 17.5 %collective-permute-start.34 = (bf16[3,64,512]{2,1,0:T(8,128)(2,1)}, bf16[3,64,512]{2,1,0:T(8,128)(2,1)}, u32[]{:S(2)}, u32[]{:S(2)}) collective-permute-start(bf16[3,64,512]{2,1,0:T(8,128)(2,1)} %copy-done.1), channel_id=1, source_target_pairs={{0,16},{4,20},{8,24},{12,28},{16,0},{20,4},{24,8},{28,12},{1,17},{... | collective-permute-start | bytes 589832 | tf_op jit(solution)/shard_map/ppermute | solution.py:393
  114.1 14.5 %collective-permute-start.35 = (bf16[3,64,512]{2,1,0:T(8,128)(2,1)}, bf16[3,64,512]{2,1,0:T(8,128)(2,1)}, u32[]{:S(2)}, u32[]{:S(2)}) collective-permute-start(bf16[3,64,512]{2,1,0:T(8,128)(2,1)} %copy-done), channel_id=1, source_target_pairs={{0,24},{4,28},{8,16},{12,20},{16,8},{20,12},{24,0},{28,4},{1,25},{... | collective-permute-start | bytes 589832 | tf_op jit(solution)/shard_map/ppermute | solution.py:393
  129.8 9.6 %collective-permute-start.36 = (bf16[3,64,512]{2,1,0:T(8,128)(2,1)S(1)}, bf16[3,64,512]{2,1,0:T(8,128)(2,1)S(1)}, u32[]{:S(2)}, u32[]{:S(2)}) collective-permute-start(bf16[3,64,512]{2,1,0:T(8,128)(2,1)S(1)} %shard_map.57.refs_0_), channel_id=1, source_target_pairs={{0,8},{4,12},{8,0},{12,4},{16,24},{20,28},{24,16},{28,20},{1,9},{5... | collective-permute-start | bytes 589832 | tf_op jit(solution)/shard_map/ppermute | solution.py:393
  134.1 12.5 %collective-permute-start.38 = (bf16[3,64,512]{2,1,0:T(8,128)(2,1)S(1)}, bf16[3,64,512]{2,1,0:T(8,128)(2,1)S(1)}, u32[]{:S(2)}, u32[]{:S(2)}) collective-permute-start(bf16[3,64,512]{2,1,0:T(8,128)(2,1)S(1)} %shard_map.57.refs_0_), channel_id=1, source_target_pairs={{0,24},{4,28},{8,16},{12,20},{16,8},{20,12},{24,0},{28,4},{1,25},{... | collective-permute-start | bytes 589832 | tf_op jit(solution)/shard_map/ppermute | solution.py:393
  136.5 16.1 %collective-permute-start.37 = (bf16[3,64,512]{2,1,0:T(8,128)(2,1)S(1)}, bf16[3,64,512]{2,1,0:T(8,128)(2,1)S(1)}, u32[]{:S(2)}, u32[]{:S(2)}) collective-permute-start(bf16[3,64,512]{2,1,0:T(8,128)(2,1)S(1)} %shard_map.57.refs_0_), channel_id=1, source_target_pairs={{0,16},{4,20},{8,24},{12,28},{16,0},{20,4},{24,8},{28,12},{1,17},{... | collective-permute-start | bytes 589832 | tf_op jit(solution)/shard_map/ppermute | solution.py:393
  140.4 13.2 %collective-permute-start.40 = (bf16[3,128,256]{2,1,0:T(8,128)(2,1)S(1)}, bf16[3,128,256]{2,1,0:T(8,128)(2,1)S(1)}, u32[]{:S(2)}, u32[]{:S(2)}) collective-permute-start(bf16[3,128,256]{2,1,0:T(8,128)(2,1)S(1)} %get-tuple-element.107), channel_id=1, source_target_pairs={{0,4},{4,0},{8,12},{12,8},{16,20},{20,16},{24,28},{28,24},{1,5},{5... | collective-permute-start | bytes 589832 | tf_op jit(solution)/shard_map/ppermute | solution.py:390
  141.4 12.1 %collective-permute-start.39 = (bf16[3,128,256]{2,1,0:T(8,128)(2,1)S(1)}, bf16[3,128,256]{2,1,0:T(8,128)(2,1)S(1)}, u32[]{:S(2)}, u32[]{:S(2)}) collective-permute-start(bf16[3,128,256]{2,1,0:T(8,128)(2,1)S(1)} %get-tuple-element.104.a0), channel_id=1, source_target_pairs={{0,2},{1,3},{2,0},{3,1},{4,6},{5,7},{6,4},{7,5},{8,10},{9,11},{10,... | collective-permute-start | bytes 589832 | tf_op jit(solution)/shard_map/ppermute | solution.py:387
  155.3 11.1 %collective-permute-start.42 = (bf16[3,128,256]{2,1,0:T(8,128)(2,1)S(1)}, bf16[3,128,256]{2,1,0:T(8,128)(2,1)S(1)}, u32[]{:S(2)}, u32[]{:S(2)}) collective-permute-start(bf16[3,128,256]{2,1,0:T(8,128)(2,1)S(1)} %get-tuple-element.113.a0), channel_id=1, source_target_pairs={{0,2},{1,3},{2,0},{3,1},{4,6},{5,7},{6,4},{7,5},{8,10},{9,11},{10,... | collective-permute-start | bytes 589832 | tf_op jit(solution)/shard_map/ppermute | solution.py:387
  (24 other events, 241.2 us)

commit v3 on v2

--- a/solution.py
+++ b/solution.py
@@ -313,16 +313,16 @@
 def last_kernel(place, a0, a1, a2, a3, x, out_weight, gain, keep, send):
     x_bit, core = place[0], place[1]
     seqs, rows, _ = x.shape
-    quarter = keep.shape[3]
+    quarter = keep.shape[2]
     columns = [head_columns((a0, a1, a2, a3), s * HEAD_DIM) for s in range(seqs)]
     old = jnp.concatenate([x[s] for s in range(seqs)], axis=0)
     made = normalized(jnp.concatenate(columns, axis=0), old, out_weight, gain)
-    half = jnp.where(x_bit == 1, made[:, 2 * quarter :], made[:, : 2 * quarter]).astype(BF16)
+    half = jnp.where(x_bit == 1, made[:, 2 * quarter :], made[:, : 2 * quarter])
     low, high = half[:, :quarter], half[:, quarter:]
     mine, theirs = jnp.where(core == 1, high, low), jnp.where(core == 1, low, high)
     for s in range(seqs):
-        keep[s % 2, s // 2] = mine[s * rows : (s + 1) * rows]
-        send[s % 2, s // 2] = theirs[s * rows : (s + 1) * rows]
+        keep[s % 2, s // 2] = mine[s * rows : (s + 1) * rows].T.astype(BF16)
+        send[s % 2, s // 2] = theirs[s * rows : (s + 1) * rows].T.astype(BF16)
 
 
 def last_layer(place, attended, x, out_weight, gain):
@@ -331,32 +331,30 @@
         last_kernel,
         in_specs=[SMEM] + [FULL] * 7,
         out_specs=[FULL] * 2,
-        out_shape=[jax.ShapeDtypeStruct((2, seqs // 2, rows, width // 4), BF16)] * 2,
+        out_shape=[jax.ShapeDtypeStruct((2, seqs // 2, width // 4, rows), BF16)] * 2,
         compiler_params=params(),
         cost_estimate=cost(2 * seqs * rows * width * width, 3 * nbytes(x) + nbytes(out_weight)),
     )(place, *attended, x, out_weight, gain)
-    return [a.reshape(seqs, rows, width // 4) for a in made]
+    return [a.reshape(seqs, width // 4, rows) for a in made]
 
 
 def placed_kernel(count, place, *refs):
     out = refs[-1]
-    rows = refs[0].shape[1]
+    rows = refs[0].shape[2]
     for n, ref in enumerate(refs[:-1]):
         core = jnp.bitwise_xor(place[1], n // count)
         start = (core * count + jnp.bitwise_xor(place[3], n % count)) * rows
-        out[:, pl.ds(pl.multiple_of(start, rows), rows), :] = ref[...]
+        out[:, :, pl.ds(pl.multiple_of(start, rows), rows)] = ref[...]
 
 
 def placed(place, kept, other):
-    seqs, rows, width = kept[0].shape
+    seqs, width, rows = kept[0].shape
     count = len(kept)
-    piece = pl.BlockSpec((2, rows, width), lambda s: (s, 0, 0))
     return pl.pallas_call(
         functools.partial(placed_kernel, count),
-        grid=(seqs // 2,),
-        in_specs=[SMEM] + [piece] * (2 * count),
-        out_specs=pl.BlockSpec((2, 2 * count * rows, width), lambda s: (s, 0, 0)),
-        out_shape=jax.ShapeDtypeStruct((seqs, 2 * count * rows, width), BF16),
+        in_specs=[SMEM] + [FULL] * (2 * count),
+        out_specs=FULL,
+        out_shape=jax.ShapeDtypeStruct((seqs, width, 2 * count * rows), BF16),
         compiler_params=params(),
         cost_estimate=cost(0, 4 * nbytes(*kept)),
     )(place, *kept, *other)
@@ -388,6 +386,10 @@
 
     def over_y(a):
         return lax.ppermute(a, "rows", [(i, i ^ 1) for i in range(n_rows)])
+
+    def over_xy(a):
+        order = [(r * n_groups + g, (r ^ 1) * n_groups + (g ^ 2)) for r in range(n_rows) for g in range(n_groups)]
+        return lax.ppermute(a, ("rows", "heads"), order)
 
     def over_z(a, d):
         return lax.ppermute(a, "rows", [(i, i ^ (2 * d)) for i in range(n_rows)])
@@ -444,7 +446,8 @@
         weights = softmax_sum(terms)
         gain = norm_gain[layer : layer + 1]
         pieces = [weights] + [over_z(weights, d) for d in range(1, depth)]
-        attended = []
+        attended, made = [], []
+        both = layer + 2 < layers
         for g in range(count):
             near_part, far_part = weighted_values(place, pieces[g * each : (g + 1) * each], value)
             if g:
@@ -453,16 +456,22 @@
                     (near_part, far_part, before[1], before[2])
                 )
             x_near, y_near = over_x(near_part), over_y(far_part)
-            parts = [near_part, x_near, y_near, over_x(y_near)]
-            if more:
-                parts += [far_part, over_x(far_part), over_y(near_part), over_y(x_near)]
-            attended.append(parts)
+            if not more:
+                attended.append([near_part, x_near, y_near, over_xy(far_part)])
+                continue
+            x_far, y_far = over_x(far_part), over_y(near_part)
+            if g:
+                done = next_layer(place, g - 1, attended[-1], near[g - 1], far[g - 1], out_mat, gain, weight, both)
+                x_near, y_near, *done = lax.optimization_barrier((x_near, y_near, *done))
+                made.append(done)
+            attended.append(
+                [near_part, x_near, y_near, over_x(y_near), far_part, x_far, y_far, over_y(x_near)]
+            )
         if more:
-            both = layer + 2 < layers
-            made = [
+            g = count - 1
+            made.append(
                 next_layer(place, g, attended[g], near[g], far[g], out_mat, gain, weight, both)
-                for g in range(count)
-            ]
+            )
             near = [m[0] for m in made]
             far = [m[1] for m in made] if both else near
             queries, keys, values = ([m[i] for m in made] for i in (-3, -2, -1))
@@ -471,7 +480,7 @@
         keep, send = last_layer(place, attended[g], near[g], out_mat, gain)
         kept.append(keep)
         other.append(over_core(send))
-    return placed(place, kept, other)
+    return jnp.swapaxes(placed(place, kept, other), 1, 2)
 
 
 def solution(mesh):

time: 174 us -> 166 us (0.954)
  waiting for transfers between devices: 82.4 us -> 70.7 us
  starting transfers between devices: 52.4 us -> 56.1 us
    ppermute x12, waiting for transfers between devices: 46.1 us -> 40 us  [over_z(): return lax.ppermute(a, 'rows', [(i, i ^ 2 * d) for i in range(n_rows)])]
    ppermute x11, waiting for transfers between devices: 16.8 us -> 11.1 us  [over_y(): return lax.ppermute(a, 'rows', [(i, i ^ 1) for i in range(n_rows)])]
    ppermute x12, starting transfers between devices: 21.7 us -> 24 us  [over_z(): return lax.ppermute(a, 'rows', [(i, i ^ 2 * d) for i in range(n_rows)])]
    ppermute x13 -> x11, waiting for transfers between devices: 15.9 us -> 13.9 us  [over_x(): return lax.ppermute(a, 'heads', [(i, i ^ 2) for i in range(n_groups)])]
    ppermute x0 -> x2, waiting for transfers between devices: none -> 2.03 us  [over_xy(): return lax.ppermute(a, ('rows', 'heads'), order)]
    ppermute x0 -> x2, starting transfers between devices: none -> 1.85 us  [over_xy(): return lax.ppermute(a, ('rows', 'heads'), order)]
    ppermute x13 -> x11, starting transfers between devices: 15.4 us -> 13.7 us  [over_x(): return lax.ppermute(a, 'heads', [(i, i ^ 2) for i in range(n_groups)])]
  transfers between devices with their start and end apart: 47 -> 47, of which waited for: 22 -> 22; matrix products, arithmetic and copies ran while one was open for 4% -> 4% of each run, Pallas kernels for 14% -> 15%
where the time goes in v3:
time: 166 us
  waiting for transfers between devices  70.7 us (43%)
  starting transfers between devices  56.1 us (34%)
  Pallas kernels  27.5 us (17%)
  local copies, waits for them, and re-layouts  10.6 us (6%)
    ppermute x12, waiting for transfers between devices, over_z(): return lax.ppermute(a, 'rows', [(i, i ^ 2 * d) for i in range(n_rows)])  40 us
    ppermute x12, starting transfers between devices, over_z(): return lax.ppermute(a, 'rows', [(i, i ^ 2 * d) for i in range(n_rows)])  24 us
    ppermute x11, starting transfers between devices, over_y(): return lax.ppermute(a, 'rows', [(i, i ^ 1) for i in range(n_rows)])  14.6 us
    ppermute x11, waiting for transfers between devices, over_x(): return lax.ppermute(a, 'heads', [(i, i ^ 2) for i in range(n_groups)])  13.9 us
    ppermute x11, starting transfers between devices, over_x(): return lax.ppermute(a, 'heads', [(i, i ^ 2) for i in range(n_groups)])  13.7 us
    ppermute x11, waiting for transfers between devices, over_y(): return lax.ppermute(a, 'rows', [(i, i ^ 1) for i in range(n_rows)])  11.1 us
    pallas_call x2, Pallas kernels, next_layer(): pl.pallas_call(functools.partial(next_kernel, g), in_specs=[SMEM] + [FULL...  8.36 us
    pallas_call x2, Pallas kernels, first(): pl.pallas_call(first_kernel, in_specs=[SMEM] + [FULL] * 7, out_specs=[FUL...  4.92 us
  transfers between devices with their start and end apart: 47, of which 22 were waited for; matrix products, arithmetic and copies ran while one was open for 4% of the time, Pallas kernels for 15%

profile of v3, /device:TPU:0, one launch (start us, length us, event | category | flops | bytes accessed | tf_op | source)
XLA Modules:
  0.0 165.8 jit_solution(14340270327535513362)
XLA Ops:
  2.7 2.6 %collective-permute-start.1 = (bf16[2,256,384]{2,1,0:T(8,128)(2,1)S(1)}, bf16[2,256,384]{2,1,0:T(8,128)(2,1)S(1)}, u32[]{:S(2)}, u32[]{:S(2)}) collective-permute-start(bf16[2,256,384]{2,1,0:T(8,128)(2,1)S(1)} %pad_maximum_fusion.2.p0), channel_id=1, source_target_pairs={{0,2},{1,3},{2,0},{3,1},{4,6},{5,7},{6,4},{7,5},{8,10},{9,11},{10,... | collective-permute-start | bytes 1179656 | tf_op jit(solution)/shard_map/ppermute | solution.py:385
  8.5 6.7 %collective-permute-done.1.p2 = bf16[2,256,384]{2,1,0:T(8,128)(2,1)S(1)} collective-permute-done((bf16[2,256,384]{2,1,0:T(8,128)(2,1)S(1)}, bf16[2,256,384]{2,1,0:T(8,128)(2,1)S(1)}, u32[]{:S(2)}, u32[]{:S(2)}) %collective-permute-start.1) | collective-permute-done | bytes 393248 | tf_op jit(solution)/shard_map/ppermute | solution.py:385
  15.2 2.0 %collective-permute-start.5 = (bf16[2,256,384]{2,1,0:T(8,128)(2,1)S(1)}, bf16[2,256,384]{2,1,0:T(8,128)(2,1)S(1)}, u32[]{:S(2)}, u32[]{:S(2)}) collective-permute-start(bf16[2,256,384]{2,1,0:T(8,128)(2,1)S(1)} %collective-permute-done.1.p2), channel_id=1, source_target_pairs={{0,4},{4,0},{8,12},{12,8},{16,20},{20,16},{24,28},{28,24},{1,5},{5... | collective-permute-start | bytes 1179656 | tf_op jit(solution)/shard_map/ppermute | solution.py:388
  18.7 2.0 %dynamic-slice_bitcast_fusion.3 = (bf16[768,192]{1,0:T(8,128)(2,1)S(1)}, bf16[768,192]{1,0:T(8,128)(2,1)S(1)}, bf16[768,192]{1,0:T(8,128)(2,1)S(1)}) fusion(bf16[2,768,3,768]{3,1,2,0:T(8,128)(2,1)} %param.5, s32[]{:T(128)S(6)} %select_n.71), kind=kLoop, calls=%fused_computation.7 | loop fusion | bytes 1769476 | tf_op jit(solution)/shard_map/reshape | solution.py:401
  20.7 2.9 %collective-permute-done.2.p3 = bf16[2,256,384]{2,1,0:T(8,128)(2,1)S(1)} collective-permute-done((bf16[2,256,384]{2,1,0:T(8,128)(2,1)S(1)}, bf16[2,256,384]{2,1,0:T(8,128)(2,1)S(1)}, u32[]{:S(2)}, u32[]{:S(2)}) %collective-permute-start.2) | collective-permute-done | bytes 393248 | tf_op jit(solution)/shard_map/ppermute | solution.py:385
  23.6 2.5 %shard_map.46 = (bf16[4,256,768]{2,1,0:T(8,128)(2,1)S(1)}, bf16[3,256,256]{2,1,0:T(8,128)(2,1)S(1)}, bf16[3,256,256]{2,1,0:T(8,128)(2,1)S(1)}, bf16[3,256,256]{2,1,0:T(8,128)(2,1)S(1)}) custom-call(s32[5]{0:T(128)S(1)} %stack.23.place, bf16[2,256,384]{2,1,0:T(8,128)(2,1)S(1)} %pad_maximum_fusion.2.p0, bf16[2,256,384]{2,1,0:T(8,128)(2,1)S(1)} %collective-permute-done.p1, ...), custom_call_target="tpu_custom_call" | custom-call | flops 905969664 | bytes 9830400 | tf_op jit(solution)/shard_map/pallas_call | solution.py:81
  27.3 6.0 %collective-permute-done.5.p2 = bf16[2,256,384]{2,1,0:T(8,128)(2,1)S(1)} collective-permute-done((bf16[2,256,384]{2,1,0:T(8,128)(2,1)S(1)}, bf16[2,256,384]{2,1,0:T(8,128)(2,1)S(1)}, u32[]{:S(2)}, u32[]{:S(2)}) %collective-permute-start.5) | collective-permute-done | bytes 393248 | tf_op jit(solution)/shard_map/ppermute | solution.py:388
  33.3 2.5 %shard_map.47 = (bf16[4,256,768]{2,1,0:T(8,128)(2,1)S(1)}, bf16[3,256,256]{2,1,0:T(8,128)(2,1)S(1)}, bf16[3,256,256]{2,1,0:T(8,128)(2,1)S(1)}, bf16[3,256,256]{2,1,0:T(8,128)(2,1)S(1)}) custom-call(s32[5]{0:T(128)S(1)} %stack.23.place, bf16[2,256,384]{2,1,0:T(8,128)(2,1)S(1)} %collective-permute-done.3.p0, ...), custom_call_target="tpu_custom_call" | custom-call | flops 905969664 | bytes 9830400 | tf_op jit(solution)/shard_map/pallas_call | solution.py:81
  40.4 2.6 %collective-permute-start.12 = (bf16[3,64,512]{2,1,0:T(8,128)(2,1)S(1)}, bf16[3,64,512]{2,1,0:T(8,128)(2,1)S(1)}, u32[]{:S(2)}, u32[]{:S(2)}) collective-permute-start(bf16[3,64,512]{2,1,0:T(8,128)(2,1)S(1)} %get-tuple-element.79), channel_id=1, source_target_pairs={{0,16},{4,20},{8,24},{12,28},{16,0},{20,4},{24,8},{28,12},{1,17},{... | collective-permute-start | bytes 589832 | tf_op jit(solution)/shard_map/ppermute | solution.py:395
  43.2 2.1 %dynamic-slice_bitcast_fusion = (bf16[768,192]{1,0:T(8,128)(2,1)S(1)}, bf16[768,192]{1,0:T(8,128)(2,1)S(1)}, bf16[768,192]{1,0:T(8,128)(2,1)S(1)}) fusion(bf16[2,768,3,768]{3,1,2,0:T(8,128)(2,1)} %param.5, s32[]{:T(128)S(6)} %select_n.72), kind=kLoop, calls=%fused_computation.4 | loop fusion | bytes 1769476 | tf_op jit(solution)/shard_map/reshape | solution.py:401
  45.9 3.5 %collective-permute-done.11.refs_1_ = bf16[3,64,512]{2,1,0:T(8,128)(2,1)S(1)} collective-permute-done((bf16[3,64,512]{2,1,0:T(8,128)(2,1)S(1)}, bf16[3,64,512]{2,1,0:T(8,128)(2,1)S(1)}, u32[]{:S(2)}, u32[]{:S(2)}) %collective-permute-start.11) | collective-permute-done | bytes 196640 | tf_op jit(solution)/shard_map/ppermute | solution.py:395
  49.4 8.1 %collective-permute-done.12.refs_2_ = bf16[3,64,512]{2,1,0:T(8,128)(2,1)S(1)} collective-permute-done((bf16[3,64,512]{2,1,0:T(8,128)(2,1)S(1)}, bf16[3,64,512]{2,1,0:T(8,128)(2,1)S(1)}, u32[]{:S(2)}, u32[]{:S(2)}) %collective-permute-start.12) | collective-permute-done | bytes 196640 | tf_op jit(solution)/shard_map/ppermute | solution.py:395
  57.8 3.8 %collective-permute-start.16 = (bf16[3,64,512]{2,1,0:T(8,128)(2,1)S(1)}, bf16[3,64,512]{2,1,0:T(8,128)(2,1)S(1)}, u32[]{:S(2)}, u32[]{:S(2)}) collective-permute-start(bf16[3,64,512]{2,1,0:T(8,128)(2,1)S(1)} %shard_map.50.refs_0_), channel_id=1, source_target_pairs={{0,8},{4,12},{8,0},{12,4},{16,24},{20,28},{24,16},{28,20},{1,9},{5... | collective-permute-start | bytes 589832 | tf_op jit(solution)/shard_map/ppermute | solution.py:395
  61.6 2.5 %collective-permute-start.15 = (bf16[3,64,512]{2,1,0:T(8,128)(2,1)S(1)}, bf16[3,64,512]{2,1,0:T(8,128)(2,1)S(1)}, u32[]{:S(2)}, u32[]{:S(2)}) collective-permute-start(bf16[3,64,512]{2,1,0:T(8,128)(2,1)S(1)} %shard_map.50.refs_0_), channel_id=1, source_target_pairs={{0,24},{4,28},{8,16},{12,20},{16,8},{20,12},{24,0},{28,4},{1,25},{... | collective-permute-start | bytes 589832 | tf_op jit(solution)/shard_map/ppermute | solution.py:395
  64.1 2.9 %collective-permute-done.16.refs_1_ = bf16[3,64,512]{2,1,0:T(8,128)(2,1)S(1)} collective-permute-done((bf16[3,64,512]{2,1,0:T(8,128)(2,1)S(1)}, bf16[3,64,512]{2,1,0:T(8,128)(2,1)S(1)}, u32[]{:S(2)}, u32[]{:S(2)}) %collective-permute-start.16) | collective-permute-done | bytes 196640 | tf_op jit(solution)/shard_map/ppermute | solution.py:395
  70.6 3.5 %collective-permute-start.14 = (bf16[3,64,512]{2,1,0:T(8,128)(2,1)S(1)}, bf16[3,64,512]{2,1,0:T(8,128)(2,1)S(1)}, u32[]{:S(2)}, u32[]{:S(2)}) collective-permute-start(bf16[3,64,512]{2,1,0:T(8,128)(2,1)S(1)} %shard_map.50.refs_0_), channel_id=1, source_target_pairs={{0,16},{4,20},{8,24},{12,28},{16,0},{20,4},{24,8},{28,12},{1,17},{... | collective-permute-start | bytes 589832 | tf_op jit(solution)/shard_map/ppermute | solution.py:395
  78.1 2.4 %collective-permute-done.14.refs_0_ = bf16[3,64,512]{2,1,0:T(8,128)(2,1)S(1)} collective-permute-done((bf16[3,64,512]{2,1,0:T(8,128)(2,1)S(1)}, bf16[3,64,512]{2,1,0:T(8,128)(2,1)S(1)}, u32[]{:S(2)}, u32[]{:S(2)}) %collective-permute-start.14) | collective-permute-done | bytes 196640 | tf_op jit(solution)/shard_map/ppermute | solution.py:395
  85.6 4.3 %shard_map.53 = (bf16[4,128,768]{2,1,0:T(8,128)(2,1)S(1)}, bf16[3,128,512]{2,1,0:T(8,128)(2,1)S(1)}, bf16[3,128,512]{2,1,0:T(8,128)(2,1)S(1)}, bf16[3,128,512]{2,1,0:T(8,128)(2,1)S(1)}) custom-call(s32[5]{0:T(128)S(1)} %stack.23.place, bf16[3,128,256]{2,1,0:T(8,128)(2,1)S(1)} %get-tuple-element.84.refs_0_, ...), custom_call_target="tpu_custom_call" | custom-call | flops 2113929216 | bytes 5210112 | tf_op jit(solution)/shard_map/pallas_call | solution.py:302
  91.7 1.7 %collective-permute-start.28 = (bf16[3,128,256]{2,1,0:T(8,128)(2,1)S(1)}, bf16[3,128,256]{2,1,0:T(8,128)(2,1)S(1)}, u32[]{:S(2)}, u32[]{:S(2)}) collective-permute-start(bf16[3,128,256]{2,1,0:T(8,128)(2,1)S(1)} %collective-permute-done.19.refs_1_), channel_id=1, source_target_pairs={{0,4},{4,0},{8,12},{12,8},{16,20},{20,16},{24,28},{28,24},{1,5},{5... | collective-permute-start | bytes 589832 | tf_op jit(solution)/shard_map/ppermute | solution.py:388
  94.6 2.8 %collective-permute-done.28.refs_7_ = bf16[3,128,256]{2,1,0:T(8,128)(2,1)S(1)} collective-permute-done((bf16[3,128,256]{2,1,0:T(8,128)(2,1)S(1)}, bf16[3,128,256]{2,1,0:T(8,128)(2,1)S(1)}, u32[]{:S(2)}, u32[]{:S(2)}) %collective-permute-start.28) | collective-permute-done | bytes 196640 | tf_op jit(solution)/shard_map/ppermute | solution.py:388
  97.4 1.7 %collective-permute-done.25.refs_3_ = bf16[3,128,256]{2,1,0:T(8,128)(2,1)S(1)} collective-permute-done((bf16[3,128,256]{2,1,0:T(8,128)(2,1)S(1)}, bf16[3,128,256]{2,1,0:T(8,128)(2,1)S(1)}, u32[]{:S(2)}, u32[]{:S(2)}) %collective-permute-start.25) | collective-permute-done | bytes 196640 | tf_op jit(solution)/shard_map/ppermute | solution.py:385
  99.1 4.1 %shard_map.54 = (bf16[4,128,768]{2,1,0:T(8,128)(2,1)S(1)}, bf16[3,128,512]{2,1,0:T(8,128)(2,1)S(1)}, bf16[3,128,512]{2,1,0:T(8,128)(2,1)S(1)}, bf16[3,128,512]{2,1,0:T(8,128)(2,1)S(1)}) custom-call(s32[5]{0:T(128)S(1)} %stack.23.place, bf16[3,128,256]{2,1,0:T(8,128)(2,1)S(1)} %get-tuple-element.86.refs_0_, ...), custom_call_target="tpu_custom_call" | custom-call | flops 2113929216 | bytes 5210112 | tf_op jit(solution)/shard_map/pallas_call | solution.py:302
  110.3 2.4 %collective-permute-start.35 = (bf16[3,64,512]{2,1,0:T(8,128)(2,1)}, bf16[3,64,512]{2,1,0:T(8,128)(2,1)}, u32[]{:S(2)}, u32[]{:S(2)}) collective-permute-start(bf16[3,64,512]{2,1,0:T(8,128)(2,1)} %copy-done), channel_id=1, source_target_pairs={{0,24},{4,28},{8,16},{12,20},{16,8},{20,12},{24,0},{28,4},{1,25},{... | collective-permute-start | bytes 589832 | tf_op jit(solution)/shard_map/ppermute | solution.py:395
  114.7 3.9 %collective-permute-done.33.refs_1_ = bf16[3,64,512]{2,1,0:T(8,128)(2,1)S(1)} collective-permute-done((bf16[3,64,512]{2,1,0:T(8,128)(2,1)}, bf16[3,64,512]{2,1,0:T(8,128)(2,1)S(1)}, u32[]{:S(2)}, u32[]{:S(2)}) %collective-permute-start.33) | collective-permute-done | bytes 196640 | tf_op jit(solution)/shard_map/ppermute | solution.py:395
  118.6 7.4 %collective-permute-done.34.refs_2_ = bf16[3,64,512]{2,1,0:T(8,128)(2,1)} collective-permute-done((bf16[3,64,512]{2,1,0:T(8,128)(2,1)}, bf16[3,64,512]{2,1,0:T(8,128)(2,1)}, u32[]{:S(2)}, u32[]{:S(2)}) %collective-permute-start.34) | collective-permute-done | bytes 196640 | tf_op jit(solution)/shard_map/ppermute | solution.py:395
  127.4 3.8 %collective-permute-start.36 = (bf16[3,64,512]{2,1,0:T(8,128)(2,1)S(1)}, bf16[3,64,512]{2,1,0:T(8,128)(2,1)S(1)}, u32[]{:S(2)}, u32[]{:S(2)}) collective-permute-start(bf16[3,64,512]{2,1,0:T(8,128)(2,1)S(1)} %shard_map.57.refs_0_), channel_id=1, source_target_pairs={{0,8},{4,12},{8,0},{12,4},{16,24},{20,28},{24,16},{28,20},{1,9},{5... | collective-permute-start | bytes 589832 | tf_op jit(solution)/shard_map/ppermute | solution.py:395
  131.1 1.7 %collective-permute-start.38 = (bf16[3,64,512]{2,1,0:T(8,128)(2,1)S(1)}, bf16[3,64,512]{2,1,0:T(8,128)(2,1)S(1)}, u32[]{:S(2)}, u32[]{:S(2)}) collective-permute-start(bf16[3,64,512]{2,1,0:T(8,128)(2,1)S(1)} %shard_map.57.refs_0_), channel_id=1, source_target_pairs={{0,24},{4,28},{8,16},{12,20},{16,8},{20,12},{24,0},{28,4},{1,25},{... | collective-permute-start | bytes 589832 | tf_op jit(solution)/shard_map/ppermute | solution.py:395
  132.8 4.0 %collective-permute-done.36.refs_1_ = bf16[3,64,512]{2,1,0:T(8,128)(2,1)S(1)} collective-permute-done((bf16[3,64,512]{2,1,0:T(8,128)(2,1)S(1)}, bf16[3,64,512]{2,1,0:T(8,128)(2,1)S(1)}, u32[]{:S(2)}, u32[]{:S(2)}) %collective-permute-start.36) | collective-permute-done | bytes 196640 | tf_op jit(solution)/shard_map/ppermute | solution.py:395
  143.0 6.2 %collective-permute-done.37.refs_0_ = bf16[3,64,512]{2,1,0:T(8,128)(2,1)S(1)} collective-permute-done((bf16[3,64,512]{2,1,0:T(8,128)(2,1)S(1)}, bf16[3,64,512]{2,1,0:T(8,128)(2,1)S(1)}, u32[]{:S(2)}, u32[]{:S(2)}) %collective-permute-start.37) | collective-permute-done | bytes 196640 | tf_op jit(solution)/shard_map/ppermute | solution.py:395
  153.6 2.1 %shard_map.60 = (bf16[2,2,192,128]{3,2,1,0:T(8,128)(2,1)S(1)}, bf16[2,2,192,128]{3,2,1,0:T(8,128)(2,1)S(1)}) custom-call(s32[5]{0:T(128)S(1)} %stack.23.place, bf16[3,128,256]{2,1,0:T(8,128)(2,1)S(1)} %get-tuple-element.116.a0, bf16[3,128,256]{2,1,0:T(8,128)(2,1)S(1)} %collective-permute-done.39.a1, bf16[3,128,256]{2,1,0:T(8,128)(2,1)S(1)} %collective-permute-done.40.a2, ...), custom_call_target="tpu_custom_call" | custom-call | flops 603979776 | bytes 3538944 | tf_op jit(solution)/shard_map/pallas_call | solution.py:330
  157.4 2.0 %collective-permute-done.44.a3 = bf16[3,128,256]{2,1,0:T(8,128)(2,1)S(1)} collective-permute-done((bf16[3,128,256]{2,1,0:T(8,128)(2,1)S(1)}, bf16[3,128,256]{2,1,0:T(8,128)(2,1)S(1)}, u32[]{:S(2)}, u32[]{:S(2)}) %collective-permute-start.44) | collective-permute-done | bytes 196640 | tf_op jit(solution)/shard_map/ppermute | solution.py:392
  160.7 2.1 %shard_map.61 = (bf16[2,2,192,128]{3,2,1,0:T(8,128)(2,1)S(1)}, bf16[2,2,192,128]{3,2,1,0:T(8,128)(2,1)S(1)}) custom-call(s32[5]{0:T(128)S(1)} %stack.23.place, bf16[3,128,256]{2,1,0:T(8,128)(2,1)S(1)} %get-tuple-element.125.a0, bf16[3,128,256]{2,1,0:T(8,128)(2,1)S(1)} %collective-permute-done.42.a1, bf16[3,128,256]{2,1,0:T(8,128)(2,1)S(1)} %collective-permute-done.43.a2, ...), custom_call_target="tpu_custom_call" | custom-call | flops 603979776 | bytes 3538944 | tf_op jit(solution)/shard_map/pallas_call | solution.py:330
  (112 shorter events, 56.8 us)
Async XLA Ops:
  2.7 12.5 %collective-permute-start.1 = (bf16[2,256,384]{2,1,0:T(8,128)(2,1)S(1)}, bf16[2,256,384]{2,1,0:T(8,128)(2,1)S(1)}, u32[]{:S(2)}, u32[]{:S(2)}) collective-permute-start(bf16[2,256,384]{2,1,0:T(8,128)(2,1)S(1)} %pad_maximum_fusion.2.p0), channel_id=1, source_target_pairs={{0,2},{1,3},{2,0},{3,1},{4,6},{5,7},{6,4},{7,5},{8,10},{9,11},{10,... | collective-permute-start | bytes 1179656 | tf_op jit(solution)/shard_map/ppermute | solution.py:385
  5.2 11.9 %collective-permute-start.4 = (bf16[2,256,384]{2,1,0:T(8,128)(2,1)S(1)}, bf16[2,256,384]{2,1,0:T(8,128)(2,1)S(1)}, u32[]{:S(2)}, u32[]{:S(2)}) collective-permute-start(bf16[2,256,384]{2,1,0:T(8,128)(2,1)S(1)} %collective-permute-done.p1), channel_id=1, source_target_pairs={{0,4},{4,0},{8,12},{12,8},{16,20},{20,16},{24,28},{28,24},{1,5},{5... | collective-permute-start | bytes 1179656 | tf_op jit(solution)/shard_map/ppermute | solution.py:388
  6.8 16.9 %collective-permute-start.2 = (bf16[2,256,384]{2,1,0:T(8,128)(2,1)S(1)}, bf16[2,256,384]{2,1,0:T(8,128)(2,1)S(1)}, u32[]{:S(2)}, u32[]{:S(2)}) collective-permute-start(bf16[2,256,384]{2,1,0:T(8,128)(2,1)S(1)} %collective-permute-done.p1), channel_id=1, source_target_pairs={{0,2},{1,3},{2,0},{3,1},{4,6},{5,7},{6,4},{7,5},{8,10},{9,11},{10,... | collective-permute-start | bytes 1179656 | tf_op jit(solution)/shard_map/ppermute | solution.py:385
  8.0 19.3 %collective-permute-start.3 = (bf16[2,256,384]{2,1,0:T(8,128)(2,1)S(1)}, bf16[2,256,384]{2,1,0:T(8,128)(2,1)S(1)}, u32[]{:S(2)}, u32[]{:S(2)}) collective-permute-start(bf16[2,256,384]{2,1,0:T(8,128)(2,1)S(1)} %pad_maximum_fusion.2.p0), channel_id=1, source_target_pairs={{0,4},{4,0},{8,12},{12,8},{16,20},{20,16},{24,28},{28,24},{1,5},{5... | collective-permute-start | bytes 1179656 | tf_op jit(solution)/shard_map/ppermute | solution.py:388
  15.2 18.1 %collective-permute-start.5 = (bf16[2,256,384]{2,1,0:T(8,128)(2,1)S(1)}, bf16[2,256,384]{2,1,0:T(8,128)(2,1)S(1)}, u32[]{:S(2)}, u32[]{:S(2)}) collective-permute-start(bf16[2,256,384]{2,1,0:T(8,128)(2,1)S(1)} %collective-permute-done.1.p2), channel_id=1, source_target_pairs={{0,4},{4,0},{8,12},{12,8},{16,20},{20,16},{24,28},{28,24},{1,5},{5... | collective-permute-start | bytes 1179656 | tf_op jit(solution)/shard_map/ppermute | solution.py:388
  17.2 16.1 %collective-permute-start.6 = (bf16[2,256,384]{2,1,0:T(8,128)(2,1)S(1)}, bf16[2,256,384]{2,1,0:T(8,128)(2,1)S(1)}, u32[]{:S(2)}, u32[]{:S(2)}) collective-permute-start(bf16[2,256,384]{2,1,0:T(8,128)(2,1)S(1)} %collective-permute-done.4.p1), channel_id=1, source_target_pairs={{0,2},{1,3},{2,0},{3,1},{4,6},{5,7},{6,4},{7,5},{8,10},{9,11},{10,... | collective-permute-start | bytes 1179656 | tf_op jit(solution)/shard_map/ppermute | solution.py:385
  27.3 9.2 %collective-permute-start.7 = (bf16[3,256,256]{2,1,0:T(8,128)(2,1)S(1)}, bf16[3,256,256]{2,1,0:T(8,128)(2,1)S(1)}, u32[]{:S(2)}, u32[]{:S(2)}) collective-permute-start(bf16[3,256,256]{2,1,0:T(8,128)(2,1)S(1)} %get-tuple-element.70.refs_2_), channel_id=1, source_target_pairs={{0,1},{1,0},{2,3},{3,2},{4,5},{5,4},{6,7},{7,6},{8,9},{9,8},{10,11... | collective-permute-start | bytes 1179656 | tf_op jit(solution)/shard_map/ppermute | solution.py:382
  35.9 9.6 %collective-permute-start.9 = (bf16[3,256,256]{2,1,0:T(8,128)(2,1)S(1)}, bf16[3,256,256]{2,1,0:T(8,128)(2,1)S(1)}, u32[]{:S(2)}, u32[]{:S(2)}) collective-permute-start(bf16[3,256,256]{2,1,0:T(8,128)(2,1)S(1)} %get-tuple-element.75.near), channel_id=1, source_target_pairs={{0,1},{1,0},{2,3},{3,2},{4,5},{5,4},{6,7},{7,6},{8,9},{9,8},{10,11... | collective-permute-start | bytes 1179656 | tf_op jit(solution)/shard_map/ppermute | solution.py:382
  36.4 9.2 %collective-permute-start.10 = (bf16[3,256,256]{2,1,0:T(8,128)(2,1)S(1)}, bf16[3,256,256]{2,1,0:T(8,128)(2,1)S(1)}, u32[]{:S(2)}, u32[]{:S(2)}) collective-permute-start(bf16[3,256,256]{2,1,0:T(8,128)(2,1)S(1)} %get-tuple-element.76.far), channel_id=1, source_target_pairs={{0,1},{1,0},{2,3},{3,2},{4,5},{5,4},{6,7},{7,6},{8,9},{9,8},{10,11... | collective-permute-start | bytes 1179656 | tf_op jit(solution)/shard_map/ppermute | solution.py:382
  38.8 10.6 %collective-permute-start.11 = (bf16[3,64,512]{2,1,0:T(8,128)(2,1)S(1)}, bf16[3,64,512]{2,1,0:T(8,128)(2,1)S(1)}, u32[]{:S(2)}, u32[]{:S(2)}) collective-permute-start(bf16[3,64,512]{2,1,0:T(8,128)(2,1)S(1)} %get-tuple-element.78), channel_id=1, source_target_pairs={{0,8},{4,12},{8,0},{12,4},{16,24},{20,28},{24,16},{28,20},{1,9},{5... | collective-permute-start | bytes 589832 | tf_op jit(solution)/shard_map/ppermute | solution.py:395
  40.4 17.1 %collective-permute-start.12 = (bf16[3,64,512]{2,1,0:T(8,128)(2,1)S(1)}, bf16[3,64,512]{2,1,0:T(8,128)(2,1)S(1)}, u32[]{:S(2)}, u32[]{:S(2)}) collective-permute-start(bf16[3,64,512]{2,1,0:T(8,128)(2,1)S(1)} %get-tuple-element.79), channel_id=1, source_target_pairs={{0,16},{4,20},{8,24},{12,28},{16,0},{20,4},{24,8},{28,12},{1,17},{... | collective-permute-start | bytes 589832 | tf_op jit(solution)/shard_map/ppermute | solution.py:395
  43.0 14.5 %collective-permute-start.13 = (bf16[3,64,512]{2,1,0:T(8,128)(2,1)S(1)}, bf16[3,64,512]{2,1,0:T(8,128)(2,1)S(1)}, u32[]{:S(2)}, u32[]{:S(2)}) collective-permute-start(bf16[3,64,512]{2,1,0:T(8,128)(2,1)S(1)} %get-tuple-element.80), channel_id=1, source_target_pairs={{0,24},{4,28},{8,16},{12,20},{16,8},{20,12},{24,0},{28,4},{1,25},{... | collective-permute-start | bytes 589832 | tf_op jit(solution)/shard_map/ppermute | solution.py:395
  57.8 9.1 %collective-permute-start.16 = (bf16[3,64,512]{2,1,0:T(8,128)(2,1)S(1)}, bf16[3,64,512]{2,1,0:T(8,128)(2,1)S(1)}, u32[]{:S(2)}, u32[]{:S(2)}) collective-permute-start(bf16[3,64,512]{2,1,0:T(8,128)(2,1)S(1)} %shard_map.50.refs_0_), channel_id=1, source_target_pairs={{0,8},{4,12},{8,0},{12,4},{16,24},{20,28},{24,16},{28,20},{1,9},{5... | collective-permute-start | bytes 589832 | tf_op jit(solution)/shard_map/ppermute | solution.py:395
  61.6 13.0 %collective-permute-start.15 = (bf16[3,64,512]{2,1,0:T(8,128)(2,1)S(1)}, bf16[3,64,512]{2,1,0:T(8,128)(2,1)S(1)}, u32[]{:S(2)}, u32[]{:S(2)}) collective-permute-start(bf16[3,64,512]{2,1,0:T(8,128)(2,1)S(1)} %shard_map.50.refs_0_), channel_id=1, source_target_pairs={{0,24},{4,28},{8,16},{12,20},{16,8},{20,12},{24,0},{28,4},{1,25},{... | collective-permute-start | bytes 589832 | tf_op jit(solution)/shard_map/ppermute | solution.py:395
  70.6 9.9 %collective-permute-start.14 = (bf16[3,64,512]{2,1,0:T(8,128)(2,1)S(1)}, bf16[3,64,512]{2,1,0:T(8,128)(2,1)S(1)}, u32[]{:S(2)}, u32[]{:S(2)}) collective-permute-start(bf16[3,64,512]{2,1,0:T(8,128)(2,1)S(1)} %shard_map.50.refs_0_), channel_id=1, source_target_pairs={{0,16},{4,20},{8,24},{12,28},{16,0},{20,4},{24,8},{28,12},{1,17},{... | collective-permute-start | bytes 589832 | tf_op jit(solution)/shard_map/ppermute | solution.py:395
  74.1 8.8 %collective-permute-start.23 = (bf16[3,128,256]{2,1,0:T(8,128)(2,1)S(1)}, bf16[3,128,256]{2,1,0:T(8,128)(2,1)S(1)}, u32[]{:S(2)}, u32[]{:S(2)}) collective-permute-start(bf16[3,128,256]{2,1,0:T(8,128)(2,1)S(1)} %get-tuple-element.84.refs_0_), channel_id=1, source_target_pairs={{0,4},{4,0},{8,12},{12,8},{16,20},{20,16},{24,28},{28,24},{1,5},{5... | collective-permute-start | bytes 589832 | tf_op jit(solution)/shard_map/ppermute | solution.py:388
  74.6 9.3 %collective-permute-start.22 = (bf16[3,128,256]{2,1,0:T(8,128)(2,1)S(1)}, bf16[3,128,256]{2,1,0:T(8,128)(2,1)S(1)}, u32[]{:S(2)}, u32[]{:S(2)}) collective-permute-start(bf16[3,128,256]{2,1,0:T(8,128)(2,1)S(1)} %get-tuple-element.85.refs_4_), channel_id=1, source_target_pairs={{0,2},{1,3},{2,0},{3,1},{4,6},{5,7},{6,4},{7,5},{8,10},{9,11},{10,... | collective-permute-start | bytes 589832 | tf_op jit(solution)/shard_map/ppermute | solution.py:385
  75.5 9.5 %collective-permute-start.24 = (bf16[3,128,256]{2,1,0:T(8,128)(2,1)S(1)}, bf16[3,128,256]{2,1,0:T(8,128)(2,1)S(1)}, u32[]{:S(2)}, u32[]{:S(2)}) collective-permute-start(bf16[3,128,256]{2,1,0:T(8,128)(2,1)S(1)} %collective-permute-done.17.refs_1_), channel_id=1, source_target_pairs={{0,4},{4,0},{8,12},{12,8},{16,20},{20,16},{24,28},{28,24},{1,5},{5... | collective-permute-start | bytes 589832 | tf_op jit(solution)/shard_map/ppermute | solution.py:388
  81.4 13.1 %collective-permute-start.27 = (bf16[3,128,256]{2,1,0:T(8,128)(2,1)S(1)}, bf16[3,128,256]{2,1,0:T(8,128)(2,1)S(1)}, u32[]{:S(2)}, u32[]{:S(2)}) collective-permute-start(bf16[3,128,256]{2,1,0:T(8,128)(2,1)S(1)} %get-tuple-element.86.refs_0_), channel_id=1, source_target_pairs={{0,4},{4,0},{8,12},{12,8},{16,20},{20,16},{24,28},{28,24},{1,5},{5... | collective-permute-start | bytes 589832 | tf_op jit(solution)/shard_map/ppermute | solution.py:388
  83.9 10.6 %collective-permute-start.26 = (bf16[3,128,256]{2,1,0:T(8,128)(2,1)S(1)}, bf16[3,128,256]{2,1,0:T(8,128)(2,1)S(1)}, u32[]{:S(2)}, u32[]{:S(2)}) collective-permute-start(bf16[3,128,256]{2,1,0:T(8,128)(2,1)S(1)} %get-tuple-element.87.refs_4_), channel_id=1, source_target_pairs={{0,2},{1,3},{2,0},{3,1},{4,6},{5,7},{6,4},{7,5},{8,10},{9,11},{10,... | collective-permute-start | bytes 589832 | tf_op jit(solution)/shard_map/ppermute | solution.py:385
  94.5 9.3 %collective-permute-start.29 = (bf16[3,128,512]{2,1,0:T(8,128)(2,1)S(1)}, bf16[3,128,512]{2,1,0:T(8,128)(2,1)S(1)}, u32[]{:S(2)}, u32[]{:S(2)}) collective-permute-start(bf16[3,128,512]{2,1,0:T(8,128)(2,1)S(1)} %get-tuple-element.104.refs_2_), channel_id=1, source_target_pairs={{0,1},{1,0},{2,3},{3,2},{4,5},{5,4},{6,7},{7,6},{8,9},{9,8},{10,11... | collective-permute-start | bytes 1179656 | tf_op jit(solution)/shard_map/ppermute | solution.py:382
  103.3 10.7 %collective-permute-start.31 = (bf16[3,128,512]{2,1,0:T(8,128)(2,1)S(1)}, bf16[3,128,512]{2,1,0:T(8,128)(2,1)S(1)}, u32[]{:S(2)}, u32[]{:S(2)}) collective-permute-start(bf16[3,128,512]{2,1,0:T(8,128)(2,1)S(1)} %get-tuple-element.109.refs_0_), channel_id=1, source_target_pairs={{0,1},{1,0},{2,3},{3,2},{4,5},{5,4},{6,7},{7,6},{8,9},{9,8},{10,11... | collective-permute-start | bytes 1179656 | tf_op jit(solution)/shard_map/ppermute | solution.py:382
  103.8 10.2 %collective-permute-start.32 = (bf16[3,128,512]{2,1,0:T(8,128)(2,1)S(1)}, bf16[3,128,512]{2,1,0:T(8,128)(2,1)S(1)}, u32[]{:S(2)}, u32[]{:S(2)}) collective-permute-start(bf16[3,128,512]{2,1,0:T(8,128)(2,1)S(1)} %get-tuple-element.110.refs_1_), channel_id=1, source_target_pairs={{0,1},{1,0},{2,3},{3,2},{4,5},{5,4},{6,7},{7,6},{8,9},{9,8},{10,11... | collective-permute-start | bytes 1179656 | tf_op jit(solution)/shard_map/ppermute | solution.py:382
  108.3 10.4 %collective-permute-start.33 = (bf16[3,64,512]{2,1,0:T(8,128)(2,1)}, bf16[3,64,512]{2,1,0:T(8,128)(2,1)S(1)}, u32[]{:S(2)}, u32[]{:S(2)}) collective-permute-start(bf16[3,64,512]{2,1,0:T(8,128)(2,1)} %copy-done.2), channel_id=1, source_target_pairs={{0,8},{4,12},{8,0},{12,4},{16,24},{20,28},{24,16},{28,20},{1,9},{5... | collective-permute-start | bytes 589832 | tf_op jit(solution)/shard_map/ppermute | solution.py:395
  108.7 17.4 %collective-permute-start.34 = (bf16[3,64,512]{2,1,0:T(8,128)(2,1)}, bf16[3,64,512]{2,1,0:T(8,128)(2,1)}, u32[]{:S(2)}, u32[]{:S(2)}) collective-permute-start(bf16[3,64,512]{2,1,0:T(8,128)(2,1)} %copy-done.1), channel_id=1, source_target_pairs={{0,16},{4,20},{8,24},{12,28},{16,0},{20,4},{24,8},{28,12},{1,17},{... | collective-permute-start | bytes 589832 | tf_op jit(solution)/shard_map/ppermute | solution.py:395
  110.3 15.8 %collective-permute-start.35 = (bf16[3,64,512]{2,1,0:T(8,128)(2,1)}, bf16[3,64,512]{2,1,0:T(8,128)(2,1)}, u32[]{:S(2)}, u32[]{:S(2)}) collective-permute-start(bf16[3,64,512]{2,1,0:T(8,128)(2,1)} %copy-done), channel_id=1, source_target_pairs={{0,24},{4,28},{8,16},{12,20},{16,8},{20,12},{24,0},{28,4},{1,25},{... | collective-permute-start | bytes 589832 | tf_op jit(solution)/shard_map/ppermute | solution.py:395
  127.4 9.5 %collective-permute-start.36 = (bf16[3,64,512]{2,1,0:T(8,128)(2,1)S(1)}, bf16[3,64,512]{2,1,0:T(8,128)(2,1)S(1)}, u32[]{:S(2)}, u32[]{:S(2)}) collective-permute-start(bf16[3,64,512]{2,1,0:T(8,128)(2,1)S(1)} %shard_map.57.refs_0_), channel_id=1, source_target_pairs={{0,8},{4,12},{8,0},{12,4},{16,24},{20,28},{24,16},{28,20},{1,9},{5... | collective-permute-start | bytes 589832 | tf_op jit(solution)/shard_map/ppermute | solution.py:395
  131.1 11.8 %collective-permute-start.38 = (bf16[3,64,512]{2,1,0:T(8,128)(2,1)S(1)}, bf16[3,64,512]{2,1,0:T(8,128)(2,1)S(1)}, u32[]{:S(2)}, u32[]{:S(2)}) collective-permute-start(bf16[3,64,512]{2,1,0:T(8,128)(2,1)S(1)} %shard_map.57.refs_0_), channel_id=1, source_target_pairs={{0,24},{4,28},{8,16},{12,20},{16,8},{20,12},{24,0},{28,4},{1,25},{... | collective-permute-start | bytes 589832 | tf_op jit(solution)/shard_map/ppermute | solution.py:395
  132.8 16.3 %collective-permute-start.37 = (bf16[3,64,512]{2,1,0:T(8,128)(2,1)S(1)}, bf16[3,64,512]{2,1,0:T(8,128)(2,1)S(1)}, u32[]{:S(2)}, u32[]{:S(2)}) collective-permute-start(bf16[3,64,512]{2,1,0:T(8,128)(2,1)S(1)} %shard_map.57.refs_0_), channel_id=1, source_target_pairs={{0,16},{4,20},{8,24},{12,28},{16,0},{20,4},{24,8},{28,12},{1,17},{... | collective-permute-start | bytes 589832 | tf_op jit(solution)/shard_map/ppermute | solution.py:395
  137.8 12.3 %collective-permute-start.39 = (bf16[3,128,256]{2,1,0:T(8,128)(2,1)S(1)}, bf16[3,128,256]{2,1,0:T(8,128)(2,1)S(1)}, u32[]{:S(2)}, u32[]{:S(2)}) collective-permute-start(bf16[3,128,256]{2,1,0:T(8,128)(2,1)S(1)} %get-tuple-element.116.a0), channel_id=1, source_target_pairs={{0,2},{1,3},{2,0},{3,1},{4,6},{5,7},{6,4},{7,5},{8,10},{9,11},{10,... | collective-permute-start | bytes 589832 | tf_op jit(solution)/shard_map/ppermute | solution.py:385
  138.6 11.4 %collective-permute-start.40 = (bf16[3,128,256]{2,1,0:T(8,128)(2,1)S(1)}, bf16[3,128,256]{2,1,0:T(8,128)(2,1)S(1)}, u32[]{:S(2)}, u32[]{:S(2)}) collective-permute-start(bf16[3,128,256]{2,1,0:T(8,128)(2,1)S(1)} %get-tuple-element.119), channel_id=1, source_target_pairs={{0,4},{4,0},{8,12},{12,8},{16,20},{20,16},{24,28},{28,24},{1,5},{5... | collective-permute-start | bytes 589832 | tf_op jit(solution)/shard_map/ppermute | solution.py:388
  140.3 13.4 %collective-permute-start.41 = (bf16[3,128,256]{2,1,0:T(8,128)(2,1)S(1)}, bf16[3,128,256]{2,1,0:T(8,128)(2,1)S(1)}, u32[]{:S(2)}, u32[]{:S(2)}) collective-permute-start(bf16[3,128,256]{2,1,0:T(8,128)(2,1)S(1)} %get-tuple-element.119), channel_id=1, source_target_pairs={{0,6},{1,7},{2,4},{3,5},{4,2},{5,3},{6,0},{7,1},{8,14},{9,15},{10,... | collective-permute-start | bytes 589832 | tf_op jit(solution)/shard_map/ppermute | solution.py:392
  (24 other events, 209.9 us)

commit v4 on v3

--- a/solution.py
+++ b/solution.py
@@ -365,9 +365,10 @@
     layers, width = norm_gain.shape
     n_rows, n_groups = lax.axis_size("rows"), lax.axis_size("heads")
     all_heads = width // HEAD_DIM
-    row, group = lax.axis_index("rows"), lax.axis_index("heads")
-    core, x_bit = group % 2, group // 2
-    y_bit, z = row % 2, row // 2
+    row = lax.axis_index("rows").astype(jnp.uint32)
+    group = lax.axis_index("heads").astype(jnp.uint32)
+    core, x_bit = group & 1, group >> 1
+    y_bit, z = row & 1, row >> 1
     depth = n_rows // 2
     own = x_bit * 2 + y_bit
     heads = all_heads // 4
@@ -377,6 +378,13 @@
     count = min(depth, PIECES)
     each = depth // count
     place = jnp.stack([x_bit, core, z, z // each, z % each]).astype(jnp.int32)
+    at_mine, at_theirs = core * half, (1 - core) * half
+    at_columns = own * own_width
+    at_rows = [(own ^ d) * own_width for d in (0, 2, 1, 3)]
+    place, at_mine, at_theirs, at_columns, at_rows = lax.optimization_barrier(
+        (place, at_mine, at_theirs, at_columns, at_rows)
+    )
+    zero = jnp.uint32(0)
 
     def over_core(a):
         return lax.ppermute(a, "heads", [(i, i ^ 1) for i in range(n_groups)])
@@ -397,28 +405,28 @@
     def own_columns(layer, at):
         return tuple(
             lax.dynamic_slice(
-                qkv_weight, (layer, 0, which, at * own_width), (1, width, 1, own_width)
+                qkv_weight, (jnp.uint32(layer), zero, jnp.uint32(which), at), (1, width, 1, own_width)
             ).reshape(width, own_width)
             for which in range(qkv_weight.shape[2])
         )
 
-    def out_rows(layer, at):
+    def out_rows(layer, starts):
         parts = [
-            lax.dynamic_slice(out_weight, (layer, (at ^ d) * own_width, 0), (1, own_width, width))[0]
-            for d in (0, 2, 1, 3)
+            lax.dynamic_slice(out_weight, (jnp.uint32(layer), at, zero), (1, own_width, width))[0]
+            for at in starts
         ]
         return jnp.concatenate(parts, axis=0)
 
-    def packed(which):
-        part = lax.dynamic_slice_in_dim(tokens, which * half, half, 1)
+    def packed(at):
+        part = lax.dynamic_slice(tokens, (zero, at, zero), (seqs, half, tokens.shape[2]))
         return jnp.concatenate([part[: seqs // 2], part[seqs // 2 :]], axis=2)
 
-    mine = packed(core)
-    sibling = over_core(packed(1 - core))
+    mine = packed(at_mine)
+    sibling = over_core(packed(at_theirs))
     x_mine, y_mine = over_x(mine), over_y(mine)
     x_sibling, y_sibling = over_x(sibling), over_y(sibling)
     d_mine, d_sibling = over_y(x_mine), over_x(y_sibling)
-    weight = own_columns(0, own)
+    weight = own_columns(0, at_columns)
     streams, queries, keys, values = [], [], [], []
     for pieces in ((mine, sibling, x_mine, x_sibling), (y_mine, y_sibling, d_mine, d_sibling)):
         made = first(place, pieces, weight, heads)
@@ -439,9 +447,9 @@
             value = gather_first(values, other_values)
         else:
             value = gather(place, values, other_values)
-        own_late, kept = lax.optimization_barrier((own, chunks[0]))
-        out_mat = out_rows(layer, own_late)
-        weight = own_columns(layer + 1, own_late) if more else ()
+        columns_late, rows_late, kept = lax.optimization_barrier((at_columns, at_rows, chunks[0]))
+        out_mat = out_rows(layer, rows_late)
+        weight = own_columns(layer + 1, columns_late) if more else ()
         terms[0], out_mat, weight, value = lax.optimization_barrier((kept, out_mat, weight, value))
         weights = softmax_sum(terms)
         gain = norm_gain[layer : layer + 1]

time: 166 us -> 163 us (0.982)
  local copies, waits for them, and re-layouts: 10.6 us -> 6.63 us
  waiting for transfers between devices: 70.7 us -> 72.8 us
    unnamed x22 -> x8, local copies, waits for them, and re-layouts: 3.83 us -> 0.54 us
  transfers between devices with their start and end apart: 47 -> 47, of which waited for: 22 -> 22; matrix products, arithmetic and copies ran while one was open for 4% -> 3% of each run, Pallas kernels for 15% -> 15%
where the time goes in v4:
time: 163 us
  waiting for transfers between devices  72.8 us (45%)
  starting transfers between devices  56.2 us (34%)
  Pallas kernels  26.3 us (16%)
  local copies, waits for them, and re-layouts  6.63 us (4%)
    ppermute x12, waiting for transfers between devices, over_z(): return lax.ppermute(a, 'rows', [(i, i ^ 2 * d) for i in range(n_rows)])  40.8 us
    ppermute x12, starting transfers between devices, over_z(): return lax.ppermute(a, 'rows', [(i, i ^ 2 * d) for i in range(n_rows)])  24.1 us
    ppermute x11, starting transfers between devices, over_y(): return lax.ppermute(a, 'rows', [(i, i ^ 1) for i in range(n_rows)])  14.6 us
    ppermute x11, waiting for transfers between devices, over_x(): return lax.ppermute(a, 'heads', [(i, i ^ 2) for i in range(n_groups)])  14 us
    ppermute x11, starting transfers between devices, over_x(): return lax.ppermute(a, 'heads', [(i, i ^ 2) for i in range(n_groups)])  13.5 us
    ppermute x11, waiting for transfers between devices, over_y(): return lax.ppermute(a, 'rows', [(i, i ^ 1) for i in range(n_rows)])  12.1 us
    pallas_call x2, Pallas kernels, next_layer(): pl.pallas_call(functools.partial(next_kernel, g), in_specs=[SMEM] + [FULL...  8.2 us
    pallas_call x2, Pallas kernels, first(): pl.pallas_call(first_kernel, in_specs=[SMEM] + [FULL] * 7, out_specs=[FUL...  4.91 us
  transfers between devices with their start and end apart: 47, of which 22 were waited for; matrix products, arithmetic and copies ran while one was open for 3% of the time, Pallas kernels for 15%

profile of v4, /device:TPU:0, one launch (start us, length us, event | category | flops | bytes accessed | tf_op | source)
XLA Modules:
  0.0 162.7 jit_solution(11453788132586544735)
XLA Ops:
  3.1 2.5 %collective-permute-start.1 = (bf16[2,256,384]{2,1,0:T(8,128)(2,1)S(1)}, bf16[2,256,384]{2,1,0:T(8,128)(2,1)S(1)}, u32[]{:S(2)}, u32[]{:S(2)}) collective-permute-start(bf16[2,256,384]{2,1,0:T(8,128)(2,1)S(1)} %pad_maximum_fusion.2.p0), channel_id=1, source_target_pairs={{0,2},{1,3},{2,0},{3,1},{4,6},{5,7},{6,4},{7,5},{8,10},{9,11},{10,... | collective-permute-start | bytes 1179656 | tf_op jit(solution)/shard_map/ppermute | solution.py:393
  8.8 6.7 %collective-permute-done.1.p2 = bf16[2,256,384]{2,1,0:T(8,128)(2,1)S(1)} collective-permute-done((bf16[2,256,384]{2,1,0:T(8,128)(2,1)S(1)}, bf16[2,256,384]{2,1,0:T(8,128)(2,1)S(1)}, u32[]{:S(2)}, u32[]{:S(2)}) %collective-permute-start.1) | collective-permute-done | bytes 393248 | tf_op jit(solution)/shard_map/ppermute | solution.py:393
  15.6 2.0 %collective-permute-start.5 = (bf16[2,256,384]{2,1,0:T(8,128)(2,1)S(1)}, bf16[2,256,384]{2,1,0:T(8,128)(2,1)S(1)}, u32[]{:S(2)}, u32[]{:S(2)}) collective-permute-start(bf16[2,256,384]{2,1,0:T(8,128)(2,1)S(1)} %collective-permute-done.1.p2), channel_id=1, source_target_pairs={{0,4},{4,0},{8,12},{12,8},{16,20},{20,16},{24,28},{28,24},{1,5},{5... | collective-permute-start | bytes 1179656 | tf_op jit(solution)/shard_map/ppermute | solution.py:396
  19.0 2.0 %dynamic-slice_bitcast_fusion.3 = (bf16[768,192]{1,0:T(8,128)(2,1)S(1)}, bf16[768,192]{1,0:T(8,128)(2,1)S(1)}, bf16[768,192]{1,0:T(8,128)(2,1)S(1)}) fusion(bf16[2,768,3,768]{3,1,2,0:T(8,128)(2,1)} %param.5, u32[]{:T(128)S(6)} %mul.25), kind=kLoop, calls=%fused_computation.7 | loop fusion | bytes 1769476 | tf_op jit(solution)/shard_map/reshape | solution.py:409
  21.0 3.0 %collective-permute-done.2.p3 = bf16[2,256,384]{2,1,0:T(8,128)(2,1)S(1)} collective-permute-done((bf16[2,256,384]{2,1,0:T(8,128)(2,1)S(1)}, bf16[2,256,384]{2,1,0:T(8,128)(2,1)S(1)}, u32[]{:S(2)}, u32[]{:S(2)}) %collective-permute-start.2) | collective-permute-done | bytes 393248 | tf_op jit(solution)/shard_map/ppermute | solution.py:393
  24.0 2.5 %shard_map.46 = (bf16[4,256,768]{2,1,0:T(8,128)(2,1)S(1)}, bf16[3,256,256]{2,1,0:T(8,128)(2,1)S(1)}, bf16[3,256,256]{2,1,0:T(8,128)(2,1)S(1)}, bf16[3,256,256]{2,1,0:T(8,128)(2,1)S(1)}) custom-call(s32[5]{0:T(128)S(1)} %convert_element_type.15.place, bf16[2,256,384]{2,1,0:T(8,128)(2,1)S(1)} %pad_maximum_fusion.2.p0, ...), custom_call_target="tpu_custom_call" | custom-call | flops 905969664 | bytes 9830400 | tf_op jit(solution)/shard_map/pallas_call | solution.py:81
  26.5 7.1 %collective-permute-done.5.p2 = bf16[2,256,384]{2,1,0:T(8,128)(2,1)S(1)} collective-permute-done((bf16[2,256,384]{2,1,0:T(8,128)(2,1)S(1)}, bf16[2,256,384]{2,1,0:T(8,128)(2,1)S(1)}, u32[]{:S(2)}, u32[]{:S(2)}) %collective-permute-start.5) | collective-permute-done | bytes 393248 | tf_op jit(solution)/shard_map/ppermute | solution.py:396
  33.7 2.4 %shard_map.47 = (bf16[4,256,768]{2,1,0:T(8,128)(2,1)S(1)}, bf16[3,256,256]{2,1,0:T(8,128)(2,1)S(1)}, bf16[3,256,256]{2,1,0:T(8,128)(2,1)S(1)}, bf16[3,256,256]{2,1,0:T(8,128)(2,1)S(1)}) custom-call(s32[5]{0:T(128)S(1)} %convert_element_type.15.place, bf16[2,256,384]{2,1,0:T(8,128)(2,1)S(1)} %collective-permute-done.3.p0, ...), custom_call_target="tpu_custom_call" | custom-call | flops 905969664 | bytes 9830400 | tf_op jit(solution)/shard_map/pallas_call | solution.py:81
  40.7 2.6 %collective-permute-start.12 = (bf16[3,64,512]{2,1,0:T(8,128)(2,1)S(1)}, bf16[3,64,512]{2,1,0:T(8,128)(2,1)S(1)}, u32[]{:S(2)}, u32[]{:S(2)}) collective-permute-start(bf16[3,64,512]{2,1,0:T(8,128)(2,1)S(1)} %get-tuple-element.106), channel_id=1, source_target_pairs={{0,16},{4,20},{8,24},{12,28},{16,0},{20,4},{24,8},{28,12},{1,17},{... | collective-permute-start | bytes 589832 | tf_op jit(solution)/shard_map/ppermute | solution.py:403
  43.6 2.0 %dynamic-slice_bitcast_fusion = (bf16[768,192]{1,0:T(8,128)(2,1)S(1)}, bf16[768,192]{1,0:T(8,128)(2,1)S(1)}, bf16[768,192]{1,0:T(8,128)(2,1)S(1)}) fusion(bf16[2,768,3,768]{3,1,2,0:T(8,128)(2,1)} %param.5, u32[]{:T(128)S(6)} %mul.25), kind=kLoop, calls=%fused_computation.4 | loop fusion | bytes 1769476 | tf_op jit(solution)/shard_map/reshape | solution.py:409
  46.2 3.5 %collective-permute-done.11.refs_1_ = bf16[3,64,512]{2,1,0:T(8,128)(2,1)S(1)} collective-permute-done((bf16[3,64,512]{2,1,0:T(8,128)(2,1)S(1)}, bf16[3,64,512]{2,1,0:T(8,128)(2,1)S(1)}, u32[]{:S(2)}, u32[]{:S(2)}) %collective-permute-start.11) | collective-permute-done | bytes 196640 | tf_op jit(solution)/shard_map/ppermute | solution.py:403
  49.7 8.1 %collective-permute-done.12.refs_2_ = bf16[3,64,512]{2,1,0:T(8,128)(2,1)S(1)} collective-permute-done((bf16[3,64,512]{2,1,0:T(8,128)(2,1)S(1)}, bf16[3,64,512]{2,1,0:T(8,128)(2,1)S(1)}, u32[]{:S(2)}, u32[]{:S(2)}) %collective-permute-start.12) | collective-permute-done | bytes 196640 | tf_op jit(solution)/shard_map/ppermute | solution.py:403
  58.1 3.8 %collective-permute-start.16 = (bf16[3,64,512]{2,1,0:T(8,128)(2,1)S(1)}, bf16[3,64,512]{2,1,0:T(8,128)(2,1)S(1)}, u32[]{:S(2)}, u32[]{:S(2)}) collective-permute-start(bf16[3,64,512]{2,1,0:T(8,128)(2,1)S(1)} %shard_map.50.refs_0_), channel_id=1, source_target_pairs={{0,8},{4,12},{8,0},{12,4},{16,24},{20,28},{24,16},{28,20},{1,9},{5... | collective-permute-start | bytes 589832 | tf_op jit(solution)/shard_map/ppermute | solution.py:403
  61.9 2.5 %collective-permute-start.15 = (bf16[3,64,512]{2,1,0:T(8,128)(2,1)S(1)}, bf16[3,64,512]{2,1,0:T(8,128)(2,1)S(1)}, u32[]{:S(2)}, u32[]{:S(2)}) collective-permute-start(bf16[3,64,512]{2,1,0:T(8,128)(2,1)S(1)} %shard_map.50.refs_0_), channel_id=1, source_target_pairs={{0,24},{4,28},{8,16},{12,20},{16,8},{20,12},{24,0},{28,4},{1,25},{... | collective-permute-start | bytes 589832 | tf_op jit(solution)/shard_map/ppermute | solution.py:403
  64.4 2.9 %collective-permute-done.16.refs_1_ = bf16[3,64,512]{2,1,0:T(8,128)(2,1)S(1)} collective-permute-done((bf16[3,64,512]{2,1,0:T(8,128)(2,1)S(1)}, bf16[3,64,512]{2,1,0:T(8,128)(2,1)S(1)}, u32[]{:S(2)}, u32[]{:S(2)}) %collective-permute-start.16) | collective-permute-done | bytes 196640 | tf_op jit(solution)/shard_map/ppermute | solution.py:403
  70.9 3.5 %collective-permute-start.14 = (bf16[3,64,512]{2,1,0:T(8,128)(2,1)S(1)}, bf16[3,64,512]{2,1,0:T(8,128)(2,1)S(1)}, u32[]{:S(2)}, u32[]{:S(2)}) collective-permute-start(bf16[3,64,512]{2,1,0:T(8,128)(2,1)S(1)} %shard_map.50.refs_0_), channel_id=1, source_target_pairs={{0,16},{4,20},{8,24},{12,28},{16,0},{20,4},{24,8},{28,12},{1,17},{... | collective-permute-start | bytes 589832 | tf_op jit(solution)/shard_map/ppermute | solution.py:403
  78.4 2.4 %collective-permute-done.14.refs_0_ = bf16[3,64,512]{2,1,0:T(8,128)(2,1)S(1)} collective-permute-done((bf16[3,64,512]{2,1,0:T(8,128)(2,1)S(1)}, bf16[3,64,512]{2,1,0:T(8,128)(2,1)S(1)}, u32[]{:S(2)}, u32[]{:S(2)}) %collective-permute-start.14) | collective-permute-done | bytes 196640 | tf_op jit(solution)/shard_map/ppermute | solution.py:403
  85.9 4.2 %shard_map.53 = (bf16[4,128,768]{2,1,0:T(8,128)(2,1)S(1)}, bf16[3,128,512]{2,1,0:T(8,128)(2,1)S(1)}, bf16[3,128,512]{2,1,0:T(8,128)(2,1)S(1)}, bf16[3,128,512]{2,1,0:T(8,128)(2,1)S(1)}) custom-call(s32[5]{0:T(128)S(1)} %convert_element_type.15.place, bf16[3,128,256]{2,1,0:T(8,128)(2,1)S(1)} %get-tuple-element.111.refs_0_, ...), custom_call_target="tpu_custom_call" | custom-call | flops 2113929216 | bytes 5210112 | tf_op jit(solution)/shard_map/pallas_call | solution.py:302
  92.0 1.7 %collective-permute-start.28 = (bf16[3,128,256]{2,1,0:T(8,128)(2,1)S(1)}, bf16[3,128,256]{2,1,0:T(8,128)(2,1)S(1)}, u32[]{:S(2)}, u32[]{:S(2)}) collective-permute-start(bf16[3,128,256]{2,1,0:T(8,128)(2,1)S(1)} %collective-permute-done.19.refs_1_), channel_id=1, source_target_pairs={{0,4},{4,0},{8,12},{12,8},{16,20},{20,16},{24,28},{28,24},{1,5},{5... | collective-permute-start | bytes 589832 | tf_op jit(solution)/shard_map/ppermute | solution.py:396
  94.9 2.8 %collective-permute-done.28.refs_7_ = bf16[3,128,256]{2,1,0:T(8,128)(2,1)S(1)} collective-permute-done((bf16[3,128,256]{2,1,0:T(8,128)(2,1)S(1)}, bf16[3,128,256]{2,1,0:T(8,128)(2,1)S(1)}, u32[]{:S(2)}, u32[]{:S(2)}) %collective-permute-start.28) | collective-permute-done | bytes 196640 | tf_op jit(solution)/shard_map/ppermute | solution.py:396
  97.7 1.7 %collective-permute-done.25.refs_3_ = bf16[3,128,256]{2,1,0:T(8,128)(2,1)S(1)} collective-permute-done((bf16[3,128,256]{2,1,0:T(8,128)(2,1)S(1)}, bf16[3,128,256]{2,1,0:T(8,128)(2,1)S(1)}, u32[]{:S(2)}, u32[]{:S(2)}) %collective-permute-start.25) | collective-permute-done | bytes 196640 | tf_op jit(solution)/shard_map/ppermute | solution.py:393
  99.4 4.0 %shard_map.54 = (bf16[4,128,768]{2,1,0:T(8,128)(2,1)S(1)}, bf16[3,128,512]{2,1,0:T(8,128)(2,1)S(1)}, bf16[3,128,512]{2,1,0:T(8,128)(2,1)S(1)}, bf16[3,128,512]{2,1,0:T(8,128)(2,1)S(1)}) custom-call(s32[5]{0:T(128)S(1)} %convert_element_type.15.place, bf16[3,128,256]{2,1,0:T(8,128)(2,1)S(1)} %get-tuple-element.113.refs_0_, ...), custom_call_target="tpu_custom_call" | custom-call | flops 2113929216 | bytes 5210112 | tf_op jit(solution)/shard_map/pallas_call | solution.py:302
  108.5 2.4 %collective-permute-start.35 = (bf16[3,64,512]{2,1,0:T(8,128)(2,1)S(1)}, bf16[3,64,512]{2,1,0:T(8,128)(2,1)S(1)}, u32[]{:S(2)}, u32[]{:S(2)}) collective-permute-start(bf16[3,64,512]{2,1,0:T(8,128)(2,1)S(1)} %get-tuple-element.144), channel_id=1, source_target_pairs={{0,24},{4,28},{8,16},{12,20},{16,8},{20,12},{24,0},{28,4},{1,25},{... | collective-permute-start | bytes 589832 | tf_op jit(solution)/shard_map/ppermute | solution.py:403
  112.0 4.7 %collective-permute-done.33.refs_1_ = bf16[3,64,512]{2,1,0:T(8,128)(2,1)S(1)} collective-permute-done((bf16[3,64,512]{2,1,0:T(8,128)(2,1)S(1)}, bf16[3,64,512]{2,1,0:T(8,128)(2,1)S(1)}, u32[]{:S(2)}, u32[]{:S(2)}) %collective-permute-start.33) | collective-permute-done | bytes 196640 | tf_op jit(solution)/shard_map/ppermute | solution.py:403
  116.7 7.3 %collective-permute-done.34.refs_2_ = bf16[3,64,512]{2,1,0:T(8,128)(2,1)S(1)} collective-permute-done((bf16[3,64,512]{2,1,0:T(8,128)(2,1)S(1)}, bf16[3,64,512]{2,1,0:T(8,128)(2,1)S(1)}, u32[]{:S(2)}, u32[]{:S(2)}) %collective-permute-start.34) | collective-permute-done | bytes 196640 | tf_op jit(solution)/shard_map/ppermute | solution.py:403
  124.3 3.8 %collective-permute-start.36 = (bf16[3,64,512]{2,1,0:T(8,128)(2,1)S(1)}, bf16[3,64,512]{2,1,0:T(8,128)(2,1)S(1)}, u32[]{:S(2)}, u32[]{:S(2)}) collective-permute-start(bf16[3,64,512]{2,1,0:T(8,128)(2,1)S(1)} %shard_map.57.refs_0_), channel_id=1, source_target_pairs={{0,8},{4,12},{8,0},{12,4},{16,24},{20,28},{24,16},{28,20},{1,9},{5... | collective-permute-start | bytes 589832 | tf_op jit(solution)/shard_map/ppermute | solution.py:403
  128.1 1.7 %collective-permute-start.38 = (bf16[3,64,512]{2,1,0:T(8,128)(2,1)S(1)}, bf16[3,64,512]{2,1,0:T(8,128)(2,1)S(1)}, u32[]{:S(2)}, u32[]{:S(2)}) collective-permute-start(bf16[3,64,512]{2,1,0:T(8,128)(2,1)S(1)} %shard_map.57.refs_0_), channel_id=1, source_target_pairs={{0,24},{4,28},{8,16},{12,20},{16,8},{20,12},{24,0},{28,4},{1,25},{... | collective-permute-start | bytes 589832 | tf_op jit(solution)/shard_map/ppermute | solution.py:403
  129.7 4.3 %collective-permute-done.36.refs_1_ = bf16[3,64,512]{2,1,0:T(8,128)(2,1)S(1)} collective-permute-done((bf16[3,64,512]{2,1,0:T(8,128)(2,1)S(1)}, bf16[3,64,512]{2,1,0:T(8,128)(2,1)S(1)}, u32[]{:S(2)}, u32[]{:S(2)}) %collective-permute-start.36) | collective-permute-done | bytes 196640 | tf_op jit(solution)/shard_map/ppermute | solution.py:403
  139.9 6.2 %collective-permute-done.37.refs_0_ = bf16[3,64,512]{2,1,0:T(8,128)(2,1)S(1)} collective-permute-done((bf16[3,64,512]{2,1,0:T(8,128)(2,1)S(1)}, bf16[3,64,512]{2,1,0:T(8,128)(2,1)S(1)}, u32[]{:S(2)}, u32[]{:S(2)}) %collective-permute-start.37) | collective-permute-done | bytes 196640 | tf_op jit(solution)/shard_map/ppermute | solution.py:403
  150.6 2.1 %shard_map.60 = (bf16[2,2,192,128]{3,2,1,0:T(8,128)(2,1)S(1)}, bf16[2,2,192,128]{3,2,1,0:T(8,128)(2,1)S(1)}) custom-call(s32[5]{0:T(128)S(1)} %convert_element_type.15.place, bf16[3,128,256]{2,1,0:T(8,128)(2,1)S(1)} %get-tuple-element.146.a0, bf16[3,128,256]{2,1,0:T(8,128)(2,1)S(1)} %collective-permute-done.39.a1, ...), custom_call_target="tpu_custom_call" | custom-call | flops 603979776 | bytes 3538944 | tf_op jit(solution)/shard_map/pallas_call | solution.py:330
  154.3 2.1 %collective-permute-done.44.a3 = bf16[3,128,256]{2,1,0:T(8,128)(2,1)S(1)} collective-permute-done((bf16[3,128,256]{2,1,0:T(8,128)(2,1)S(1)}, bf16[3,128,256]{2,1,0:T(8,128)(2,1)S(1)}, u32[]{:S(2)}, u32[]{:S(2)}) %collective-permute-start.44) | collective-permute-done | bytes 196640 | tf_op jit(solution)/shard_map/ppermute | solution.py:400
  157.6 2.1 %shard_map.61 = (bf16[2,2,192,128]{3,2,1,0:T(8,128)(2,1)S(1)}, bf16[2,2,192,128]{3,2,1,0:T(8,128)(2,1)S(1)}) custom-call(s32[5]{0:T(128)S(1)} %convert_element_type.15.place, bf16[3,128,256]{2,1,0:T(8,128)(2,1)S(1)} %get-tuple-element.155.a0, bf16[3,128,256]{2,1,0:T(8,128)(2,1)S(1)} %collective-permute-done.42.a1, ...), custom_call_target="tpu_custom_call" | custom-call | flops 603979776 | bytes 3538944 | tf_op jit(solution)/shard_map/pallas_call | solution.py:330
  (99 shorter events, 51.9 us)
Async XLA Ops:
  3.1 12.5 %collective-permute-start.1 = (bf16[2,256,384]{2,1,0:T(8,128)(2,1)S(1)}, bf16[2,256,384]{2,1,0:T(8,128)(2,1)S(1)}, u32[]{:S(2)}, u32[]{:S(2)}) collective-permute-start(bf16[2,256,384]{2,1,0:T(8,128)(2,1)S(1)} %pad_maximum_fusion.2.p0), channel_id=1, source_target_pairs={{0,2},{1,3},{2,0},{3,1},{4,6},{5,7},{6,4},{7,5},{8,10},{9,11},{10,... | collective-permute-start | bytes 1179656 | tf_op jit(solution)/shard_map/ppermute | solution.py:393
  5.6 11.9 %collective-permute-start.4 = (bf16[2,256,384]{2,1,0:T(8,128)(2,1)S(1)}, bf16[2,256,384]{2,1,0:T(8,128)(2,1)S(1)}, u32[]{:S(2)}, u32[]{:S(2)}) collective-permute-start(bf16[2,256,384]{2,1,0:T(8,128)(2,1)S(1)} %collective-permute-done.p1), channel_id=1, source_target_pairs={{0,4},{4,0},{8,12},{12,8},{16,20},{20,16},{24,28},{28,24},{1,5},{5... | collective-permute-start | bytes 1179656 | tf_op jit(solution)/shard_map/ppermute | solution.py:396
  7.1 16.9 %collective-permute-start.2 = (bf16[2,256,384]{2,1,0:T(8,128)(2,1)S(1)}, bf16[2,256,384]{2,1,0:T(8,128)(2,1)S(1)}, u32[]{:S(2)}, u32[]{:S(2)}) collective-permute-start(bf16[2,256,384]{2,1,0:T(8,128)(2,1)S(1)} %collective-permute-done.p1), channel_id=1, source_target_pairs={{0,2},{1,3},{2,0},{3,1},{4,6},{5,7},{6,4},{7,5},{8,10},{9,11},{10,... | collective-permute-start | bytes 1179656 | tf_op jit(solution)/shard_map/ppermute | solution.py:393
  8.3 18.2 %collective-permute-start.3 = (bf16[2,256,384]{2,1,0:T(8,128)(2,1)S(1)}, bf16[2,256,384]{2,1,0:T(8,128)(2,1)S(1)}, u32[]{:S(2)}, u32[]{:S(2)}) collective-permute-start(bf16[2,256,384]{2,1,0:T(8,128)(2,1)S(1)} %pad_maximum_fusion.2.p0), channel_id=1, source_target_pairs={{0,4},{4,0},{8,12},{12,8},{16,20},{20,16},{24,28},{28,24},{1,5},{5... | collective-permute-start | bytes 1179656 | tf_op jit(solution)/shard_map/ppermute | solution.py:396
  15.6 18.1 %collective-permute-start.5 = (bf16[2,256,384]{2,1,0:T(8,128)(2,1)S(1)}, bf16[2,256,384]{2,1,0:T(8,128)(2,1)S(1)}, u32[]{:S(2)}, u32[]{:S(2)}) collective-permute-start(bf16[2,256,384]{2,1,0:T(8,128)(2,1)S(1)} %collective-permute-done.1.p2), channel_id=1, source_target_pairs={{0,4},{4,0},{8,12},{12,8},{16,20},{20,16},{24,28},{28,24},{1,5},{5... | collective-permute-start | bytes 1179656 | tf_op jit(solution)/shard_map/ppermute | solution.py:396
  17.5 16.1 %collective-permute-start.6 = (bf16[2,256,384]{2,1,0:T(8,128)(2,1)S(1)}, bf16[2,256,384]{2,1,0:T(8,128)(2,1)S(1)}, u32[]{:S(2)}, u32[]{:S(2)}) collective-permute-start(bf16[2,256,384]{2,1,0:T(8,128)(2,1)S(1)} %collective-permute-done.4.p1), channel_id=1, source_target_pairs={{0,2},{1,3},{2,0},{3,1},{4,6},{5,7},{6,4},{7,5},{8,10},{9,11},{10,... | collective-permute-start | bytes 1179656 | tf_op jit(solution)/shard_map/ppermute | solution.py:393
  26.4 10.3 %collective-permute-start.7 = (bf16[3,256,256]{2,1,0:T(8,128)(2,1)S(1)}, bf16[3,256,256]{2,1,0:T(8,128)(2,1)S(1)}, u32[]{:S(2)}, u32[]{:S(2)}) collective-permute-start(bf16[3,256,256]{2,1,0:T(8,128)(2,1)S(1)} %get-tuple-element.93.refs_2_), channel_id=1, source_target_pairs={{0,1},{1,0},{2,3},{3,2},{4,5},{5,4},{6,7},{7,6},{8,9},{9,8},{10,11... | collective-permute-start | bytes 1179656 | tf_op jit(solution)/shard_map/ppermute | solution.py:390
  36.2 9.6 %collective-permute-start.9 = (bf16[3,256,256]{2,1,0:T(8,128)(2,1)S(1)}, bf16[3,256,256]{2,1,0:T(8,128)(2,1)S(1)}, u32[]{:S(2)}, u32[]{:S(2)}) collective-permute-start(bf16[3,256,256]{2,1,0:T(8,128)(2,1)S(1)} %get-tuple-element.102.near), channel_id=1, source_target_pairs={{0,1},{1,0},{2,3},{3,2},{4,5},{5,4},{6,7},{7,6},{8,9},{9,8},{10,11... | collective-permute-start | bytes 1179656 | tf_op jit(solution)/shard_map/ppermute | solution.py:390
  36.7 9.1 %collective-permute-start.10 = (bf16[3,256,256]{2,1,0:T(8,128)(2,1)S(1)}, bf16[3,256,256]{2,1,0:T(8,128)(2,1)S(1)}, u32[]{:S(2)}, u32[]{:S(2)}) collective-permute-start(bf16[3,256,256]{2,1,0:T(8,128)(2,1)S(1)} %get-tuple-element.103.far), channel_id=1, source_target_pairs={{0,1},{1,0},{2,3},{3,2},{4,5},{5,4},{6,7},{7,6},{8,9},{9,8},{10,11... | collective-permute-start | bytes 1179656 | tf_op jit(solution)/shard_map/ppermute | solution.py:390
  39.1 10.6 %collective-permute-start.11 = (bf16[3,64,512]{2,1,0:T(8,128)(2,1)S(1)}, bf16[3,64,512]{2,1,0:T(8,128)(2,1)S(1)}, u32[]{:S(2)}, u32[]{:S(2)}) collective-permute-start(bf16[3,64,512]{2,1,0:T(8,128)(2,1)S(1)} %get-tuple-element.105), channel_id=1, source_target_pairs={{0,8},{4,12},{8,0},{12,4},{16,24},{20,28},{24,16},{28,20},{1,9},{5... | collective-permute-start | bytes 589832 | tf_op jit(solution)/shard_map/ppermute | solution.py:403
  40.7 17.1 %collective-permute-start.12 = (bf16[3,64,512]{2,1,0:T(8,128)(2,1)S(1)}, bf16[3,64,512]{2,1,0:T(8,128)(2,1)S(1)}, u32[]{:S(2)}, u32[]{:S(2)}) collective-permute-start(bf16[3,64,512]{2,1,0:T(8,128)(2,1)S(1)} %get-tuple-element.106), channel_id=1, source_target_pairs={{0,16},{4,20},{8,24},{12,28},{16,0},{20,4},{24,8},{28,12},{1,17},{... | collective-permute-start | bytes 589832 | tf_op jit(solution)/shard_map/ppermute | solution.py:403
  43.3 14.5 %collective-permute-start.13 = (bf16[3,64,512]{2,1,0:T(8,128)(2,1)S(1)}, bf16[3,64,512]{2,1,0:T(8,128)(2,1)S(1)}, u32[]{:S(2)}, u32[]{:S(2)}) collective-permute-start(bf16[3,64,512]{2,1,0:T(8,128)(2,1)S(1)} %get-tuple-element.107), channel_id=1, source_target_pairs={{0,24},{4,28},{8,16},{12,20},{16,8},{20,12},{24,0},{28,4},{1,25},{... | collective-permute-start | bytes 589832 | tf_op jit(solution)/shard_map/ppermute | solution.py:403
  58.1 9.1 %collective-permute-start.16 = (bf16[3,64,512]{2,1,0:T(8,128)(2,1)S(1)}, bf16[3,64,512]{2,1,0:T(8,128)(2,1)S(1)}, u32[]{:S(2)}, u32[]{:S(2)}) collective-permute-start(bf16[3,64,512]{2,1,0:T(8,128)(2,1)S(1)} %shard_map.50.refs_0_), channel_id=1, source_target_pairs={{0,8},{4,12},{8,0},{12,4},{16,24},{20,28},{24,16},{28,20},{1,9},{5... | collective-permute-start | bytes 589832 | tf_op jit(solution)/shard_map/ppermute | solution.py:403
  61.9 13.0 %collective-permute-start.15 = (bf16[3,64,512]{2,1,0:T(8,128)(2,1)S(1)}, bf16[3,64,512]{2,1,0:T(8,128)(2,1)S(1)}, u32[]{:S(2)}, u32[]{:S(2)}) collective-permute-start(bf16[3,64,512]{2,1,0:T(8,128)(2,1)S(1)} %shard_map.50.refs_0_), channel_id=1, source_target_pairs={{0,24},{4,28},{8,16},{12,20},{16,8},{20,12},{24,0},{28,4},{1,25},{... | collective-permute-start | bytes 589832 | tf_op jit(solution)/shard_map/ppermute | solution.py:403
  70.9 9.9 %collective-permute-start.14 = (bf16[3,64,512]{2,1,0:T(8,128)(2,1)S(1)}, bf16[3,64,512]{2,1,0:T(8,128)(2,1)S(1)}, u32[]{:S(2)}, u32[]{:S(2)}) collective-permute-start(bf16[3,64,512]{2,1,0:T(8,128)(2,1)S(1)} %shard_map.50.refs_0_), channel_id=1, source_target_pairs={{0,16},{4,20},{8,24},{12,28},{16,0},{20,4},{24,8},{28,12},{1,17},{... | collective-permute-start | bytes 589832 | tf_op jit(solution)/shard_map/ppermute | solution.py:403
  74.4 8.8 %collective-permute-start.23 = (bf16[3,128,256]{2,1,0:T(8,128)(2,1)S(1)}, bf16[3,128,256]{2,1,0:T(8,128)(2,1)S(1)}, u32[]{:S(2)}, u32[]{:S(2)}) collective-permute-start(bf16[3,128,256]{2,1,0:T(8,128)(2,1)S(1)} %get-tuple-element.111.refs_0_), channel_id=1, source_target_pairs={{0,4},{4,0},{8,12},{12,8},{16,20},{20,16},{24,28},{28,24},{1,5},{5... | collective-permute-start | bytes 589832 | tf_op jit(solution)/shard_map/ppermute | solution.py:396
  74.9 9.3 %collective-permute-start.22 = (bf16[3,128,256]{2,1,0:T(8,128)(2,1)S(1)}, bf16[3,128,256]{2,1,0:T(8,128)(2,1)S(1)}, u32[]{:S(2)}, u32[]{:S(2)}) collective-permute-start(bf16[3,128,256]{2,1,0:T(8,128)(2,1)S(1)} %get-tuple-element.112.refs_4_), channel_id=1, source_target_pairs={{0,2},{1,3},{2,0},{3,1},{4,6},{5,7},{6,4},{7,5},{8,10},{9,11},{10,... | collective-permute-start | bytes 589832 | tf_op jit(solution)/shard_map/ppermute | solution.py:393
  75.8 9.5 %collective-permute-start.24 = (bf16[3,128,256]{2,1,0:T(8,128)(2,1)S(1)}, bf16[3,128,256]{2,1,0:T(8,128)(2,1)S(1)}, u32[]{:S(2)}, u32[]{:S(2)}) collective-permute-start(bf16[3,128,256]{2,1,0:T(8,128)(2,1)S(1)} %collective-permute-done.17.refs_1_), channel_id=1, source_target_pairs={{0,4},{4,0},{8,12},{12,8},{16,20},{20,16},{24,28},{28,24},{1,5},{5... | collective-permute-start | bytes 589832 | tf_op jit(solution)/shard_map/ppermute | solution.py:396
  77.3 8.6 %collective-permute-start.21 = (bf16[3,128,256]{2,1,0:T(8,128)(2,1)S(1)}, bf16[3,128,256]{2,1,0:T(8,128)(2,1)S(1)}, u32[]{:S(2)}, u32[]{:S(2)}) collective-permute-start(bf16[3,128,256]{2,1,0:T(8,128)(2,1)S(1)} %collective-permute-done.18.refs_2_), channel_id=1, source_target_pairs={{0,2},{1,3},{2,0},{3,1},{4,6},{5,7},{6,4},{7,5},{8,10},{9,11},{10,... | collective-permute-start | bytes 589832 | tf_op jit(solution)/shard_map/ppermute | solution.py:393
  81.7 13.1 %collective-permute-start.27 = (bf16[3,128,256]{2,1,0:T(8,128)(2,1)S(1)}, bf16[3,128,256]{2,1,0:T(8,128)(2,1)S(1)}, u32[]{:S(2)}, u32[]{:S(2)}) collective-permute-start(bf16[3,128,256]{2,1,0:T(8,128)(2,1)S(1)} %get-tuple-element.113.refs_0_), channel_id=1, source_target_pairs={{0,4},{4,0},{8,12},{12,8},{16,20},{20,16},{24,28},{28,24},{1,5},{5... | collective-permute-start | bytes 589832 | tf_op jit(solution)/shard_map/ppermute | solution.py:396
  84.2 10.7 %collective-permute-start.26 = (bf16[3,128,256]{2,1,0:T(8,128)(2,1)S(1)}, bf16[3,128,256]{2,1,0:T(8,128)(2,1)S(1)}, u32[]{:S(2)}, u32[]{:S(2)}) collective-permute-start(bf16[3,128,256]{2,1,0:T(8,128)(2,1)S(1)} %get-tuple-element.114.refs_4_), channel_id=1, source_target_pairs={{0,2},{1,3},{2,0},{3,1},{4,6},{5,7},{6,4},{7,5},{8,10},{9,11},{10,... | collective-permute-start | bytes 589832 | tf_op jit(solution)/shard_map/ppermute | solution.py:393
  94.9 9.2 %collective-permute-start.29 = (bf16[3,128,512]{2,1,0:T(8,128)(2,1)S(1)}, bf16[3,128,512]{2,1,0:T(8,128)(2,1)S(1)}, u32[]{:S(2)}, u32[]{:S(2)}) collective-permute-start(bf16[3,128,512]{2,1,0:T(8,128)(2,1)S(1)} %get-tuple-element.131.refs_2_), channel_id=1, source_target_pairs={{0,1},{1,0},{2,3},{3,2},{4,5},{5,4},{6,7},{7,6},{8,9},{9,8},{10,11... | collective-permute-start | bytes 1179656 | tf_op jit(solution)/shard_map/ppermute | solution.py:390
  106.5 10.2 %collective-permute-start.33 = (bf16[3,64,512]{2,1,0:T(8,128)(2,1)S(1)}, bf16[3,64,512]{2,1,0:T(8,128)(2,1)S(1)}, u32[]{:S(2)}, u32[]{:S(2)}) collective-permute-start(bf16[3,64,512]{2,1,0:T(8,128)(2,1)S(1)} %get-tuple-element.142), channel_id=1, source_target_pairs={{0,8},{4,12},{8,0},{12,4},{16,24},{20,28},{24,16},{28,20},{1,9},{5... | collective-permute-start | bytes 589832 | tf_op jit(solution)/shard_map/ppermute | solution.py:403
  106.9 17.1 %collective-permute-start.34 = (bf16[3,64,512]{2,1,0:T(8,128)(2,1)S(1)}, bf16[3,64,512]{2,1,0:T(8,128)(2,1)S(1)}, u32[]{:S(2)}, u32[]{:S(2)}) collective-permute-start(bf16[3,64,512]{2,1,0:T(8,128)(2,1)S(1)} %get-tuple-element.143), channel_id=1, source_target_pairs={{0,16},{4,20},{8,24},{12,28},{16,0},{20,4},{24,8},{28,12},{1,17},{... | collective-permute-start | bytes 589832 | tf_op jit(solution)/shard_map/ppermute | solution.py:403
  108.5 15.5 %collective-permute-start.35 = (bf16[3,64,512]{2,1,0:T(8,128)(2,1)S(1)}, bf16[3,64,512]{2,1,0:T(8,128)(2,1)S(1)}, u32[]{:S(2)}, u32[]{:S(2)}) collective-permute-start(bf16[3,64,512]{2,1,0:T(8,128)(2,1)S(1)} %get-tuple-element.144), channel_id=1, source_target_pairs={{0,24},{4,28},{8,16},{12,20},{16,8},{20,12},{24,0},{28,4},{1,25},{... | collective-permute-start | bytes 589832 | tf_op jit(solution)/shard_map/ppermute | solution.py:403
  124.3 9.7 %collective-permute-start.36 = (bf16[3,64,512]{2,1,0:T(8,128)(2,1)S(1)}, bf16[3,64,512]{2,1,0:T(8,128)(2,1)S(1)}, u32[]{:S(2)}, u32[]{:S(2)}) collective-permute-start(bf16[3,64,512]{2,1,0:T(8,128)(2,1)S(1)} %shard_map.57.refs_0_), channel_id=1, source_target_pairs={{0,8},{4,12},{8,0},{12,4},{16,24},{20,28},{24,16},{28,20},{1,9},{5... | collective-permute-start | bytes 589832 | tf_op jit(solution)/shard_map/ppermute | solution.py:403
  128.1 11.8 %collective-permute-start.38 = (bf16[3,64,512]{2,1,0:T(8,128)(2,1)S(1)}, bf16[3,64,512]{2,1,0:T(8,128)(2,1)S(1)}, u32[]{:S(2)}, u32[]{:S(2)}) collective-permute-start(bf16[3,64,512]{2,1,0:T(8,128)(2,1)S(1)} %shard_map.57.refs_0_), channel_id=1, source_target_pairs={{0,24},{4,28},{8,16},{12,20},{16,8},{20,12},{24,0},{28,4},{1,25},{... | collective-permute-start | bytes 589832 | tf_op jit(solution)/shard_map/ppermute | solution.py:403
  129.7 16.3 %collective-permute-start.37 = (bf16[3,64,512]{2,1,0:T(8,128)(2,1)S(1)}, bf16[3,64,512]{2,1,0:T(8,128)(2,1)S(1)}, u32[]{:S(2)}, u32[]{:S(2)}) collective-permute-start(bf16[3,64,512]{2,1,0:T(8,128)(2,1)S(1)} %shard_map.57.refs_0_), channel_id=1, source_target_pairs={{0,16},{4,20},{8,24},{12,28},{16,0},{20,4},{24,8},{28,12},{1,17},{... | collective-permute-start | bytes 589832 | tf_op jit(solution)/shard_map/ppermute | solution.py:403
  134.9 12.1 %collective-permute-start.39 = (bf16[3,128,256]{2,1,0:T(8,128)(2,1)S(1)}, bf16[3,128,256]{2,1,0:T(8,128)(2,1)S(1)}, u32[]{:S(2)}, u32[]{:S(2)}) collective-permute-start(bf16[3,128,256]{2,1,0:T(8,128)(2,1)S(1)} %get-tuple-element.146.a0), channel_id=1, source_target_pairs={{0,2},{1,3},{2,0},{3,1},{4,6},{5,7},{6,4},{7,5},{8,10},{9,11},{10,... | collective-permute-start | bytes 589832 | tf_op jit(solution)/shard_map/ppermute | solution.py:393
  135.6 11.4 %collective-permute-start.40 = (bf16[3,128,256]{2,1,0:T(8,128)(2,1)S(1)}, bf16[3,128,256]{2,1,0:T(8,128)(2,1)S(1)}, u32[]{:S(2)}, u32[]{:S(2)}) collective-permute-start(bf16[3,128,256]{2,1,0:T(8,128)(2,1)S(1)} %get-tuple-element.149), channel_id=1, source_target_pairs={{0,4},{4,0},{8,12},{12,8},{16,20},{20,16},{24,28},{28,24},{1,5},{5... | collective-permute-start | bytes 589832 | tf_op jit(solution)/shard_map/ppermute | solution.py:396
  137.2 13.4 %collective-permute-start.41 = (bf16[3,128,256]{2,1,0:T(8,128)(2,1)S(1)}, bf16[3,128,256]{2,1,0:T(8,128)(2,1)S(1)}, u32[]{:S(2)}, u32[]{:S(2)}) collective-permute-start(bf16[3,128,256]{2,1,0:T(8,128)(2,1)S(1)} %get-tuple-element.149), channel_id=1, source_target_pairs={{0,6},{1,7},{2,4},{3,5},{4,2},{5,3},{6,0},{7,1},{8,14},{9,15},{10,... | collective-permute-start | bytes 589832 | tf_op jit(solution)/shard_map/ppermute | solution.py:400
  149.0 8.6 %collective-permute-start.43 = (bf16[3,128,256]{2,1,0:T(8,128)(2,1)S(1)}, bf16[3,128,256]{2,1,0:T(8,128)(2,1)S(1)}, u32[]{:S(2)}, u32[]{:S(2)}) collective-permute-start(bf16[3,128,256]{2,1,0:T(8,128)(2,1)S(1)} %get-tuple-element.156), channel_id=1, source_target_pairs={{0,4},{4,0},{8,12},{12,8},{16,20},{20,16},{24,28},{28,24},{1,5},{5... | collective-permute-start | bytes 589832 | tf_op jit(solution)/shard_map/ppermute | solution.py:396
  (17 other events, 127.4 us)

commit v5 on v4

--- a/solution.py
+++ b/solution.py
@@ -318,11 +318,11 @@
     old = jnp.concatenate([x[s] for s in range(seqs)], axis=0)
     made = normalized(jnp.concatenate(columns, axis=0), old, out_weight, gain)
     half = jnp.where(x_bit == 1, made[:, 2 * quarter :], made[:, : 2 * quarter])
-    low, high = half[:, :quarter], half[:, quarter:]
-    mine, theirs = jnp.where(core == 1, high, low), jnp.where(core == 1, low, high)
     for s in range(seqs):
-        keep[s % 2, s // 2] = mine[s * rows : (s + 1) * rows].T.astype(BF16)
-        send[s % 2, s // 2] = theirs[s * rows : (s + 1) * rows].T.astype(BF16)
+        turned = half[s * rows : (s + 1) * rows].T.astype(BF16)
+        low, high = turned[:quarter], turned[quarter:]
+        keep[s % 2, s // 2] = jnp.where(core == 1, high, low)
+        send[s % 2, s // 2] = jnp.where(core == 1, low, high)
 
 
 def last_layer(place, attended, x, out_weight, gain):
@@ -467,7 +467,15 @@
             if not more:
                 attended.append([near_part, x_near, y_near, over_xy(far_part)])
                 continue
-            x_far, y_far = over_x(far_part), over_y(near_part)
+            near_send, far_send = near_part, far_part
+            if g:
+                tied = (5, 6)
+                near_send, far_send, *now = lax.optimization_barrier(
+                    (near_part, far_part, *(before[i] for i in tied))
+                )
+                for i, one in zip(tied, now):
+                    before[i] = one
+            x_far, y_far = over_x(far_send), over_y(near_send)
             if g:
                 done = next_layer(place, g - 1, attended[-1], near[g - 1], far[g - 1], out_mat, gain, weight, both)
                 x_near, y_near, *done = lax.optimization_barrier((x_near, y_near, *done))

time: 163 us -> 162 us (level)
  transfers between devices with their start and end apart: 47 -> 47, of which waited for: 22 -> 22; matrix products, arithmetic and copies ran while one was open for 3% -> 3% of each run, Pallas kernels for 15% -> 14%
where the time goes in v5:
time: 162 us
  waiting for transfers between devices  72.7 us (45%)
  starting transfers between devices  56 us (35%)
  Pallas kernels  25.5 us (16%)
  local copies, waits for them, and re-layouts  6.63 us (4%)
    ppermute x12, waiting for transfers between devices, over_z(): return lax.ppermute(a, 'rows', [(i, i ^ 2 * d) for i in range(n_rows)])  40.6 us
    ppermute x12, starting transfers between devices, over_z(): return lax.ppermute(a, 'rows', [(i, i ^ 2 * d) for i in range(n_rows)])  24.4 us
    ppermute x11, starting transfers between devices, over_x(): return lax.ppermute(a, 'heads', [(i, i ^ 2) for i in range(n_groups)])  14.6 us
    ppermute x11, starting transfers between devices, over_y(): return lax.ppermute(a, 'rows', [(i, i ^ 1) for i in range(n_rows)])  13.3 us
    ppermute x11, waiting for transfers between devices, over_y(): return lax.ppermute(a, 'rows', [(i, i ^ 1) for i in range(n_rows)])  13.2 us
    ppermute x11, waiting for transfers between devices, over_x(): return lax.ppermute(a, 'heads', [(i, i ^ 2) for i in range(n_groups)])  12.8 us
    pallas_call x2, Pallas kernels, next_layer(): pl.pallas_call(functools.partial(next_kernel, g), in_specs=[SMEM] + [FULL...  8.2 us
    pallas_call x2, Pallas kernels, first(): pl.pallas_call(first_kernel, in_specs=[SMEM] + [FULL] * 7, out_specs=[FUL...  4.91 us
  transfers between devices with their start and end apart: 47, of which 22 were waited for; matrix products, arithmetic and copies ran while one was open for 3% of the time, Pallas kernels for 14%

profile of v5, /device:TPU:0, one launch (start us, length us, event | category | flops | bytes accessed | tf_op | source)
XLA Modules:
  0.0 161.8 jit_solution(4989221831547056015)
XLA Ops:
  3.1 2.5 %collective-permute-start.1 = (bf16[2,256,384]{2,1,0:T(8,128)(2,1)S(1)}, bf16[2,256,384]{2,1,0:T(8,128)(2,1)S(1)}, u32[]{:S(2)}, u32[]{:S(2)}) collective-permute-start(bf16[2,256,384]{2,1,0:T(8,128)(2,1)S(1)} %pad_maximum_fusion.2.p0), channel_id=1, source_target_pairs={{0,2},{1,3},{2,0},{3,1},{4,6},{5,7},{6,4},{7,5},{8,10},{9,11},{10,... | collective-permute-start | bytes 1179656 | tf_op jit(solution)/shard_map/ppermute | solution.py:393
  8.8 6.7 %collective-permute-done.1.p2 = bf16[2,256,384]{2,1,0:T(8,128)(2,1)S(1)} collective-permute-done((bf16[2,256,384]{2,1,0:T(8,128)(2,1)S(1)}, bf16[2,256,384]{2,1,0:T(8,128)(2,1)S(1)}, u32[]{:S(2)}, u32[]{:S(2)}) %collective-permute-start.1) | collective-permute-done | bytes 393248 | tf_op jit(solution)/shard_map/ppermute | solution.py:393
  15.6 2.0 %collective-permute-start.5 = (bf16[2,256,384]{2,1,0:T(8,128)(2,1)S(1)}, bf16[2,256,384]{2,1,0:T(8,128)(2,1)S(1)}, u32[]{:S(2)}, u32[]{:S(2)}) collective-permute-start(bf16[2,256,384]{2,1,0:T(8,128)(2,1)S(1)} %collective-permute-done.1.p2), channel_id=1, source_target_pairs={{0,4},{4,0},{8,12},{12,8},{16,20},{20,16},{24,28},{28,24},{1,5},{5... | collective-permute-start | bytes 1179656 | tf_op jit(solution)/shard_map/ppermute | solution.py:396
  19.0 2.0 %dynamic-slice_bitcast_fusion.3 = (bf16[768,192]{1,0:T(8,128)(2,1)S(1)}, bf16[768,192]{1,0:T(8,128)(2,1)S(1)}, bf16[768,192]{1,0:T(8,128)(2,1)S(1)}) fusion(bf16[2,768,3,768]{3,1,2,0:T(8,128)(2,1)} %param.5, u32[]{:T(128)S(6)} %mul.25), kind=kLoop, calls=%fused_computation.7 | loop fusion | bytes 1769476 | tf_op jit(solution)/shard_map/reshape | solution.py:409
  21.0 3.0 %collective-permute-done.2.p3 = bf16[2,256,384]{2,1,0:T(8,128)(2,1)S(1)} collective-permute-done((bf16[2,256,384]{2,1,0:T(8,128)(2,1)S(1)}, bf16[2,256,384]{2,1,0:T(8,128)(2,1)S(1)}, u32[]{:S(2)}, u32[]{:S(2)}) %collective-permute-start.2) | collective-permute-done | bytes 393248 | tf_op jit(solution)/shard_map/ppermute | solution.py:393
  24.0 2.5 %shard_map.46 = (bf16[4,256,768]{2,1,0:T(8,128)(2,1)S(1)}, bf16[3,256,256]{2,1,0:T(8,128)(2,1)S(1)}, bf16[3,256,256]{2,1,0:T(8,128)(2,1)S(1)}, bf16[3,256,256]{2,1,0:T(8,128)(2,1)S(1)}) custom-call(s32[5]{0:T(128)S(1)} %convert_element_type.15.place, bf16[2,256,384]{2,1,0:T(8,128)(2,1)S(1)} %pad_maximum_fusion.2.p0, ...), custom_call_target="tpu_custom_call" | custom-call | flops 905969664 | bytes 9830400 | tf_op jit(solution)/shard_map/pallas_call | solution.py:81
  26.5 7.1 %collective-permute-done.5.p2 = bf16[2,256,384]{2,1,0:T(8,128)(2,1)S(1)} collective-permute-done((bf16[2,256,384]{2,1,0:T(8,128)(2,1)S(1)}, bf16[2,256,384]{2,1,0:T(8,128)(2,1)S(1)}, u32[]{:S(2)}, u32[]{:S(2)}) %collective-permute-start.5) | collective-permute-done | bytes 393248 | tf_op jit(solution)/shard_map/ppermute | solution.py:396
  33.7 2.4 %shard_map.47 = (bf16[4,256,768]{2,1,0:T(8,128)(2,1)S(1)}, bf16[3,256,256]{2,1,0:T(8,128)(2,1)S(1)}, bf16[3,256,256]{2,1,0:T(8,128)(2,1)S(1)}, bf16[3,256,256]{2,1,0:T(8,128)(2,1)S(1)}) custom-call(s32[5]{0:T(128)S(1)} %convert_element_type.15.place, bf16[2,256,384]{2,1,0:T(8,128)(2,1)S(1)} %collective-permute-done.3.p0, ...), custom_call_target="tpu_custom_call" | custom-call | flops 905969664 | bytes 9830400 | tf_op jit(solution)/shard_map/pallas_call | solution.py:81
  40.7 2.6 %collective-permute-start.12 = (bf16[3,64,512]{2,1,0:T(8,128)(2,1)S(1)}, bf16[3,64,512]{2,1,0:T(8,128)(2,1)S(1)}, u32[]{:S(2)}, u32[]{:S(2)}) collective-permute-start(bf16[3,64,512]{2,1,0:T(8,128)(2,1)S(1)} %get-tuple-element.110), channel_id=1, source_target_pairs={{0,16},{4,20},{8,24},{12,28},{16,0},{20,4},{24,8},{28,12},{1,17},{... | collective-permute-start | bytes 589832 | tf_op jit(solution)/shard_map/ppermute | solution.py:403
  43.6 2.0 %dynamic-slice_bitcast_fusion = (bf16[768,192]{1,0:T(8,128)(2,1)S(1)}, bf16[768,192]{1,0:T(8,128)(2,1)S(1)}, bf16[768,192]{1,0:T(8,128)(2,1)S(1)}) fusion(bf16[2,768,3,768]{3,1,2,0:T(8,128)(2,1)} %param.5, u32[]{:T(128)S(6)} %mul.25), kind=kLoop, calls=%fused_computation.4 | loop fusion | bytes 1769476 | tf_op jit(solution)/shard_map/reshape | solution.py:409
  46.2 3.5 %collective-permute-done.11.refs_1_ = bf16[3,64,512]{2,1,0:T(8,128)(2,1)S(1)} collective-permute-done((bf16[3,64,512]{2,1,0:T(8,128)(2,1)S(1)}, bf16[3,64,512]{2,1,0:T(8,128)(2,1)S(1)}, u32[]{:S(2)}, u32[]{:S(2)}) %collective-permute-start.11) | collective-permute-done | bytes 196640 | tf_op jit(solution)/shard_map/ppermute | solution.py:403
  49.7 8.1 %collective-permute-done.12.refs_2_ = bf16[3,64,512]{2,1,0:T(8,128)(2,1)S(1)} collective-permute-done((bf16[3,64,512]{2,1,0:T(8,128)(2,1)S(1)}, bf16[3,64,512]{2,1,0:T(8,128)(2,1)S(1)}, u32[]{:S(2)}, u32[]{:S(2)}) %collective-permute-start.12) | collective-permute-done | bytes 196640 | tf_op jit(solution)/shard_map/ppermute | solution.py:403
  58.1 3.8 %collective-permute-start.16 = (bf16[3,64,512]{2,1,0:T(8,128)(2,1)S(1)}, bf16[3,64,512]{2,1,0:T(8,128)(2,1)S(1)}, u32[]{:S(2)}, u32[]{:S(2)}) collective-permute-start(bf16[3,64,512]{2,1,0:T(8,128)(2,1)S(1)} %shard_map.50.refs_0_), channel_id=1, source_target_pairs={{0,8},{4,12},{8,0},{12,4},{16,24},{20,28},{24,16},{28,20},{1,9},{5... | collective-permute-start | bytes 589832 | tf_op jit(solution)/shard_map/ppermute | solution.py:403
  61.9 2.5 %collective-permute-start.15 = (bf16[3,64,512]{2,1,0:T(8,128)(2,1)S(1)}, bf16[3,64,512]{2,1,0:T(8,128)(2,1)S(1)}, u32[]{:S(2)}, u32[]{:S(2)}) collective-permute-start(bf16[3,64,512]{2,1,0:T(8,128)(2,1)S(1)} %shard_map.50.refs_0_), channel_id=1, source_target_pairs={{0,24},{4,28},{8,16},{12,20},{16,8},{20,12},{24,0},{28,4},{1,25},{... | collective-permute-start | bytes 589832 | tf_op jit(solution)/shard_map/ppermute | solution.py:403
  64.4 2.9 %collective-permute-done.16.refs_1_ = bf16[3,64,512]{2,1,0:T(8,128)(2,1)S(1)} collective-permute-done((bf16[3,64,512]{2,1,0:T(8,128)(2,1)S(1)}, bf16[3,64,512]{2,1,0:T(8,128)(2,1)S(1)}, u32[]{:S(2)}, u32[]{:S(2)}) %collective-permute-start.16) | collective-permute-done | bytes 196640 | tf_op jit(solution)/shard_map/ppermute | solution.py:403
  70.9 3.5 %collective-permute-start.14 = (bf16[3,64,512]{2,1,0:T(8,128)(2,1)S(1)}, bf16[3,64,512]{2,1,0:T(8,128)(2,1)S(1)}, u32[]{:S(2)}, u32[]{:S(2)}) collective-permute-start(bf16[3,64,512]{2,1,0:T(8,128)(2,1)S(1)} %shard_map.50.refs_0_), channel_id=1, source_target_pairs={{0,16},{4,20},{8,24},{12,28},{16,0},{20,4},{24,8},{28,12},{1,17},{... | collective-permute-start | bytes 589832 | tf_op jit(solution)/shard_map/ppermute | solution.py:403
  78.4 2.4 %collective-permute-done.14.refs_0_ = bf16[3,64,512]{2,1,0:T(8,128)(2,1)S(1)} collective-permute-done((bf16[3,64,512]{2,1,0:T(8,128)(2,1)S(1)}, bf16[3,64,512]{2,1,0:T(8,128)(2,1)S(1)}, u32[]{:S(2)}, u32[]{:S(2)}) %collective-permute-start.14) | collective-permute-done | bytes 196640 | tf_op jit(solution)/shard_map/ppermute | solution.py:403
  85.9 4.2 %shard_map.53 = (bf16[4,128,768]{2,1,0:T(8,128)(2,1)S(1)}, bf16[3,128,512]{2,1,0:T(8,128)(2,1)S(1)}, bf16[3,128,512]{2,1,0:T(8,128)(2,1)S(1)}, bf16[3,128,512]{2,1,0:T(8,128)(2,1)S(1)}) custom-call(s32[5]{0:T(128)S(1)} %convert_element_type.15.place, bf16[3,128,256]{2,1,0:T(8,128)(2,1)S(1)} %get-tuple-element.115.refs_0_, ...), custom_call_target="tpu_custom_call" | custom-call | flops 2113929216 | bytes 5210112 | tf_op jit(solution)/shard_map/pallas_call | solution.py:302
  94.7 2.3 %collective-permute-done.28.refs_7_ = bf16[3,128,256]{2,1,0:T(8,128)(2,1)S(1)} collective-permute-done((bf16[3,128,256]{2,1,0:T(8,128)(2,1)S(1)}, bf16[3,128,256]{2,1,0:T(8,128)(2,1)S(1)}, u32[]{:S(2)}, u32[]{:S(2)}) %collective-permute-start.28) | collective-permute-done | bytes 196640 | tf_op jit(solution)/shard_map/ppermute | solution.py:396
  97.7 4.0 %shard_map.54 = (bf16[4,128,768]{2,1,0:T(8,128)(2,1)S(1)}, bf16[3,128,512]{2,1,0:T(8,128)(2,1)S(1)}, bf16[3,128,512]{2,1,0:T(8,128)(2,1)S(1)}, bf16[3,128,512]{2,1,0:T(8,128)(2,1)S(1)}) custom-call(s32[5]{0:T(128)S(1)} %convert_element_type.15.place, bf16[3,128,256]{2,1,0:T(8,128)(2,1)S(1)} %get-tuple-element.137.refs_0_, ...), custom_call_target="tpu_custom_call" | custom-call | flops 2113929216 | bytes 5210112 | tf_op jit(solution)/shard_map/pallas_call | solution.py:302
  105.4 1.8 %collective-permute-start.34 = (bf16[3,64,512]{2,1,0:T(8,128)(2,1)S(1)}, bf16[3,64,512]{2,1,0:T(8,128)(2,1)S(1)}, u32[]{:S(2)}, u32[]{:S(2)}) collective-permute-start(bf16[3,64,512]{2,1,0:T(8,128)(2,1)S(1)} %get-tuple-element.151), channel_id=1, source_target_pairs={{0,16},{4,20},{8,24},{12,28},{16,0},{20,4},{24,8},{28,12},{1,17},{... | collective-permute-start | bytes 589832 | tf_op jit(solution)/shard_map/ppermute | solution.py:403
  107.2 2.1 %collective-permute-start.35 = (bf16[3,64,512]{2,1,0:T(8,128)(2,1)S(1)}, bf16[3,64,512]{2,1,0:T(8,128)(2,1)S(1)}, u32[]{:S(2)}, u32[]{:S(2)}) collective-permute-start(bf16[3,64,512]{2,1,0:T(8,128)(2,1)S(1)} %get-tuple-element.152), channel_id=1, source_target_pairs={{0,24},{4,28},{8,16},{12,20},{16,8},{20,12},{24,0},{28,4},{1,25},{... | collective-permute-start | bytes 589832 | tf_op jit(solution)/shard_map/ppermute | solution.py:403
  110.3 4.9 %collective-permute-done.33.refs_1_ = bf16[3,64,512]{2,1,0:T(8,128)(2,1)S(1)} collective-permute-done((bf16[3,64,512]{2,1,0:T(8,128)(2,1)S(1)}, bf16[3,64,512]{2,1,0:T(8,128)(2,1)S(1)}, u32[]{:S(2)}, u32[]{:S(2)}) %collective-permute-start.33) | collective-permute-done | bytes 196640 | tf_op jit(solution)/shard_map/ppermute | solution.py:403
  115.2 7.3 %collective-permute-done.34.refs_2_ = bf16[3,64,512]{2,1,0:T(8,128)(2,1)S(1)} collective-permute-done((bf16[3,64,512]{2,1,0:T(8,128)(2,1)S(1)}, bf16[3,64,512]{2,1,0:T(8,128)(2,1)S(1)}, u32[]{:S(2)}, u32[]{:S(2)}) %collective-permute-start.34) | collective-permute-done | bytes 196640 | tf_op jit(solution)/shard_map/ppermute | solution.py:403
  122.8 3.8 %collective-permute-start.36 = (bf16[3,64,512]{2,1,0:T(8,128)(2,1)S(1)}, bf16[3,64,512]{2,1,0:T(8,128)(2,1)S(1)}, u32[]{:S(2)}, u32[]{:S(2)}) collective-permute-start(bf16[3,64,512]{2,1,0:T(8,128)(2,1)S(1)} %shard_map.57.refs_0_), channel_id=1, source_target_pairs={{0,8},{4,12},{8,0},{12,4},{16,24},{20,28},{24,16},{28,20},{1,9},{5... | collective-permute-start | bytes 589832 | tf_op jit(solution)/shard_map/ppermute | solution.py:403
  126.5 2.1 %collective-permute-start.38 = (bf16[3,64,512]{2,1,0:T(8,128)(2,1)S(1)}, bf16[3,64,512]{2,1,0:T(8,128)(2,1)S(1)}, u32[]{:S(2)}, u32[]{:S(2)}) collective-permute-start(bf16[3,64,512]{2,1,0:T(8,128)(2,1)S(1)} %shard_map.57.refs_0_), channel_id=1, source_target_pairs={{0,24},{4,28},{8,16},{12,20},{16,8},{20,12},{24,0},{28,4},{1,25},{... | collective-permute-start | bytes 589832 | tf_op jit(solution)/shard_map/ppermute | solution.py:403
  128.6 3.3 %collective-permute-done.36.refs_1_ = bf16[3,64,512]{2,1,0:T(8,128)(2,1)S(1)} collective-permute-done((bf16[3,64,512]{2,1,0:T(8,128)(2,1)S(1)}, bf16[3,64,512]{2,1,0:T(8,128)(2,1)S(1)}, u32[]{:S(2)}, u32[]{:S(2)}) %collective-permute-start.36) | collective-permute-done | bytes 196640 | tf_op jit(solution)/shard_map/ppermute | solution.py:403
  132.8 1.8 %collective-permute-start.39 = (bf16[3,128,256]{2,1,0:T(8,128)(2,1)S(1)}, bf16[3,128,256]{2,1,0:T(8,128)(2,1)S(1)}, u32[]{:S(2)}, u32[]{:S(2)}) collective-permute-start(bf16[3,128,256]{2,1,0:T(8,128)(2,1)S(1)} %get-tuple-element.154.a0), channel_id=1, source_target_pairs={{0,2},{1,3},{2,0},{3,1},{4,6},{5,7},{6,4},{7,5},{8,10},{9,11},{10,... | collective-permute-start | bytes 589832 | tf_op jit(solution)/shard_map/ppermute | solution.py:393
  136.4 2.3 %collective-permute-done.38.refs_1_ = bf16[3,64,512]{2,1,0:T(8,128)(2,1)S(1)} collective-permute-done((bf16[3,64,512]{2,1,0:T(8,128)(2,1)S(1)}, bf16[3,64,512]{2,1,0:T(8,128)(2,1)S(1)}, u32[]{:S(2)}, u32[]{:S(2)}) %collective-permute-start.38) | collective-permute-done | bytes 196640 | tf_op jit(solution)/shard_map/ppermute | solution.py:403
  138.7 5.8 %collective-permute-done.37.refs_0_ = bf16[3,64,512]{2,1,0:T(8,128)(2,1)S(1)} collective-permute-done((bf16[3,64,512]{2,1,0:T(8,128)(2,1)S(1)}, bf16[3,64,512]{2,1,0:T(8,128)(2,1)S(1)}, u32[]{:S(2)}, u32[]{:S(2)}) %collective-permute-start.37) | collective-permute-done | bytes 196640 | tf_op jit(solution)/shard_map/ppermute | solution.py:403
  150.8 2.4 %collective-permute-done.42.a1 = bf16[3,128,256]{2,1,0:T(8,128)(2,1)S(1)} collective-permute-done((bf16[3,128,256]{2,1,0:T(8,128)(2,1)S(1)}, bf16[3,128,256]{2,1,0:T(8,128)(2,1)S(1)}, u32[]{:S(2)}, u32[]{:S(2)}) %collective-permute-start.42) | collective-permute-done | bytes 196640 | tf_op jit(solution)/shard_map/ppermute | solution.py:393
  153.2 2.5 %collective-permute-done.44.a3 = bf16[3,128,256]{2,1,0:T(8,128)(2,1)S(1)} collective-permute-done((bf16[3,128,256]{2,1,0:T(8,128)(2,1)S(1)}, bf16[3,128,256]{2,1,0:T(8,128)(2,1)S(1)}, u32[]{:S(2)}, u32[]{:S(2)}) %collective-permute-start.44) | collective-permute-done | bytes 196640 | tf_op jit(solution)/shard_map/ppermute | solution.py:400
  (99 shorter events, 51.5 us)
Async XLA Ops:
  3.1 12.5 %collective-permute-start.1 = (bf16[2,256,384]{2,1,0:T(8,128)(2,1)S(1)}, bf16[2,256,384]{2,1,0:T(8,128)(2,1)S(1)}, u32[]{:S(2)}, u32[]{:S(2)}) collective-permute-start(bf16[2,256,384]{2,1,0:T(8,128)(2,1)S(1)} %pad_maximum_fusion.2.p0), channel_id=1, source_target_pairs={{0,2},{1,3},{2,0},{3,1},{4,6},{5,7},{6,4},{7,5},{8,10},{9,11},{10,... | collective-permute-start | bytes 1179656 | tf_op jit(solution)/shard_map/ppermute | solution.py:393
  5.6 11.9 %collective-permute-start.4 = (bf16[2,256,384]{2,1,0:T(8,128)(2,1)S(1)}, bf16[2,256,384]{2,1,0:T(8,128)(2,1)S(1)}, u32[]{:S(2)}, u32[]{:S(2)}) collective-permute-start(bf16[2,256,384]{2,1,0:T(8,128)(2,1)S(1)} %collective-permute-done.p1), channel_id=1, source_target_pairs={{0,4},{4,0},{8,12},{12,8},{16,20},{20,16},{24,28},{28,24},{1,5},{5... | collective-permute-start | bytes 1179656 | tf_op jit(solution)/shard_map/ppermute | solution.py:396
  7.1 16.9 %collective-permute-start.2 = (bf16[2,256,384]{2,1,0:T(8,128)(2,1)S(1)}, bf16[2,256,384]{2,1,0:T(8,128)(2,1)S(1)}, u32[]{:S(2)}, u32[]{:S(2)}) collective-permute-start(bf16[2,256,384]{2,1,0:T(8,128)(2,1)S(1)} %collective-permute-done.p1), channel_id=1, source_target_pairs={{0,2},{1,3},{2,0},{3,1},{4,6},{5,7},{6,4},{7,5},{8,10},{9,11},{10,... | collective-permute-start | bytes 1179656 | tf_op jit(solution)/shard_map/ppermute | solution.py:393
  8.3 18.2 %collective-permute-start.3 = (bf16[2,256,384]{2,1,0:T(8,128)(2,1)S(1)}, bf16[2,256,384]{2,1,0:T(8,128)(2,1)S(1)}, u32[]{:S(2)}, u32[]{:S(2)}) collective-permute-start(bf16[2,256,384]{2,1,0:T(8,128)(2,1)S(1)} %pad_maximum_fusion.2.p0), channel_id=1, source_target_pairs={{0,4},{4,0},{8,12},{12,8},{16,20},{20,16},{24,28},{28,24},{1,5},{5... | collective-permute-start | bytes 1179656 | tf_op jit(solution)/shard_map/ppermute | solution.py:396
  15.6 18.1 %collective-permute-start.5 = (bf16[2,256,384]{2,1,0:T(8,128)(2,1)S(1)}, bf16[2,256,384]{2,1,0:T(8,128)(2,1)S(1)}, u32[]{:S(2)}, u32[]{:S(2)}) collective-permute-start(bf16[2,256,384]{2,1,0:T(8,128)(2,1)S(1)} %collective-permute-done.1.p2), channel_id=1, source_target_pairs={{0,4},{4,0},{8,12},{12,8},{16,20},{20,16},{24,28},{28,24},{1,5},{5... | collective-permute-start | bytes 1179656 | tf_op jit(solution)/shard_map/ppermute | solution.py:396
  17.5 16.1 %collective-permute-start.6 = (bf16[2,256,384]{2,1,0:T(8,128)(2,1)S(1)}, bf16[2,256,384]{2,1,0:T(8,128)(2,1)S(1)}, u32[]{:S(2)}, u32[]{:S(2)}) collective-permute-start(bf16[2,256,384]{2,1,0:T(8,128)(2,1)S(1)} %collective-permute-done.4.p1), channel_id=1, source_target_pairs={{0,2},{1,3},{2,0},{3,1},{4,6},{5,7},{6,4},{7,5},{8,10},{9,11},{10,... | collective-permute-start | bytes 1179656 | tf_op jit(solution)/shard_map/ppermute | solution.py:393
  26.4 10.3 %collective-permute-start.7 = (bf16[3,256,256]{2,1,0:T(8,128)(2,1)S(1)}, bf16[3,256,256]{2,1,0:T(8,128)(2,1)S(1)}, u32[]{:S(2)}, u32[]{:S(2)}) collective-permute-start(bf16[3,256,256]{2,1,0:T(8,128)(2,1)S(1)} %get-tuple-element.97.refs_2_), channel_id=1, source_target_pairs={{0,1},{1,0},{2,3},{3,2},{4,5},{5,4},{6,7},{7,6},{8,9},{9,8},{10,11... | collective-permute-start | bytes 1179656 | tf_op jit(solution)/shard_map/ppermute | solution.py:390
  36.2 9.6 %collective-permute-start.9 = (bf16[3,256,256]{2,1,0:T(8,128)(2,1)S(1)}, bf16[3,256,256]{2,1,0:T(8,128)(2,1)S(1)}, u32[]{:S(2)}, u32[]{:S(2)}) collective-permute-start(bf16[3,256,256]{2,1,0:T(8,128)(2,1)S(1)} %get-tuple-element.106.near), channel_id=1, source_target_pairs={{0,1},{1,0},{2,3},{3,2},{4,5},{5,4},{6,7},{7,6},{8,9},{9,8},{10,11... | collective-permute-start | bytes 1179656 | tf_op jit(solution)/shard_map/ppermute | solution.py:390
  36.7 9.1 %collective-permute-start.10 = (bf16[3,256,256]{2,1,0:T(8,128)(2,1)S(1)}, bf16[3,256,256]{2,1,0:T(8,128)(2,1)S(1)}, u32[]{:S(2)}, u32[]{:S(2)}) collective-permute-start(bf16[3,256,256]{2,1,0:T(8,128)(2,1)S(1)} %get-tuple-element.107.far), channel_id=1, source_target_pairs={{0,1},{1,0},{2,3},{3,2},{4,5},{5,4},{6,7},{7,6},{8,9},{9,8},{10,11... | collective-permute-start | bytes 1179656 | tf_op jit(solution)/shard_map/ppermute | solution.py:390
  39.1 10.6 %collective-permute-start.11 = (bf16[3,64,512]{2,1,0:T(8,128)(2,1)S(1)}, bf16[3,64,512]{2,1,0:T(8,128)(2,1)S(1)}, u32[]{:S(2)}, u32[]{:S(2)}) collective-permute-start(bf16[3,64,512]{2,1,0:T(8,128)(2,1)S(1)} %get-tuple-element.109), channel_id=1, source_target_pairs={{0,8},{4,12},{8,0},{12,4},{16,24},{20,28},{24,16},{28,20},{1,9},{5... | collective-permute-start | bytes 589832 | tf_op jit(solution)/shard_map/ppermute | solution.py:403
  40.7 17.1 %collective-permute-start.12 = (bf16[3,64,512]{2,1,0:T(8,128)(2,1)S(1)}, bf16[3,64,512]{2,1,0:T(8,128)(2,1)S(1)}, u32[]{:S(2)}, u32[]{:S(2)}) collective-permute-start(bf16[3,64,512]{2,1,0:T(8,128)(2,1)S(1)} %get-tuple-element.110), channel_id=1, source_target_pairs={{0,16},{4,20},{8,24},{12,28},{16,0},{20,4},{24,8},{28,12},{1,17},{... | collective-permute-start | bytes 589832 | tf_op jit(solution)/shard_map/ppermute | solution.py:403
  43.3 14.5 %collective-permute-start.13 = (bf16[3,64,512]{2,1,0:T(8,128)(2,1)S(1)}, bf16[3,64,512]{2,1,0:T(8,128)(2,1)S(1)}, u32[]{:S(2)}, u32[]{:S(2)}) collective-permute-start(bf16[3,64,512]{2,1,0:T(8,128)(2,1)S(1)} %get-tuple-element.111), channel_id=1, source_target_pairs={{0,24},{4,28},{8,16},{12,20},{16,8},{20,12},{24,0},{28,4},{1,25},{... | collective-permute-start | bytes 589832 | tf_op jit(solution)/shard_map/ppermute | solution.py:403
  58.1 9.1 %collective-permute-start.16 = (bf16[3,64,512]{2,1,0:T(8,128)(2,1)S(1)}, bf16[3,64,512]{2,1,0:T(8,128)(2,1)S(1)}, u32[]{:S(2)}, u32[]{:S(2)}) collective-permute-start(bf16[3,64,512]{2,1,0:T(8,128)(2,1)S(1)} %shard_map.50.refs_0_), channel_id=1, source_target_pairs={{0,8},{4,12},{8,0},{12,4},{16,24},{20,28},{24,16},{28,20},{1,9},{5... | collective-permute-start | bytes 589832 | tf_op jit(solution)/shard_map/ppermute | solution.py:403
  61.9 13.0 %collective-permute-start.15 = (bf16[3,64,512]{2,1,0:T(8,128)(2,1)S(1)}, bf16[3,64,512]{2,1,0:T(8,128)(2,1)S(1)}, u32[]{:S(2)}, u32[]{:S(2)}) collective-permute-start(bf16[3,64,512]{2,1,0:T(8,128)(2,1)S(1)} %shard_map.50.refs_0_), channel_id=1, source_target_pairs={{0,24},{4,28},{8,16},{12,20},{16,8},{20,12},{24,0},{28,4},{1,25},{... | collective-permute-start | bytes 589832 | tf_op jit(solution)/shard_map/ppermute | solution.py:403
  70.9 9.9 %collective-permute-start.14 = (bf16[3,64,512]{2,1,0:T(8,128)(2,1)S(1)}, bf16[3,64,512]{2,1,0:T(8,128)(2,1)S(1)}, u32[]{:S(2)}, u32[]{:S(2)}) collective-permute-start(bf16[3,64,512]{2,1,0:T(8,128)(2,1)S(1)} %shard_map.50.refs_0_), channel_id=1, source_target_pairs={{0,16},{4,20},{8,24},{12,28},{16,0},{20,4},{24,8},{28,12},{1,17},{... | collective-permute-start | bytes 589832 | tf_op jit(solution)/shard_map/ppermute | solution.py:403
  74.9 9.3 %collective-permute-start.22 = (bf16[3,128,256]{2,1,0:T(8,128)(2,1)S(1)}, bf16[3,128,256]{2,1,0:T(8,128)(2,1)S(1)}, u32[]{:S(2)}, u32[]{:S(2)}) collective-permute-start(bf16[3,128,256]{2,1,0:T(8,128)(2,1)S(1)} %get-tuple-element.116.refs_4_), channel_id=1, source_target_pairs={{0,2},{1,3},{2,0},{3,1},{4,6},{5,7},{6,4},{7,5},{8,10},{9,11},{10,... | collective-permute-start | bytes 589832 | tf_op jit(solution)/shard_map/ppermute | solution.py:393
  75.8 9.5 %collective-permute-start.24 = (bf16[3,128,256]{2,1,0:T(8,128)(2,1)S(1)}, bf16[3,128,256]{2,1,0:T(8,128)(2,1)S(1)}, u32[]{:S(2)}, u32[]{:S(2)}) collective-permute-start(bf16[3,128,256]{2,1,0:T(8,128)(2,1)S(1)} %collective-permute-done.17.refs_1_), channel_id=1, source_target_pairs={{0,4},{4,0},{8,12},{12,8},{16,20},{20,16},{24,28},{28,24},{1,5},{5... | collective-permute-start | bytes 589832 | tf_op jit(solution)/shard_map/ppermute | solution.py:396
  77.3 8.6 %collective-permute-start.21 = (bf16[3,128,256]{2,1,0:T(8,128)(2,1)S(1)}, bf16[3,128,256]{2,1,0:T(8,128)(2,1)S(1)}, u32[]{:S(2)}, u32[]{:S(2)}) collective-permute-start(bf16[3,128,256]{2,1,0:T(8,128)(2,1)S(1)} %collective-permute-done.18.refs_2_), channel_id=1, source_target_pairs={{0,2},{1,3},{2,0},{3,1},{4,6},{5,7},{6,4},{7,5},{8,10},{9,11},{10,... | collective-permute-start | bytes 589832 | tf_op jit(solution)/shard_map/ppermute | solution.py:393
  84.2 8.9 %collective-permute-start.26 = (bf16[3,128,256]{2,1,0:T(8,128)(2,1)S(1)}, bf16[3,128,256]{2,1,0:T(8,128)(2,1)S(1)}, u32[]{:S(2)}, u32[]{:S(2)}) collective-permute-start(bf16[3,128,256]{2,1,0:T(8,128)(2,1)S(1)} %get-tuple-element.136.refs_4_), channel_id=1, source_target_pairs={{0,2},{1,3},{2,0},{3,1},{4,6},{5,7},{6,4},{7,5},{8,10},{9,11},{10,... | collective-permute-start | bytes 589832 | tf_op jit(solution)/shard_map/ppermute | solution.py:393
  85.2 9.5 %collective-permute-start.27 = (bf16[3,128,256]{2,1,0:T(8,128)(2,1)S(1)}, bf16[3,128,256]{2,1,0:T(8,128)(2,1)S(1)}, u32[]{:S(2)}, u32[]{:S(2)}) collective-permute-start(bf16[3,128,256]{2,1,0:T(8,128)(2,1)S(1)} %get-tuple-element.137.refs_0_), channel_id=1, source_target_pairs={{0,4},{4,0},{8,12},{12,8},{16,20},{20,16},{24,28},{28,24},{1,5},{5... | collective-permute-start | bytes 589832 | tf_op jit(solution)/shard_map/ppermute | solution.py:396
  93.1 9.3 %collective-permute-start.29 = (bf16[3,128,512]{2,1,0:T(8,128)(2,1)S(1)}, bf16[3,128,512]{2,1,0:T(8,128)(2,1)S(1)}, u32[]{:S(2)}, u32[]{:S(2)}) collective-permute-start(bf16[3,128,512]{2,1,0:T(8,128)(2,1)S(1)} %get-tuple-element.139.refs_2_), channel_id=1, source_target_pairs={{0,1},{1,0},{2,3},{3,2},{4,5},{5,4},{6,7},{7,6},{8,9},{9,8},{10,11... | collective-permute-start | bytes 1179656 | tf_op jit(solution)/shard_map/ppermute | solution.py:390
  104.8 10.4 %collective-permute-start.33 = (bf16[3,64,512]{2,1,0:T(8,128)(2,1)S(1)}, bf16[3,64,512]{2,1,0:T(8,128)(2,1)S(1)}, u32[]{:S(2)}, u32[]{:S(2)}) collective-permute-start(bf16[3,64,512]{2,1,0:T(8,128)(2,1)S(1)} %get-tuple-element.150), channel_id=1, source_target_pairs={{0,8},{4,12},{8,0},{12,4},{16,24},{20,28},{24,16},{28,20},{1,9},{5... | collective-permute-start | bytes 589832 | tf_op jit(solution)/shard_map/ppermute | solution.py:403
  105.4 17.1 %collective-permute-start.34 = (bf16[3,64,512]{2,1,0:T(8,128)(2,1)S(1)}, bf16[3,64,512]{2,1,0:T(8,128)(2,1)S(1)}, u32[]{:S(2)}, u32[]{:S(2)}) collective-permute-start(bf16[3,64,512]{2,1,0:T(8,128)(2,1)S(1)} %get-tuple-element.151), channel_id=1, source_target_pairs={{0,16},{4,20},{8,24},{12,28},{16,0},{20,4},{24,8},{28,12},{1,17},{... | collective-permute-start | bytes 589832 | tf_op jit(solution)/shard_map/ppermute | solution.py:403
  107.2 15.3 %collective-permute-start.35 = (bf16[3,64,512]{2,1,0:T(8,128)(2,1)S(1)}, bf16[3,64,512]{2,1,0:T(8,128)(2,1)S(1)}, u32[]{:S(2)}, u32[]{:S(2)}) collective-permute-start(bf16[3,64,512]{2,1,0:T(8,128)(2,1)S(1)} %get-tuple-element.152), channel_id=1, source_target_pairs={{0,24},{4,28},{8,16},{12,20},{16,8},{20,12},{24,0},{28,4},{1,25},{... | collective-permute-start | bytes 589832 | tf_op jit(solution)/shard_map/ppermute | solution.py:403
  122.8 9.1 %collective-permute-start.36 = (bf16[3,64,512]{2,1,0:T(8,128)(2,1)S(1)}, bf16[3,64,512]{2,1,0:T(8,128)(2,1)S(1)}, u32[]{:S(2)}, u32[]{:S(2)}) collective-permute-start(bf16[3,64,512]{2,1,0:T(8,128)(2,1)S(1)} %shard_map.57.refs_0_), channel_id=1, source_target_pairs={{0,8},{4,12},{8,0},{12,4},{16,24},{20,28},{24,16},{28,20},{1,9},{5... | collective-permute-start | bytes 589832 | tf_op jit(solution)/shard_map/ppermute | solution.py:403
  126.5 12.2 %collective-permute-start.38 = (bf16[3,64,512]{2,1,0:T(8,128)(2,1)S(1)}, bf16[3,64,512]{2,1,0:T(8,128)(2,1)S(1)}, u32[]{:S(2)}, u32[]{:S(2)}) collective-permute-start(bf16[3,64,512]{2,1,0:T(8,128)(2,1)S(1)} %shard_map.57.refs_0_), channel_id=1, source_target_pairs={{0,24},{4,28},{8,16},{12,20},{16,8},{20,12},{24,0},{28,4},{1,25},{... | collective-permute-start | bytes 589832 | tf_op jit(solution)/shard_map/ppermute | solution.py:403
  128.6 15.9 %collective-permute-start.37 = (bf16[3,64,512]{2,1,0:T(8,128)(2,1)S(1)}, bf16[3,64,512]{2,1,0:T(8,128)(2,1)S(1)}, u32[]{:S(2)}, u32[]{:S(2)}) collective-permute-start(bf16[3,64,512]{2,1,0:T(8,128)(2,1)S(1)} %shard_map.57.refs_0_), channel_id=1, source_target_pairs={{0,16},{4,20},{8,24},{12,28},{16,0},{20,4},{24,8},{28,12},{1,17},{... | collective-permute-start | bytes 589832 | tf_op jit(solution)/shard_map/ppermute | solution.py:403
  132.8 12.6 %collective-permute-start.39 = (bf16[3,128,256]{2,1,0:T(8,128)(2,1)S(1)}, bf16[3,128,256]{2,1,0:T(8,128)(2,1)S(1)}, u32[]{:S(2)}, u32[]{:S(2)}) collective-permute-start(bf16[3,128,256]{2,1,0:T(8,128)(2,1)S(1)} %get-tuple-element.154.a0), channel_id=1, source_target_pairs={{0,2},{1,3},{2,0},{3,1},{4,6},{5,7},{6,4},{7,5},{8,10},{9,11},{10,... | collective-permute-start | bytes 589832 | tf_op jit(solution)/shard_map/ppermute | solution.py:393
  134.6 10.9 %collective-permute-start.40 = (bf16[3,128,256]{2,1,0:T(8,128)(2,1)S(1)}, bf16[3,128,256]{2,1,0:T(8,128)(2,1)S(1)}, u32[]{:S(2)}, u32[]{:S(2)}) collective-permute-start(bf16[3,128,256]{2,1,0:T(8,128)(2,1)S(1)} %get-tuple-element.157), channel_id=1, source_target_pairs={{0,4},{4,0},{8,12},{12,8},{16,20},{20,16},{24,28},{28,24},{1,5},{5... | collective-permute-start | bytes 589832 | tf_op jit(solution)/shard_map/ppermute | solution.py:396
  136.3 12.7 %collective-permute-start.41 = (bf16[3,128,256]{2,1,0:T(8,128)(2,1)S(1)}, bf16[3,128,256]{2,1,0:T(8,128)(2,1)S(1)}, u32[]{:S(2)}, u32[]{:S(2)}) collective-permute-start(bf16[3,128,256]{2,1,0:T(8,128)(2,1)S(1)} %get-tuple-element.157), channel_id=1, source_target_pairs={{0,6},{1,7},{2,4},{3,5},{4,2},{5,3},{6,0},{7,1},{8,14},{9,15},{10,... | collective-permute-start | bytes 589832 | tf_op jit(solution)/shard_map/ppermute | solution.py:400
  146.7 9.0 %collective-permute-start.44 = (bf16[3,128,256]{2,1,0:T(8,128)(2,1)S(1)}, bf16[3,128,256]{2,1,0:T(8,128)(2,1)S(1)}, u32[]{:S(2)}, u32[]{:S(2)}) collective-permute-start(bf16[3,128,256]{2,1,0:T(8,128)(2,1)S(1)} %get-tuple-element.164), channel_id=1, source_target_pairs={{0,6},{1,7},{2,4},{3,5},{4,2},{5,3},{6,0},{7,1},{8,14},{9,15},{10,... | collective-permute-start | bytes 589832 | tf_op jit(solution)/shard_map/ppermute | solution.py:400
  148.2 8.8 %collective-permute-start.43 = (bf16[3,128,256]{2,1,0:T(8,128)(2,1)S(1)}, bf16[3,128,256]{2,1,0:T(8,128)(2,1)S(1)}, u32[]{:S(2)}, u32[]{:S(2)}) collective-permute-start(bf16[3,128,256]{2,1,0:T(8,128)(2,1)S(1)} %get-tuple-element.164), channel_id=1, source_target_pairs={{0,4},{4,0},{8,12},{12,8},{16,20},{20,16},{24,28},{28,24},{1,5},{5... | collective-permute-start | bytes 589832 | tf_op jit(solution)/shard_map/ppermute | solution.py:396
  (17 other events, 131.4 us)

commit v6 on v5

--- a/solution.py
+++ b/solution.py
@@ -95,9 +95,10 @@
     residues = queries[0].shape[1]
     for head in range(heads):
         near = dot_t(queries[0][head], keys[0][head]) + dot_t(queries[1][head], keys[1][head])
-        hold[:, :residues] = (near * scale).astype(hold.dtype)
         far = dot_t(queries[0][head], others[0][head]) + dot_t(queries[1][head], others[1][head])
-        hold[:, residues:] = (far * scale).astype(hold.dtype)
+        mean = (jnp.sum(near, axis=1, keepdims=True) + jnp.sum(far, axis=1, keepdims=True)) / (2 * residues)
+        hold[:, :residues] = ((near - mean) * scale).astype(hold.dtype)
+        hold[:, residues:] = ((far - mean) * scale).astype(hold.dtype)
         for d, out in enumerate(outs):
             start = pl.multiple_of(jnp.bitwise_xor(z, d) * rows, rows)
             out[head] = hold[pl.ds(start, rows), :].astype(BF16)
@@ -132,7 +133,8 @@
                 start = side * residues + jnp.bitwise_xor(high, g) * piece_rows
                 key_hold[pl.ds(pl.multiple_of(start, piece_rows), piece_rows), :] = ref[head]
         query = jnp.concatenate([ref[head] for ref in queries], axis=0)
-        scores = dot_t(query, key_hold[...]) * scale
+        scores = dot_t(query, key_hold[...])
+        scores = (scores - jnp.mean(scores, axis=1, keepdims=True)) * scale
         if each == 1:
             for g, out in enumerate(outs):
                 out[head] = scores[g * rows : (g + 1) * rows].astype(BF16)

time: 162 us -> 162 us (level)
  transfers between devices with their start and end apart: 47 -> 47, of which waited for: 22 -> 22; matrix products, arithmetic and copies ran while one was open for 3% -> 3% of each run, Pallas kernels for 14% -> 15%
where the time goes in v6:
time: 162 us
  waiting for transfers between devices  72.8 us (45%)
  starting transfers between devices  56 us (35%)
  Pallas kernels  25.6 us (16%)
  local copies, waits for them, and re-layouts  6.63 us (4%)
    ppermute x12, waiting for transfers between devices, over_z(): return lax.ppermute(a, 'rows', [(i, i ^ 2 * d) for i in range(n_rows)])  40.6 us
    ppermute x12, starting transfers between devices, over_z(): return lax.ppermute(a, 'rows', [(i, i ^ 2 * d) for i in range(n_rows)])  24.5 us
    ppermute x11, starting transfers between devices, over_x(): return lax.ppermute(a, 'heads', [(i, i ^ 2) for i in range(n_groups)])  14.7 us
    ppermute x11, waiting for transfers between devices, over_y(): return lax.ppermute(a, 'rows', [(i, i ^ 1) for i in range(n_rows)])  13.2 us
    ppermute x11, starting transfers between devices, over_y(): return lax.ppermute(a, 'rows', [(i, i ^ 1) for i in range(n_rows)])  13.2 us
    ppermute x11, waiting for transfers between devices, over_x(): return lax.ppermute(a, 'heads', [(i, i ^ 2) for i in range(n_groups)])  12.8 us
    pallas_call x2, Pallas kernels, next_layer(): pl.pallas_call(functools.partial(next_kernel, g), in_specs=[SMEM] + [FULL...  8.16 us
    pallas_call x2, Pallas kernels, first(): pl.pallas_call(first_kernel, in_specs=[SMEM] + [FULL] * 7, out_specs=[FUL...  4.91 us
  transfers between devices with their start and end apart: 47, of which 22 were waited for; matrix products, arithmetic and copies ran while one was open for 3% of the time, Pallas kernels for 15%

profile of v6, /device:TPU:0, one launch (start us, length us, event | category | flops | bytes accessed | tf_op | source)
XLA Modules:
  0.0 161.9 jit_solution(6388920221851337169)
XLA Ops:
  3.1 2.5 %collective-permute-start.1 = (bf16[2,256,384]{2,1,0:T(8,128)(2,1)S(1)}, bf16[2,256,384]{2,1,0:T(8,128)(2,1)S(1)}, u32[]{:S(2)}, u32[]{:S(2)}) collective-permute-start(bf16[2,256,384]{2,1,0:T(8,128)(2,1)S(1)} %pad_maximum_fusion.2.p0), channel_id=1, source_target_pairs={{0,2},{1,3},{2,0},{3,1},{4,6},{5,7},{6,4},{7,5},{8,10},{9,11},{10,... | collective-permute-start | bytes 1179656 | tf_op jit(solution)/shard_map/ppermute | solution.py:395
  8.8 6.7 %collective-permute-done.1.p2 = bf16[2,256,384]{2,1,0:T(8,128)(2,1)S(1)} collective-permute-done((bf16[2,256,384]{2,1,0:T(8,128)(2,1)S(1)}, bf16[2,256,384]{2,1,0:T(8,128)(2,1)S(1)}, u32[]{:S(2)}, u32[]{:S(2)}) %collective-permute-start.1) | collective-permute-done | bytes 393248 | tf_op jit(solution)/shard_map/ppermute | solution.py:395
  15.6 2.0 %collective-permute-start.5 = (bf16[2,256,384]{2,1,0:T(8,128)(2,1)S(1)}, bf16[2,256,384]{2,1,0:T(8,128)(2,1)S(1)}, u32[]{:S(2)}, u32[]{:S(2)}) collective-permute-start(bf16[2,256,384]{2,1,0:T(8,128)(2,1)S(1)} %collective-permute-done.1.p2), channel_id=1, source_target_pairs={{0,4},{4,0},{8,12},{12,8},{16,20},{20,16},{24,28},{28,24},{1,5},{5... | collective-permute-start | bytes 1179656 | tf_op jit(solution)/shard_map/ppermute | solution.py:398
  19.0 2.0 %dynamic-slice_bitcast_fusion.3 = (bf16[768,192]{1,0:T(8,128)(2,1)S(1)}, bf16[768,192]{1,0:T(8,128)(2,1)S(1)}, bf16[768,192]{1,0:T(8,128)(2,1)S(1)}) fusion(bf16[2,768,3,768]{3,1,2,0:T(8,128)(2,1)} %param.5, u32[]{:T(128)S(6)} %mul.25), kind=kLoop, calls=%fused_computation.7 | loop fusion | bytes 1769476 | tf_op jit(solution)/shard_map/reshape | solution.py:411
  21.0 3.0 %collective-permute-done.2.p3 = bf16[2,256,384]{2,1,0:T(8,128)(2,1)S(1)} collective-permute-done((bf16[2,256,384]{2,1,0:T(8,128)(2,1)S(1)}, bf16[2,256,384]{2,1,0:T(8,128)(2,1)S(1)}, u32[]{:S(2)}, u32[]{:S(2)}) %collective-permute-start.2) | collective-permute-done | bytes 393248 | tf_op jit(solution)/shard_map/ppermute | solution.py:395
  24.0 2.5 %shard_map.46 = (bf16[4,256,768]{2,1,0:T(8,128)(2,1)S(1)}, bf16[3,256,256]{2,1,0:T(8,128)(2,1)S(1)}, bf16[3,256,256]{2,1,0:T(8,128)(2,1)S(1)}, bf16[3,256,256]{2,1,0:T(8,128)(2,1)S(1)}) custom-call(s32[5]{0:T(128)S(1)} %convert_element_type.15.place, bf16[2,256,384]{2,1,0:T(8,128)(2,1)S(1)} %pad_maximum_fusion.2.p0, ...), custom_call_target="tpu_custom_call" | custom-call | flops 905969664 | bytes 9830400 | tf_op jit(solution)/shard_map/pallas_call | solution.py:81
  26.5 7.1 %collective-permute-done.5.p2 = bf16[2,256,384]{2,1,0:T(8,128)(2,1)S(1)} collective-permute-done((bf16[2,256,384]{2,1,0:T(8,128)(2,1)S(1)}, bf16[2,256,384]{2,1,0:T(8,128)(2,1)S(1)}, u32[]{:S(2)}, u32[]{:S(2)}) %collective-permute-start.5) | collective-permute-done | bytes 393248 | tf_op jit(solution)/shard_map/ppermute | solution.py:398
  33.7 2.4 %shard_map.47 = (bf16[4,256,768]{2,1,0:T(8,128)(2,1)S(1)}, bf16[3,256,256]{2,1,0:T(8,128)(2,1)S(1)}, bf16[3,256,256]{2,1,0:T(8,128)(2,1)S(1)}, bf16[3,256,256]{2,1,0:T(8,128)(2,1)S(1)}) custom-call(s32[5]{0:T(128)S(1)} %convert_element_type.15.place, bf16[2,256,384]{2,1,0:T(8,128)(2,1)S(1)} %collective-permute-done.3.p0, ...), custom_call_target="tpu_custom_call" | custom-call | flops 905969664 | bytes 9830400 | tf_op jit(solution)/shard_map/pallas_call | solution.py:81
  40.8 2.6 %collective-permute-start.12 = (bf16[3,64,512]{2,1,0:T(8,128)(2,1)S(1)}, bf16[3,64,512]{2,1,0:T(8,128)(2,1)S(1)}, u32[]{:S(2)}, u32[]{:S(2)}) collective-permute-start(bf16[3,64,512]{2,1,0:T(8,128)(2,1)S(1)} %get-tuple-element.110), channel_id=1, source_target_pairs={{0,16},{4,20},{8,24},{12,28},{16,0},{20,4},{24,8},{28,12},{1,17},{... | collective-permute-start | bytes 589832 | tf_op jit(solution)/shard_map/ppermute | solution.py:405
  43.6 2.0 %dynamic-slice_bitcast_fusion = (bf16[768,192]{1,0:T(8,128)(2,1)S(1)}, bf16[768,192]{1,0:T(8,128)(2,1)S(1)}, bf16[768,192]{1,0:T(8,128)(2,1)S(1)}) fusion(bf16[2,768,3,768]{3,1,2,0:T(8,128)(2,1)} %param.5, u32[]{:T(128)S(6)} %mul.25), kind=kLoop, calls=%fused_computation.4 | loop fusion | bytes 1769476 | tf_op jit(solution)/shard_map/reshape | solution.py:411
  46.3 3.5 %collective-permute-done.11.refs_1_ = bf16[3,64,512]{2,1,0:T(8,128)(2,1)S(1)} collective-permute-done((bf16[3,64,512]{2,1,0:T(8,128)(2,1)S(1)}, bf16[3,64,512]{2,1,0:T(8,128)(2,1)S(1)}, u32[]{:S(2)}, u32[]{:S(2)}) %collective-permute-start.11) | collective-permute-done | bytes 196640 | tf_op jit(solution)/shard_map/ppermute | solution.py:405
  49.8 8.1 %collective-permute-done.12.refs_2_ = bf16[3,64,512]{2,1,0:T(8,128)(2,1)S(1)} collective-permute-done((bf16[3,64,512]{2,1,0:T(8,128)(2,1)S(1)}, bf16[3,64,512]{2,1,0:T(8,128)(2,1)S(1)}, u32[]{:S(2)}, u32[]{:S(2)}) %collective-permute-start.12) | collective-permute-done | bytes 196640 | tf_op jit(solution)/shard_map/ppermute | solution.py:405
  58.2 3.8 %collective-permute-start.16 = (bf16[3,64,512]{2,1,0:T(8,128)(2,1)S(1)}, bf16[3,64,512]{2,1,0:T(8,128)(2,1)S(1)}, u32[]{:S(2)}, u32[]{:S(2)}) collective-permute-start(bf16[3,64,512]{2,1,0:T(8,128)(2,1)S(1)} %shard_map.50.refs_0_), channel_id=1, source_target_pairs={{0,8},{4,12},{8,0},{12,4},{16,24},{20,28},{24,16},{28,20},{1,9},{5... | collective-permute-start | bytes 589832 | tf_op jit(solution)/shard_map/ppermute | solution.py:405
  62.0 2.5 %collective-permute-start.15 = (bf16[3,64,512]{2,1,0:T(8,128)(2,1)S(1)}, bf16[3,64,512]{2,1,0:T(8,128)(2,1)S(1)}, u32[]{:S(2)}, u32[]{:S(2)}) collective-permute-start(bf16[3,64,512]{2,1,0:T(8,128)(2,1)S(1)} %shard_map.50.refs_0_), channel_id=1, source_target_pairs={{0,24},{4,28},{8,16},{12,20},{16,8},{20,12},{24,0},{28,4},{1,25},{... | collective-permute-start | bytes 589832 | tf_op jit(solution)/shard_map/ppermute | solution.py:405
  64.5 2.9 %collective-permute-done.16.refs_1_ = bf16[3,64,512]{2,1,0:T(8,128)(2,1)S(1)} collective-permute-done((bf16[3,64,512]{2,1,0:T(8,128)(2,1)S(1)}, bf16[3,64,512]{2,1,0:T(8,128)(2,1)S(1)}, u32[]{:S(2)}, u32[]{:S(2)}) %collective-permute-start.16) | collective-permute-done | bytes 196640 | tf_op jit(solution)/shard_map/ppermute | solution.py:405
  71.0 3.5 %collective-permute-start.14 = (bf16[3,64,512]{2,1,0:T(8,128)(2,1)S(1)}, bf16[3,64,512]{2,1,0:T(8,128)(2,1)S(1)}, u32[]{:S(2)}, u32[]{:S(2)}) collective-permute-start(bf16[3,64,512]{2,1,0:T(8,128)(2,1)S(1)} %shard_map.50.refs_0_), channel_id=1, source_target_pairs={{0,16},{4,20},{8,24},{12,28},{16,0},{20,4},{24,8},{28,12},{1,17},{... | collective-permute-start | bytes 589832 | tf_op jit(solution)/shard_map/ppermute | solution.py:405
  78.5 2.4 %collective-permute-done.14.refs_0_ = bf16[3,64,512]{2,1,0:T(8,128)(2,1)S(1)} collective-permute-done((bf16[3,64,512]{2,1,0:T(8,128)(2,1)S(1)}, bf16[3,64,512]{2,1,0:T(8,128)(2,1)S(1)}, u32[]{:S(2)}, u32[]{:S(2)}) %collective-permute-start.14) | collective-permute-done | bytes 196640 | tf_op jit(solution)/shard_map/ppermute | solution.py:405
  86.0 4.2 %shard_map.53 = (bf16[4,128,768]{2,1,0:T(8,128)(2,1)S(1)}, bf16[3,128,512]{2,1,0:T(8,128)(2,1)S(1)}, bf16[3,128,512]{2,1,0:T(8,128)(2,1)S(1)}, bf16[3,128,512]{2,1,0:T(8,128)(2,1)S(1)}) custom-call(s32[5]{0:T(128)S(1)} %convert_element_type.15.place, bf16[3,128,256]{2,1,0:T(8,128)(2,1)S(1)} %get-tuple-element.115.refs_0_, ...), custom_call_target="tpu_custom_call" | custom-call | flops 2113929216 | bytes 5210112 | tf_op jit(solution)/shard_map/pallas_call | solution.py:304
  94.9 2.3 %collective-permute-done.28.refs_7_ = bf16[3,128,256]{2,1,0:T(8,128)(2,1)S(1)} collective-permute-done((bf16[3,128,256]{2,1,0:T(8,128)(2,1)S(1)}, bf16[3,128,256]{2,1,0:T(8,128)(2,1)S(1)}, u32[]{:S(2)}, u32[]{:S(2)}) %collective-permute-start.28) | collective-permute-done | bytes 196640 | tf_op jit(solution)/shard_map/ppermute | solution.py:398
  97.8 4.0 %shard_map.54 = (bf16[4,128,768]{2,1,0:T(8,128)(2,1)S(1)}, bf16[3,128,512]{2,1,0:T(8,128)(2,1)S(1)}, bf16[3,128,512]{2,1,0:T(8,128)(2,1)S(1)}, bf16[3,128,512]{2,1,0:T(8,128)(2,1)S(1)}) custom-call(s32[5]{0:T(128)S(1)} %convert_element_type.15.place, bf16[3,128,256]{2,1,0:T(8,128)(2,1)S(1)} %get-tuple-element.137.refs_0_, ...), custom_call_target="tpu_custom_call" | custom-call | flops 2113929216 | bytes 5210112 | tf_op jit(solution)/shard_map/pallas_call | solution.py:304
  105.5 1.8 %collective-permute-start.34 = (bf16[3,64,512]{2,1,0:T(8,128)(2,1)S(1)}, bf16[3,64,512]{2,1,0:T(8,128)(2,1)S(1)}, u32[]{:S(2)}, u32[]{:S(2)}) collective-permute-start(bf16[3,64,512]{2,1,0:T(8,128)(2,1)S(1)} %get-tuple-element.151), channel_id=1, source_target_pairs={{0,16},{4,20},{8,24},{12,28},{16,0},{20,4},{24,8},{28,12},{1,17},{... | collective-permute-start | bytes 589832 | tf_op jit(solution)/shard_map/ppermute | solution.py:405
  107.4 2.1 %collective-permute-start.35 = (bf16[3,64,512]{2,1,0:T(8,128)(2,1)S(1)}, bf16[3,64,512]{2,1,0:T(8,128)(2,1)S(1)}, u32[]{:S(2)}, u32[]{:S(2)}) collective-permute-start(bf16[3,64,512]{2,1,0:T(8,128)(2,1)S(1)} %get-tuple-element.152), channel_id=1, source_target_pairs={{0,24},{4,28},{8,16},{12,20},{16,8},{20,12},{24,0},{28,4},{1,25},{... | collective-permute-start | bytes 589832 | tf_op jit(solution)/shard_map/ppermute | solution.py:405
  110.5 4.9 %collective-permute-done.33.refs_1_ = bf16[3,64,512]{2,1,0:T(8,128)(2,1)S(1)} collective-permute-done((bf16[3,64,512]{2,1,0:T(8,128)(2,1)S(1)}, bf16[3,64,512]{2,1,0:T(8,128)(2,1)S(1)}, u32[]{:S(2)}, u32[]{:S(2)}) %collective-permute-start.33) | collective-permute-done | bytes 196640 | tf_op jit(solution)/shard_map/ppermute | solution.py:405
  115.4 7.3 %collective-permute-done.34.refs_2_ = bf16[3,64,512]{2,1,0:T(8,128)(2,1)S(1)} collective-permute-done((bf16[3,64,512]{2,1,0:T(8,128)(2,1)S(1)}, bf16[3,64,512]{2,1,0:T(8,128)(2,1)S(1)}, u32[]{:S(2)}, u32[]{:S(2)}) %collective-permute-start.34) | collective-permute-done | bytes 196640 | tf_op jit(solution)/shard_map/ppermute | solution.py:405
  122.9 3.8 %collective-permute-start.36 = (bf16[3,64,512]{2,1,0:T(8,128)(2,1)S(1)}, bf16[3,64,512]{2,1,0:T(8,128)(2,1)S(1)}, u32[]{:S(2)}, u32[]{:S(2)}) collective-permute-start(bf16[3,64,512]{2,1,0:T(8,128)(2,1)S(1)} %shard_map.57.refs_0_), channel_id=1, source_target_pairs={{0,8},{4,12},{8,0},{12,4},{16,24},{20,28},{24,16},{28,20},{1,9},{5... | collective-permute-start | bytes 589832 | tf_op jit(solution)/shard_map/ppermute | solution.py:405
  126.7 2.1 %collective-permute-start.38 = (bf16[3,64,512]{2,1,0:T(8,128)(2,1)S(1)}, bf16[3,64,512]{2,1,0:T(8,128)(2,1)S(1)}, u32[]{:S(2)}, u32[]{:S(2)}) collective-permute-start(bf16[3,64,512]{2,1,0:T(8,128)(2,1)S(1)} %shard_map.57.refs_0_), channel_id=1, source_target_pairs={{0,24},{4,28},{8,16},{12,20},{16,8},{20,12},{24,0},{28,4},{1,25},{... | collective-permute-start | bytes 589832 | tf_op jit(solution)/shard_map/ppermute | solution.py:405
  128.8 3.3 %collective-permute-done.36.refs_1_ = bf16[3,64,512]{2,1,0:T(8,128)(2,1)S(1)} collective-permute-done((bf16[3,64,512]{2,1,0:T(8,128)(2,1)S(1)}, bf16[3,64,512]{2,1,0:T(8,128)(2,1)S(1)}, u32[]{:S(2)}, u32[]{:S(2)}) %collective-permute-start.36) | collective-permute-done | bytes 196640 | tf_op jit(solution)/shard_map/ppermute | solution.py:405
  133.0 1.9 %collective-permute-start.39 = (bf16[3,128,256]{2,1,0:T(8,128)(2,1)S(1)}, bf16[3,128,256]{2,1,0:T(8,128)(2,1)S(1)}, u32[]{:S(2)}, u32[]{:S(2)}) collective-permute-start(bf16[3,128,256]{2,1,0:T(8,128)(2,1)S(1)} %get-tuple-element.154.a0), channel_id=1, source_target_pairs={{0,2},{1,3},{2,0},{3,1},{4,6},{5,7},{6,4},{7,5},{8,10},{9,11},{10,... | collective-permute-start | bytes 589832 | tf_op jit(solution)/shard_map/ppermute | solution.py:395
  136.5 2.4 %collective-permute-done.38.refs_1_ = bf16[3,64,512]{2,1,0:T(8,128)(2,1)S(1)} collective-permute-done((bf16[3,64,512]{2,1,0:T(8,128)(2,1)S(1)}, bf16[3,64,512]{2,1,0:T(8,128)(2,1)S(1)}, u32[]{:S(2)}, u32[]{:S(2)}) %collective-permute-start.38) | collective-permute-done | bytes 196640 | tf_op jit(solution)/shard_map/ppermute | solution.py:405
  138.9 5.8 %collective-permute-done.37.refs_0_ = bf16[3,64,512]{2,1,0:T(8,128)(2,1)S(1)} collective-permute-done((bf16[3,64,512]{2,1,0:T(8,128)(2,1)S(1)}, bf16[3,64,512]{2,1,0:T(8,128)(2,1)S(1)}, u32[]{:S(2)}, u32[]{:S(2)}) %collective-permute-start.37) | collective-permute-done | bytes 196640 | tf_op jit(solution)/shard_map/ppermute | solution.py:405
  150.9 2.4 %collective-permute-done.42.a1 = bf16[3,128,256]{2,1,0:T(8,128)(2,1)S(1)} collective-permute-done((bf16[3,128,256]{2,1,0:T(8,128)(2,1)S(1)}, bf16[3,128,256]{2,1,0:T(8,128)(2,1)S(1)}, u32[]{:S(2)}, u32[]{:S(2)}) %collective-permute-start.42) | collective-permute-done | bytes 196640 | tf_op jit(solution)/shard_map/ppermute | solution.py:395
  153.3 2.5 %collective-permute-done.44.a3 = bf16[3,128,256]{2,1,0:T(8,128)(2,1)S(1)} collective-permute-done((bf16[3,128,256]{2,1,0:T(8,128)(2,1)S(1)}, bf16[3,128,256]{2,1,0:T(8,128)(2,1)S(1)}, u32[]{:S(2)}, u32[]{:S(2)}) %collective-permute-start.44) | collective-permute-done | bytes 196640 | tf_op jit(solution)/shard_map/ppermute | solution.py:402
  (99 shorter events, 51.6 us)
Async XLA Ops:
  3.1 12.5 %collective-permute-start.1 = (bf16[2,256,384]{2,1,0:T(8,128)(2,1)S(1)}, bf16[2,256,384]{2,1,0:T(8,128)(2,1)S(1)}, u32[]{:S(2)}, u32[]{:S(2)}) collective-permute-start(bf16[2,256,384]{2,1,0:T(8,128)(2,1)S(1)} %pad_maximum_fusion.2.p0), channel_id=1, source_target_pairs={{0,2},{1,3},{2,0},{3,1},{4,6},{5,7},{6,4},{7,5},{8,10},{9,11},{10,... | collective-permute-start | bytes 1179656 | tf_op jit(solution)/shard_map/ppermute | solution.py:395
  5.6 11.9 %collective-permute-start.4 = (bf16[2,256,384]{2,1,0:T(8,128)(2,1)S(1)}, bf16[2,256,384]{2,1,0:T(8,128)(2,1)S(1)}, u32[]{:S(2)}, u32[]{:S(2)}) collective-permute-start(bf16[2,256,384]{2,1,0:T(8,128)(2,1)S(1)} %collective-permute-done.p1), channel_id=1, source_target_pairs={{0,4},{4,0},{8,12},{12,8},{16,20},{20,16},{24,28},{28,24},{1,5},{5... | collective-permute-start | bytes 1179656 | tf_op jit(solution)/shard_map/ppermute | solution.py:398
  7.1 16.9 %collective-permute-start.2 = (bf16[2,256,384]{2,1,0:T(8,128)(2,1)S(1)}, bf16[2,256,384]{2,1,0:T(8,128)(2,1)S(1)}, u32[]{:S(2)}, u32[]{:S(2)}) collective-permute-start(bf16[2,256,384]{2,1,0:T(8,128)(2,1)S(1)} %collective-permute-done.p1), channel_id=1, source_target_pairs={{0,2},{1,3},{2,0},{3,1},{4,6},{5,7},{6,4},{7,5},{8,10},{9,11},{10,... | collective-permute-start | bytes 1179656 | tf_op jit(solution)/shard_map/ppermute | solution.py:395
  8.3 18.2 %collective-permute-start.3 = (bf16[2,256,384]{2,1,0:T(8,128)(2,1)S(1)}, bf16[2,256,384]{2,1,0:T(8,128)(2,1)S(1)}, u32[]{:S(2)}, u32[]{:S(2)}) collective-permute-start(bf16[2,256,384]{2,1,0:T(8,128)(2,1)S(1)} %pad_maximum_fusion.2.p0), channel_id=1, source_target_pairs={{0,4},{4,0},{8,12},{12,8},{16,20},{20,16},{24,28},{28,24},{1,5},{5... | collective-permute-start | bytes 1179656 | tf_op jit(solution)/shard_map/ppermute | solution.py:398
  15.6 18.1 %collective-permute-start.5 = (bf16[2,256,384]{2,1,0:T(8,128)(2,1)S(1)}, bf16[2,256,384]{2,1,0:T(8,128)(2,1)S(1)}, u32[]{:S(2)}, u32[]{:S(2)}) collective-permute-start(bf16[2,256,384]{2,1,0:T(8,128)(2,1)S(1)} %collective-permute-done.1.p2), channel_id=1, source_target_pairs={{0,4},{4,0},{8,12},{12,8},{16,20},{20,16},{24,28},{28,24},{1,5},{5... | collective-permute-start | bytes 1179656 | tf_op jit(solution)/shard_map/ppermute | solution.py:398
  17.5 16.1 %collective-permute-start.6 = (bf16[2,256,384]{2,1,0:T(8,128)(2,1)S(1)}, bf16[2,256,384]{2,1,0:T(8,128)(2,1)S(1)}, u32[]{:S(2)}, u32[]{:S(2)}) collective-permute-start(bf16[2,256,384]{2,1,0:T(8,128)(2,1)S(1)} %collective-permute-done.4.p1), channel_id=1, source_target_pairs={{0,2},{1,3},{2,0},{3,1},{4,6},{5,7},{6,4},{7,5},{8,10},{9,11},{10,... | collective-permute-start | bytes 1179656 | tf_op jit(solution)/shard_map/ppermute | solution.py:395
  26.4 10.3 %collective-permute-start.7 = (bf16[3,256,256]{2,1,0:T(8,128)(2,1)S(1)}, bf16[3,256,256]{2,1,0:T(8,128)(2,1)S(1)}, u32[]{:S(2)}, u32[]{:S(2)}) collective-permute-start(bf16[3,256,256]{2,1,0:T(8,128)(2,1)S(1)} %get-tuple-element.97.refs_2_), channel_id=1, source_target_pairs={{0,1},{1,0},{2,3},{3,2},{4,5},{5,4},{6,7},{7,6},{8,9},{9,8},{10,11... | collective-permute-start | bytes 1179656 | tf_op jit(solution)/shard_map/ppermute | solution.py:392
  36.2 9.7 %collective-permute-start.9 = (bf16[3,256,256]{2,1,0:T(8,128)(2,1)S(1)}, bf16[3,256,256]{2,1,0:T(8,128)(2,1)S(1)}, u32[]{:S(2)}, u32[]{:S(2)}) collective-permute-start(bf16[3,256,256]{2,1,0:T(8,128)(2,1)S(1)} %get-tuple-element.106.near), channel_id=1, source_target_pairs={{0,1},{1,0},{2,3},{3,2},{4,5},{5,4},{6,7},{7,6},{8,9},{9,8},{10,11... | collective-permute-start | bytes 1179656 | tf_op jit(solution)/shard_map/ppermute | solution.py:392
  36.7 9.2 %collective-permute-start.10 = (bf16[3,256,256]{2,1,0:T(8,128)(2,1)S(1)}, bf16[3,256,256]{2,1,0:T(8,128)(2,1)S(1)}, u32[]{:S(2)}, u32[]{:S(2)}) collective-permute-start(bf16[3,256,256]{2,1,0:T(8,128)(2,1)S(1)} %get-tuple-element.107.far), channel_id=1, source_target_pairs={{0,1},{1,0},{2,3},{3,2},{4,5},{5,4},{6,7},{7,6},{8,9},{9,8},{10,11... | collective-permute-start | bytes 1179656 | tf_op jit(solution)/shard_map/ppermute | solution.py:392
  39.2 10.6 %collective-permute-start.11 = (bf16[3,64,512]{2,1,0:T(8,128)(2,1)S(1)}, bf16[3,64,512]{2,1,0:T(8,128)(2,1)S(1)}, u32[]{:S(2)}, u32[]{:S(2)}) collective-permute-start(bf16[3,64,512]{2,1,0:T(8,128)(2,1)S(1)} %get-tuple-element.109), channel_id=1, source_target_pairs={{0,8},{4,12},{8,0},{12,4},{16,24},{20,28},{24,16},{28,20},{1,9},{5... | collective-permute-start | bytes 589832 | tf_op jit(solution)/shard_map/ppermute | solution.py:405
  40.8 17.1 %collective-permute-start.12 = (bf16[3,64,512]{2,1,0:T(8,128)(2,1)S(1)}, bf16[3,64,512]{2,1,0:T(8,128)(2,1)S(1)}, u32[]{:S(2)}, u32[]{:S(2)}) collective-permute-start(bf16[3,64,512]{2,1,0:T(8,128)(2,1)S(1)} %get-tuple-element.110), channel_id=1, source_target_pairs={{0,16},{4,20},{8,24},{12,28},{16,0},{20,4},{24,8},{28,12},{1,17},{... | collective-permute-start | bytes 589832 | tf_op jit(solution)/shard_map/ppermute | solution.py:405
  43.4 14.5 %collective-permute-start.13 = (bf16[3,64,512]{2,1,0:T(8,128)(2,1)S(1)}, bf16[3,64,512]{2,1,0:T(8,128)(2,1)S(1)}, u32[]{:S(2)}, u32[]{:S(2)}) collective-permute-start(bf16[3,64,512]{2,1,0:T(8,128)(2,1)S(1)} %get-tuple-element.111), channel_id=1, source_target_pairs={{0,24},{4,28},{8,16},{12,20},{16,8},{20,12},{24,0},{28,4},{1,25},{... | collective-permute-start | bytes 589832 | tf_op jit(solution)/shard_map/ppermute | solution.py:405
  58.2 9.1 %collective-permute-start.16 = (bf16[3,64,512]{2,1,0:T(8,128)(2,1)S(1)}, bf16[3,64,512]{2,1,0:T(8,128)(2,1)S(1)}, u32[]{:S(2)}, u32[]{:S(2)}) collective-permute-start(bf16[3,64,512]{2,1,0:T(8,128)(2,1)S(1)} %shard_map.50.refs_0_), channel_id=1, source_target_pairs={{0,8},{4,12},{8,0},{12,4},{16,24},{20,28},{24,16},{28,20},{1,9},{5... | collective-permute-start | bytes 589832 | tf_op jit(solution)/shard_map/ppermute | solution.py:405
  62.0 13.0 %collective-permute-start.15 = (bf16[3,64,512]{2,1,0:T(8,128)(2,1)S(1)}, bf16[3,64,512]{2,1,0:T(8,128)(2,1)S(1)}, u32[]{:S(2)}, u32[]{:S(2)}) collective-permute-start(bf16[3,64,512]{2,1,0:T(8,128)(2,1)S(1)} %shard_map.50.refs_0_), channel_id=1, source_target_pairs={{0,24},{4,28},{8,16},{12,20},{16,8},{20,12},{24,0},{28,4},{1,25},{... | collective-permute-start | bytes 589832 | tf_op jit(solution)/shard_map/ppermute | solution.py:405
  71.0 9.9 %collective-permute-start.14 = (bf16[3,64,512]{2,1,0:T(8,128)(2,1)S(1)}, bf16[3,64,512]{2,1,0:T(8,128)(2,1)S(1)}, u32[]{:S(2)}, u32[]{:S(2)}) collective-permute-start(bf16[3,64,512]{2,1,0:T(8,128)(2,1)S(1)} %shard_map.50.refs_0_), channel_id=1, source_target_pairs={{0,16},{4,20},{8,24},{12,28},{16,0},{20,4},{24,8},{28,12},{1,17},{... | collective-permute-start | bytes 589832 | tf_op jit(solution)/shard_map/ppermute | solution.py:405
  75.0 9.3 %collective-permute-start.22 = (bf16[3,128,256]{2,1,0:T(8,128)(2,1)S(1)}, bf16[3,128,256]{2,1,0:T(8,128)(2,1)S(1)}, u32[]{:S(2)}, u32[]{:S(2)}) collective-permute-start(bf16[3,128,256]{2,1,0:T(8,128)(2,1)S(1)} %get-tuple-element.116.refs_4_), channel_id=1, source_target_pairs={{0,2},{1,3},{2,0},{3,1},{4,6},{5,7},{6,4},{7,5},{8,10},{9,11},{10,... | collective-permute-start | bytes 589832 | tf_op jit(solution)/shard_map/ppermute | solution.py:395
  75.9 9.5 %collective-permute-start.24 = (bf16[3,128,256]{2,1,0:T(8,128)(2,1)S(1)}, bf16[3,128,256]{2,1,0:T(8,128)(2,1)S(1)}, u32[]{:S(2)}, u32[]{:S(2)}) collective-permute-start(bf16[3,128,256]{2,1,0:T(8,128)(2,1)S(1)} %collective-permute-done.17.refs_1_), channel_id=1, source_target_pairs={{0,4},{4,0},{8,12},{12,8},{16,20},{20,16},{24,28},{28,24},{1,5},{5... | collective-permute-start | bytes 589832 | tf_op jit(solution)/shard_map/ppermute | solution.py:398
  77.4 8.6 %collective-permute-start.21 = (bf16[3,128,256]{2,1,0:T(8,128)(2,1)S(1)}, bf16[3,128,256]{2,1,0:T(8,128)(2,1)S(1)}, u32[]{:S(2)}, u32[]{:S(2)}) collective-permute-start(bf16[3,128,256]{2,1,0:T(8,128)(2,1)S(1)} %collective-permute-done.18.refs_2_), channel_id=1, source_target_pairs={{0,2},{1,3},{2,0},{3,1},{4,6},{5,7},{6,4},{7,5},{8,10},{9,11},{10,... | collective-permute-start | bytes 589832 | tf_op jit(solution)/shard_map/ppermute | solution.py:395
  84.3 8.9 %collective-permute-start.26 = (bf16[3,128,256]{2,1,0:T(8,128)(2,1)S(1)}, bf16[3,128,256]{2,1,0:T(8,128)(2,1)S(1)}, u32[]{:S(2)}, u32[]{:S(2)}) collective-permute-start(bf16[3,128,256]{2,1,0:T(8,128)(2,1)S(1)} %get-tuple-element.136.refs_4_), channel_id=1, source_target_pairs={{0,2},{1,3},{2,0},{3,1},{4,6},{5,7},{6,4},{7,5},{8,10},{9,11},{10,... | collective-permute-start | bytes 589832 | tf_op jit(solution)/shard_map/ppermute | solution.py:395
  85.3 9.5 %collective-permute-start.27 = (bf16[3,128,256]{2,1,0:T(8,128)(2,1)S(1)}, bf16[3,128,256]{2,1,0:T(8,128)(2,1)S(1)}, u32[]{:S(2)}, u32[]{:S(2)}) collective-permute-start(bf16[3,128,256]{2,1,0:T(8,128)(2,1)S(1)} %get-tuple-element.137.refs_0_), channel_id=1, source_target_pairs={{0,4},{4,0},{8,12},{12,8},{16,20},{20,16},{24,28},{28,24},{1,5},{5... | collective-permute-start | bytes 589832 | tf_op jit(solution)/shard_map/ppermute | solution.py:398
  93.2 9.3 %collective-permute-start.29 = (bf16[3,128,512]{2,1,0:T(8,128)(2,1)S(1)}, bf16[3,128,512]{2,1,0:T(8,128)(2,1)S(1)}, u32[]{:S(2)}, u32[]{:S(2)}) collective-permute-start(bf16[3,128,512]{2,1,0:T(8,128)(2,1)S(1)} %get-tuple-element.139.refs_2_), channel_id=1, source_target_pairs={{0,1},{1,0},{2,3},{3,2},{4,5},{5,4},{6,7},{7,6},{8,9},{9,8},{10,11... | collective-permute-start | bytes 1179656 | tf_op jit(solution)/shard_map/ppermute | solution.py:392
  105.0 10.4 %collective-permute-start.33 = (bf16[3,64,512]{2,1,0:T(8,128)(2,1)S(1)}, bf16[3,64,512]{2,1,0:T(8,128)(2,1)S(1)}, u32[]{:S(2)}, u32[]{:S(2)}) collective-permute-start(bf16[3,64,512]{2,1,0:T(8,128)(2,1)S(1)} %get-tuple-element.150), channel_id=1, source_target_pairs={{0,8},{4,12},{8,0},{12,4},{16,24},{20,28},{24,16},{28,20},{1,9},{5... | collective-permute-start | bytes 589832 | tf_op jit(solution)/shard_map/ppermute | solution.py:405
  105.5 17.1 %collective-permute-start.34 = (bf16[3,64,512]{2,1,0:T(8,128)(2,1)S(1)}, bf16[3,64,512]{2,1,0:T(8,128)(2,1)S(1)}, u32[]{:S(2)}, u32[]{:S(2)}) collective-permute-start(bf16[3,64,512]{2,1,0:T(8,128)(2,1)S(1)} %get-tuple-element.151), channel_id=1, source_target_pairs={{0,16},{4,20},{8,24},{12,28},{16,0},{20,4},{24,8},{28,12},{1,17},{... | collective-permute-start | bytes 589832 | tf_op jit(solution)/shard_map/ppermute | solution.py:405
  107.4 15.3 %collective-permute-start.35 = (bf16[3,64,512]{2,1,0:T(8,128)(2,1)S(1)}, bf16[3,64,512]{2,1,0:T(8,128)(2,1)S(1)}, u32[]{:S(2)}, u32[]{:S(2)}) collective-permute-start(bf16[3,64,512]{2,1,0:T(8,128)(2,1)S(1)} %get-tuple-element.152), channel_id=1, source_target_pairs={{0,24},{4,28},{8,16},{12,20},{16,8},{20,12},{24,0},{28,4},{1,25},{... | collective-permute-start | bytes 589832 | tf_op jit(solution)/shard_map/ppermute | solution.py:405
  122.9 9.1 %collective-permute-start.36 = (bf16[3,64,512]{2,1,0:T(8,128)(2,1)S(1)}, bf16[3,64,512]{2,1,0:T(8,128)(2,1)S(1)}, u32[]{:S(2)}, u32[]{:S(2)}) collective-permute-start(bf16[3,64,512]{2,1,0:T(8,128)(2,1)S(1)} %shard_map.57.refs_0_), channel_id=1, source_target_pairs={{0,8},{4,12},{8,0},{12,4},{16,24},{20,28},{24,16},{28,20},{1,9},{5... | collective-permute-start | bytes 589832 | tf_op jit(solution)/shard_map/ppermute | solution.py:405
  126.7 12.2 %collective-permute-start.38 = (bf16[3,64,512]{2,1,0:T(8,128)(2,1)S(1)}, bf16[3,64,512]{2,1,0:T(8,128)(2,1)S(1)}, u32[]{:S(2)}, u32[]{:S(2)}) collective-permute-start(bf16[3,64,512]{2,1,0:T(8,128)(2,1)S(1)} %shard_map.57.refs_0_), channel_id=1, source_target_pairs={{0,24},{4,28},{8,16},{12,20},{16,8},{20,12},{24,0},{28,4},{1,25},{... | collective-permute-start | bytes 589832 | tf_op jit(solution)/shard_map/ppermute | solution.py:405
  128.7 15.9 %collective-permute-start.37 = (bf16[3,64,512]{2,1,0:T(8,128)(2,1)S(1)}, bf16[3,64,512]{2,1,0:T(8,128)(2,1)S(1)}, u32[]{:S(2)}, u32[]{:S(2)}) collective-permute-start(bf16[3,64,512]{2,1,0:T(8,128)(2,1)S(1)} %shard_map.57.refs_0_), channel_id=1, source_target_pairs={{0,16},{4,20},{8,24},{12,28},{16,0},{20,4},{24,8},{28,12},{1,17},{... | collective-permute-start | bytes 589832 | tf_op jit(solution)/shard_map/ppermute | solution.py:405
  133.0 12.6 %collective-permute-start.39 = (bf16[3,128,256]{2,1,0:T(8,128)(2,1)S(1)}, bf16[3,128,256]{2,1,0:T(8,128)(2,1)S(1)}, u32[]{:S(2)}, u32[]{:S(2)}) collective-permute-start(bf16[3,128,256]{2,1,0:T(8,128)(2,1)S(1)} %get-tuple-element.154.a0), channel_id=1, source_target_pairs={{0,2},{1,3},{2,0},{3,1},{4,6},{5,7},{6,4},{7,5},{8,10},{9,11},{10,... | collective-permute-start | bytes 589832 | tf_op jit(solution)/shard_map/ppermute | solution.py:395
  134.8 10.8 %collective-permute-start.40 = (bf16[3,128,256]{2,1,0:T(8,128)(2,1)S(1)}, bf16[3,128,256]{2,1,0:T(8,128)(2,1)S(1)}, u32[]{:S(2)}, u32[]{:S(2)}) collective-permute-start(bf16[3,128,256]{2,1,0:T(8,128)(2,1)S(1)} %get-tuple-element.157), channel_id=1, source_target_pairs={{0,4},{4,0},{8,12},{12,8},{16,20},{20,16},{24,28},{28,24},{1,5},{5... | collective-permute-start | bytes 589832 | tf_op jit(solution)/shard_map/ppermute | solution.py:398
  136.4 12.8 %collective-permute-start.41 = (bf16[3,128,256]{2,1,0:T(8,128)(2,1)S(1)}, bf16[3,128,256]{2,1,0:T(8,128)(2,1)S(1)}, u32[]{:S(2)}, u32[]{:S(2)}) collective-permute-start(bf16[3,128,256]{2,1,0:T(8,128)(2,1)S(1)} %get-tuple-element.157), channel_id=1, source_target_pairs={{0,6},{1,7},{2,4},{3,5},{4,2},{5,3},{6,0},{7,1},{8,14},{9,15},{10,... | collective-permute-start | bytes 589832 | tf_op jit(solution)/shard_map/ppermute | solution.py:402
  146.8 9.0 %collective-permute-start.44 = (bf16[3,128,256]{2,1,0:T(8,128)(2,1)S(1)}, bf16[3,128,256]{2,1,0:T(8,128)(2,1)S(1)}, u32[]{:S(2)}, u32[]{:S(2)}) collective-permute-start(bf16[3,128,256]{2,1,0:T(8,128)(2,1)S(1)} %get-tuple-element.164), channel_id=1, source_target_pairs={{0,6},{1,7},{2,4},{3,5},{4,2},{5,3},{6,0},{7,1},{8,14},{9,15},{10,... | collective-permute-start | bytes 589832 | tf_op jit(solution)/shard_map/ppermute | solution.py:402
  148.4 8.8 %collective-permute-start.43 = (bf16[3,128,256]{2,1,0:T(8,128)(2,1)S(1)}, bf16[3,128,256]{2,1,0:T(8,128)(2,1)S(1)}, u32[]{:S(2)}, u32[]{:S(2)}) collective-permute-start(bf16[3,128,256]{2,1,0:T(8,128)(2,1)S(1)} %get-tuple-element.164), channel_id=1, source_target_pairs={{0,4},{4,0},{8,12},{12,8},{16,20},{20,16},{24,28},{28,24},{1,5},{5... | collective-permute-start | bytes 589832 | tf_op jit(solution)/shard_map/ppermute | solution.py:398
  (17 other events, 131.7 us)
